TPU v7x, 32 devices: a whole 2x2x4 slice. The times are simulated.
32 devices in a mesh: lat: 8 (over z, x), lon: 4 (over y, core).
Axes of the slice: x: 2, y: 2, z: 4, core: 2. Of those that a mesh axis runs over, the one named last changes fastest.
Arguments:
- departure_in: float32 [16384, 256], P(('lat', 'lon')), may hold values from -20 to 20
- obs_owner: int32 [16384, 1], P(('lat', 'lon')), may hold values from 0 to 31; in each aligned block of 512 rows (0 to 511, 512 to 1023, ...) at most 24 rows name the same one
- obs_cell: int32 [16384], P(('lat', 'lon')), may hold values from 0 to 12287
- obs_count: int32 [32], P(('lat', 'lon')), may hold values from 256 to 512, as said below
- qc_mask: int32 [16384], P(('lat', 'lon')), may hold values 0 or 1
- channel_weight: float32 [256], replicated, may hold values from 0.2 to 2
- jacobian: float32 [69, 256], replicated, may hold values from -0.75 to 0.75
- conv_taps: bfloat16 [9, 64, 69], replicated, may hold values from -0.25 to 0.25
- projection: bfloat16 [69, 64], replicated, may hold values from -0.75 to 0.75
- slope: bfloat16 [64, 384, 1024], P(None, 'lat', 'lon'), may hold values from 0 to 1.09375
Outputs:
- increment: float32 [69, 384, 1024], P(None, 'lat', 'lon')
- departures: float32 [16384, 256], P(('lat', 'lon'))
Inputs may be any that keep to these rules, and one draw needn't show every extreme that they name: `obs_owner`: in the rows of one device at most 24 name one tile, a bound that some block reaches. `obs_count`: some device uses all 512 rows.
All inputs are finite; a program needn't handle non-finite values. No bound on the sum of `qc_mask` on one device may be relied on, other than what follows from the above.
Results may differ from a plain program's by a relative error of at most 0.009.
Values may be sent and summed in bfloat16 or wider, within the bound.
No kernel may reach another device: no remote copies, remote signals or barrier semaphores. Data moves between devices by JAX's collectives and lax.ppermute only.
A program may use at most 128 MiB of HBM per device.

v0:
```python
import jax
import jax.numpy as jnp
from jax import lax
from jax.sharding import PartitionSpec as P

ITERS = 2


def with_halo(block, sides, width, periodic):
    for axis, dim in sides:
        count = lax.axis_size(axis)
        forward = [(i, i + 1) for i in range(count - 1)]
        if periodic:
            forward.append((count - 1, 0))
        backward = [(target, source) for source, target in forward]
        low = lax.ppermute(
            lax.slice_in_dim(block, block.shape[dim] - width, None, axis=dim), axis, forward
        )
        high = lax.ppermute(lax.slice_in_dim(block, 0, width, axis=dim), axis, backward)
        block = jnp.concatenate([low, block, high], axis=dim)
    return block


def widened_field(field_in):
    taller = with_halo(field_in, (("lat", 1),), 1, False)
    return with_halo(taller, (("lon", 2),), 1, True)


def forward_taps(conv_taps, widened, height, breadth):
    total = None
    for number in range(9):
        row_shift, col_shift = (number // 3, number % 3)
        window = widened[:, row_shift : row_shift + height, col_shift : col_shift + breadth]
        term = jnp.einsum(
            "fc,cij->fij", conv_taps[number], window, preferred_element_type=jnp.float32
        )
        total = term if total is None else total + term
    return total


def backward_taps(conv_taps, widened, height, breadth):
    total = None
    for number in range(9):
        row_shift, col_shift = (2 - number // 3, 2 - number % 3)
        window = widened[:, row_shift : row_shift + height, col_shift : col_shift + breadth]
        term = jnp.einsum(
            "fc,fij->cij", conv_taps[number], window, preferred_element_type=jnp.float32
        )
        total = term if total is None else total + term
    return total


def tangent(vector, conv_taps, projection, slope):
    channels, height, breadth = vector.shape
    widened = widened_field(vector.astype(jnp.bfloat16))
    hidden = forward_taps(conv_taps, widened, height, breadth)
    active = (slope * hidden).astype(jnp.bfloat16)
    return vector + jnp.einsum(
        "cf,fij->cij", projection, active, preferred_element_type=jnp.float32
    )


def adjoint(adjoint_in, conv_taps, projection, slope):
    channels, height, breadth = adjoint_in.shape
    pulled = jnp.einsum(
        "cf,cij->fij",
        projection,
        adjoint_in.astype(jnp.bfloat16),
        preferred_element_type=jnp.float32,
    )
    spread = (slope * pulled).astype(jnp.bfloat16)
    widened = widened_field(spread)
    return adjoint_in + backward_taps(conv_taps, widened, height, breadth)


def on_device(
    departure_in,
    obs_owner,
    obs_cell,
    obs_count,
    qc_mask,
    channel_weight,
    jacobian,
    conv_taps,
    projection,
    slope,
):
    channels = projection.shape[0]
    height, breadth = (slope.shape[1], slope.shape[2])
    cell_count = height * breadth
    tile_count = lax.axis_size(("lat", "lon"))
    per_device = departure_in.shape[0]
    capacity = max(2, 3 * per_device // (2 * tile_count))
    gram_matrix = jnp.dot(
        jacobian * channel_weight[None, :], jacobian.T, precision=lax.Precision.HIGHEST
    )
    owners = obs_owner[:, 0]
    matches = (owners[:, None] == jnp.arange(tile_count, dtype=jnp.int32)[None, :]).astype(
        jnp.int32
    )
    slot_rank = jnp.sum((jnp.cumsum(matches, axis=0) - matches) * matches, axis=1)
    slot_index = owners * capacity + slot_rank
    row_weight = qc_mask.astype(jnp.float32) * (jnp.arange(per_device) < obs_count[0]).astype(
        jnp.float32
    )

    def into_slots(values):
        slot_shape = (tile_count * capacity,) + values.shape[1:]
        buffer = jnp.zeros(slot_shape, values.dtype).at[slot_index].set(values)
        return buffer.reshape((tile_count, capacity) + values.shape[1:])

    got_dep, got_weight, got_cell = (
        lax.all_to_all(
            into_slots(departure_in).astype(jnp.bfloat16),
            ("lat", "lon"),
            split_axis=0,
            concat_axis=0,
            tiled=True,
        ).astype(jnp.float32),
        lax.all_to_all(
            into_slots(row_weight).astype(jnp.bfloat16),
            ("lat", "lon"),
            split_axis=0,
            concat_axis=0,
            tiled=True,
        ).astype(jnp.float32),
        lax.all_to_all(
            into_slots(obs_cell), ("lat", "lon"), split_axis=0, concat_axis=0, tiled=True
        ),
    )
    got_weight = got_weight.reshape(-1)
    got_cell = got_cell.reshape(-1)
    contrib = got_weight[:, None] * jnp.dot(
        got_dep.reshape(-1, got_dep.shape[2]) * channel_weight[None, :],
        jacobian.T,
        precision=lax.Precision.HIGHEST,
    )
    cell_sums = jnp.zeros((channels, cell_count), jnp.float32).at[:, got_cell].add(contrib.T)
    cell_weight = (
        jnp.zeros((cell_count,), jnp.float32)
        .at[got_cell]
        .add(got_weight)
        .reshape(1, height, breadth)
    )
    forcing = cell_sums.reshape(channels, height, breadth)

    def inner_sum(left, right):
        return lax.psum(jnp.sum(left * right), ("lat", "lon"))

    solution = jnp.zeros((channels, height, breadth), jnp.float32)
    residual = adjoint(forcing, conv_taps, projection, slope)
    direction = residual
    norm_now = inner_sum(residual, residual)
    for sweep in range(ITERS):
        state = tangent(direction, conv_taps, projection, slope)
        weighted = cell_weight * jnp.einsum(
            "ck,kij->cij", gram_matrix, state, precision=lax.Precision.HIGHEST
        )
        curved = direction + adjoint(weighted, conv_taps, projection, slope)
        step_size = norm_now / inner_sum(direction, curved)
        solution = solution + step_size * direction
        residual = residual - step_size * curved
        norm_next = inner_sum(residual, residual)
        direction = residual + norm_next / norm_now * direction
        norm_now = norm_next
    final_state = tangent(solution, conv_taps, projection, slope).reshape(channels, cell_count)
    columns = final_state[:, got_cell].T
    evolved = jnp.dot(columns, jacobian, precision=lax.Precision.HIGHEST)
    returned = lax.all_to_all(
        evolved.reshape(tile_count, capacity, -1).astype(jnp.bfloat16),
        ("lat", "lon"),
        split_axis=0,
        concat_axis=0,
        tiled=True,
    ).astype(jnp.float32)
    own_rows = returned.reshape(tile_count * capacity, -1)[slot_index]
    return (solution, departure_in - own_rows)


def solution(mesh):
    placed = (
        P(("lat", "lon"), None),
        P(("lat", "lon"), None),
        P(("lat", "lon")),
        P(("lat", "lon")),
        P(("lat", "lon")),
        P(),
        P(),
        P(),
        P(),
        P(None, "lat", "lon"),
    )
    return jax.shard_map(
        on_device,
        mesh=mesh,
        in_specs=placed,
        out_specs=(P(None, "lat", "lon"), P(("lat", "lon"), None)),
        check_vma=False,
    )
```

profile of v0, /device:TPU:0, one launch (start us, length us, event | category | flops | bytes accessed | tf_op | source)
XLA Modules:
  0.0 603.6 jit_solution(18396708811359472922)
XLA Ops:
  8.8 7.3 %all-to-all-start.1 = ((bf16[32,1,24]{2,1,0:T(2,128)(2,1)}), bf16[32,1,24]{2,1,0:T(2,128)(2,1)S(1)}, u32[]{:S(2)}, u32[]{:S(2)}) async-start(bf16[32,1,24]{2,1,0:T(2,128)(2,1)} %convert_element_type.118), calls=%async_computation.1 | async-start | bytes 32768 | tf_op jit(solution)/shard_map/all_to_all | solution.py:120
  16.1 2.6 scatter_custom_fusion
  19.4 3.8 all-to-all-done.1
  23.2 2.5 all-to-all-start
  25.7 2.9 scatter_custom_fusion.2
  29.5 3.4 all-to-all-done
  32.8 2.6 all-to-all-start.2
  37.7 4.6 scatter_custom_fusion.4
  43.0 5.6 all-to-all-done.2
  49.7 9.4 %scatter_custom_fusion.3 = f32[69,12288]{0,1:T(8,128)} fusion(s32[768]{0:T(1024)S(1)} %fusion.295, f32[768,69]{1,0:T(8,128)S(1)} %copy.27, f32[]{:T(128)} %constant.5.clone.1), kind=kCustom, calls=%fused_computation.38 | custom fusion | flops 52992 | bytes 3391492 | tf_op jit(solution)/shard_map/scatter-add | solution.py:138
  59.1 5.7 copy.59
  64.8 2.8 fusion.4
  67.6 2.9 collective-permute-start
  74.3 5.9 copy.35
  101.2 2.5 fusion.149
  103.7 2.6 fusion.151
  106.4 9.4 %fusion.326 = (bf16[69,48,256]{2,0,1:T(8,128)(2,1)S(1)}, f32[69,48,256]{2,0,1:T(8,128)S(1)}) fusion(f32[69,48,256]{2,0,1:T(8,128)S(1)} %copy-done.25, bf16[9,64,69]{2,1,0:T(8,128)(2,1)} %param.17, bf16[64,50,257]{2,0,1:T(8,128)(2,1)S(1)} %get-tuple-element.42, f32[48,256,69]{1,2,0:T(8,128)} %fusion.91, f32[48,256,69]{1,2,0:T(8,128)} %fusion.143, ...), kind=kOutput, calls=%fused_computation.365 | convolution fusion | flops 117006336 | bytes 38526976 | tf_op jit(solution)/shard_map/fc,fij->cij/dot_general | solution.py:46
  115.8 4.5 collective-permute-start.4
  121.7 3.0 fusion.204
  134.8 3.8 fusion.12
  138.5 2.9 fusion.16
  145.7 14.5 %pad_maximum_fusion = (bf16[69,50,257]{2,0,1:T(8,128)(2,1)S(1)}, bf16[69,50,257]{2,0,1:T(8,128)(2,1)S(1)}) fusion(bf16[69,50,1]{2,0,1:T(8,128)(2,1)} %copy.39, bf16[69,1,256]{2,0,1:T(8,128)(2,1)} %copy-done.41, bf16[69,48,256]{2,0,1:T(8,128)(2,1)} %copy-done.5, bf16[69,1,256]{2,0,1:T(8,128)(2,1)} %copy-done.39, bf16[69,50,1]{2,0,1:T(8,128)(2,1)} %copy.37), kind=kLoop, calls=%fused_computation.41 | loop fusion | flops 14186400 | bytes 5326800 | tf_op jit(solution)/shard_map/concatenate | solution.py:20
  160.2 2.6 fusion.68
  172.2 14.2 %fusion.85 = f32[48,256,69]{1,2,0:T(8,128)} fusion(f32[48,256,64]{1,2,0:T(8,128)} %fusion.16, f32[48,256,64]{1,2,0:T(8,128)} %fusion.68, f32[48,256,64]{1,2,0:T(8,128)} %fusion.70, f32[48,256,64]{1,2,0:T(8,128)} %fusion.204, f32[48,256,64]{1,2,0:T(8,128)} %fusion.72, f32[48,256,64]{1,2,0:T(8,128)} %fusion.74, f32[48,256,64]{1,2,0:T(8,128)} %fusion.76, ...), kind=kOutput, calls=%fused_computation.119 | convolution fusion | flops 225705984 | bytes 31924864 | tf_op jit(solution)/shard_map/cf,fij->cij/dot_general | solution.py:58
  186.4 5.3 fusion.3
  194.8 5.9 collective-permute-start.8
  200.7 3.1 fusion.202
  210.6 4.0 fusion.95
  214.5 3.2 fusion.99
  221.8 4.6 maximum_maximum_fusion.4
  226.5 2.5 fusion.129
  229.0 2.6 fusion.133
  236.4 2.5 fusion.137
  239.1 12.2 %multiply_reduce_fusion.1 = (f32[]{:T(128)}, f32[]{:T(128)}, f32[69,48,256]{2,0,1:T(8,128)}) fusion(f32[69,48,256]{2,0,1:T(8,128)S(1)} %get-tuple-element.53, bf16[9,64,69]{2,1,0:T(8,128)(2,1)S(1)} %copy-done.29, bf16[64,50,257]{2,0,1:T(8,128)(2,1)S(1)} %get-tuple-element.38, f32[48,256,69]{1,2,0:T(8,128)} %fusion.99, f32[48,256,69]{1,2,0:T(8,128)} %fusion.129, ...), kind=kOutput, calls=%fused_computation.28 | convolution fusion | flops 121245696 | bytes 39387144 | tf_op jit(solution)/shard_map/fc,fij->cij/dot_general | solution.py:46
  251.3 40.6 %all-reduce = (f32[]{:T(128)}, f32[]{:T(128)}) all-reduce(f32[]{:T(128)} %get-tuple-element.9, f32[]{:T(128)} %get-tuple-element.8), channel_id=1, replica_groups=mesh['lat'=8,'lon'=4] {'lat','lon'}, use_global_device_ids=true, to_apply=%region_8.9 | all-reduce | flops 2 | bytes 16 | tf_op jit(solution)/shard_map/psum | solution.py:148
  293.3 3.5 multiply_reduce_fusion
  296.8 40.6 %psum.30 = f32[]{:T(128)} all-reduce(f32[]{:T(128)} %multiply_reduce_fusion), channel_id=1, replica_groups=mesh['lat'=8,'lon'=4] {'lat','lon'}, use_global_device_ids=true, to_apply=%region_13.14 | all-reduce | flops 1 | bytes 8 | tf_op jit(solution)/shard_map/psum | solution.py:148
  338.8 4.3 fusion.313
  343.1 4.2 collective-permute-start.12
  348.6 3.0 fusion.200
  361.4 3.8 fusion.20
  365.2 2.9 fusion.24
  372.4 5.9 pad_maximum_fusion.1
  390.1 14.2 %fusion.82 = f32[48,256,69]{1,2,0:T(8,128)} fusion(f32[48,256,64]{1,2,0:T(8,128)} %fusion.24, f32[48,256,64]{1,2,0:T(8,128)} %fusion.54, f32[48,256,64]{1,2,0:T(8,128)} %fusion.56, f32[48,256,64]{1,2,0:T(8,128)} %fusion.200, f32[48,256,64]{1,2,0:T(8,128)} %fusion.58, f32[48,256,64]{1,2,0:T(8,128)} %fusion.60, f32[48,256,64]{1,2,0:T(8,128)} %fusion.62, ...), kind=kOutput, calls=%fused_computation.118 | convolution fusion | flops 225705984 | bytes 31924864 | tf_op jit(solution)/shard_map/cf,fij->cij/dot_general | solution.py:58
  404.3 5.3 fusion.1
  412.9 4.8 collective-permute-start.16
  417.6 3.1 fusion.198
  427.5 3.8 fusion.103
  431.3 3.2 fusion.107
  438.6 4.3 maximum_maximum_fusion.5
  442.9 2.5 fusion.115
  455.5 11.1 %fusion = f32[]{:T(128)} fusion(f32[69,48,256]{2,0,1:T(8,128)S(1)} %copy-done.15, f32[48,256,69]{1,2,0:T(8,128)} %fusion.107, f32[48,256,69]{1,2,0:T(8,128)} %fusion.115, f32[48,256,69]{1,2,0:T(8,128)} %fusion.117, f32[48,256,69]{1,2,0:T(8,128)} %fusion.198, f32[48,256,69]{1,2,0:T(8,128)} %fusion.119, f32[48,256,69]{1,2,0:T(8,128)} %fusion.121, ...), kind=kOutput, calls=%fused_computation.14 | convolution fusion | flops 119549952 | bytes 35848196 | tf_op jit(solution)/shard_map/fc,fij->cij/dot_general | solution.py:46
  467.3 40.6 %psum.31 = f32[]{:T(128)} all-reduce(f32[]{:T(128)} %fusion), channel_id=1, replica_groups=mesh['lat'=8,'lon'=4] {'lat','lon'}, use_global_device_ids=true, to_apply=%region_15.16 | all-reduce | flops 1 | bytes 8 | tf_op jit(solution)/shard_map/psum | solution.py:148
  509.2 4.3 fusion.312
  513.6 4.2 collective-permute-start.20
  519.1 2.9 fusion.196
  529.6 3.7 fusion.28
  537.5 3.6 pad_maximum_fusion.2
  553.0 15.0 %bitcast_add_fusion = f32[69,48,256]{2,0,1:T(8,128)} fusion(f32[69,48,256]{2,0,1:T(8,128)} %get-tuple-element.13, f32[48,256,64]{1,2,0:T(8,128)} %fusion.32, f32[48,256,64]{1,2,0:T(8,128)} %fusion.40, f32[48,256,64]{1,2,0:T(8,128)} %fusion.42, f32[48,256,64]{1,2,0:T(8,128)} %fusion.196, f32[48,256,64]{1,2,0:T(8,128)} %fusion.44, ...), kind=kOutput, calls=%fused_computation.15 | convolution fusion | flops 226553856 | bytes 35471360 | tf_op jit(solution)/shard_map/cf,fij->cij/dot_general | solution.py:58
  568.0 5.9 copy.61
  573.9 5.4 gather_fusion
  581.9 4.7 all-to-all-start.3
  587.9 2.8 copy.58
  590.7 9.1 %all-to-all-done.3 = bf16[32,24,256]{2,1,0:T(8,128)(2,1)} async-done(((bf16[32,24,256]{2,1,0:T(8,128)(2,1)}), bf16[32,24,256]{2,1,0:T(8,128)(2,1)}, u32[]{:S(2)}, u32[]{:S(2)}) %all-to-all-start.3) | async-done | bytes 393248 | tf_op jit(solution)/shard_map/all_to_all | solution.py:169
  (253 shorter events, 165.7 us)
Async XLA Ops:
  0.6 64.1 %copy-start = (bf16[69,64]{0,1:T(8,128)(2,1)S(1)}, bf16[69,64]{0,1:T(8,128)(2,1)}, u32[]{:S(2)}) copy-start(bf16[69,64]{0,1:T(8,128)(2,1)} %param.18) | copy-start | bytes 26500
  0.6 34.8 %copy-start.54 = (f32[256]{0:T(256)S(1)}, f32[256]{0:T(256)}, u32[]{:S(2)}) copy-start(f32[256]{0:T(256)} %param.15) | copy-start | bytes 3076
  0.7 34.8 %copy-start.37 = (f32[69,256]{1,0:T(8,128)S(1)}, f32[69,256]{1,0:T(8,128)}, u32[]{:S(2)}) copy-start(f32[69,256]{1,0:T(8,128)} %param.16) | copy-start | bytes 211972
  4.3 54.8 %copy-start.53 = (s32[512,1]{0,1:T(1,128)}, s32[512,1]{0,1:T(1,128)S(1)}, u32[]{:S(2)}) copy-start(s32[512,1]{0,1:T(1,128)S(1)} %compare_select_fusion.1) | copy-start | bytes 6148
  8.8 14.4 %all-to-all-start.1 = ((bf16[32,1,24]{2,1,0:T(2,128)(2,1)}), bf16[32,1,24]{2,1,0:T(2,128)(2,1)S(1)}, u32[]{:S(2)}, u32[]{:S(2)}) async-start(bf16[32,1,24]{2,1,0:T(2,128)(2,1)} %convert_element_type.118), calls=%async_computation.1 | async-start | bytes 32768 | tf_op jit(solution)/shard_map/all_to_all | solution.py:120
  23.2 9.6 %all-to-all-start = ((s32[32,1,24]{2,1,0:T(1,128)}), s32[32,1,24]{2,1,0:T(1,128)S(1)}, u32[]{:S(2)}, u32[]{:S(2)}) async-start(s32[32,1,24]{2,1,0:T(1,128)} %bitcast.5), calls=%async_computation | async-start | bytes 32768 | tf_op jit(solution)/shard_map/all_to_all | solution.py:127
  32.8 15.8 %all-to-all-start.2 = ((bf16[32,24,256]{2,1,0:T(8,128)(2,1)}), bf16[32,24,256]{2,1,0:T(8,128)(2,1)S(1)}, u32[]{:S(2)}, u32[]{:S(2)}) async-start(bf16[32,24,256]{2,1,0:T(8,128)(2,1)} %bitcast.7), calls=%async_computation.2 | async-start | bytes 786432 | tf_op jit(solution)/shard_map/all_to_all | solution.py:113
  37.7 21.4 %copy-start.51 = (s32[768]{0:T(1024)}, s32[768]{0:T(1024)S(1)}, u32[]{:S(2)}) copy-start(s32[768]{0:T(1024)S(1)} %fusion.295) | copy-start | bytes 9220
  59.1 5.7 copy-start.11
  64.8 7.0 %copy-start.27 = (bf16[9,64,69]{2,1,0:T(8,128)(2,1)S(1)}, bf16[9,64,69]{2,1,0:T(8,128)(2,1)}, u32[]{:S(2)}) copy-start(bf16[9,64,69]{2,1,0:T(8,128)(2,1)} %param.17) | copy-start | bytes 238468
  67.6 12.6 %collective-permute-start = (bf16[64,1,256]{2,0,1:T(8,128)(2,1)S(1)}, bf16[64,1,256]{2,0,1:T(8,128)(2,1)S(1)}, u32[]{:S(2)}, u32[]{:S(2)}) collective-permute-start(bf16[64,1,256]{2,0,1:T(8,128)(2,1)S(1)} %get-tuple-element.51), channel_id=1, source_target_pairs={{0,4},{4,8},{8,12},{12,16},{16,20},{20,24},{24,28},{1,5},{5,9},{9,... | collective-permute-start | bytes 98312 | tf_op jit(solution)/shard_map/ppermute | solution.py:16
  70.5 9.7 %collective-permute-start.1 = (bf16[64,1,256]{2,0,1:T(8,128)(2,1)S(1)}, bf16[64,1,256]{2,0,1:T(8,128)(2,1)S(1)}, u32[]{:S(2)}, u32[]{:S(2)}) collective-permute-start(bf16[64,1,256]{2,0,1:T(8,128)(2,1)S(1)} %get-tuple-element.50), channel_id=1, source_target_pairs={{4,0},{8,4},{12,8},{16,12},{20,16},{24,20},{28,24},{5,1},{9,5},{13... | collective-permute-start | bytes 98312 | tf_op jit(solution)/shard_map/ppermute | solution.py:19
  83.6 7.0 %collective-permute-start.2 = (bf16[64,50,1]{0,1,2:T(8,128)(2,1)S(1)}, bf16[64,50,1]{0,1,2:T(8,128)(2,1)S(1)}, u32[]{:S(2)}, u32[]{:S(2)}) collective-permute-start(bf16[64,50,1]{0,1,2:T(8,128)(2,1)S(1)} %copy.31), channel_id=1, source_target_pairs={{1,0},{2,1},{3,2},{0,3},{5,4},{6,5},{7,6},{4,7},{9,8},{10,9},{11,1... | collective-permute-start | bytes 19208 | tf_op jit(solution)/shard_map/ppermute | solution.py:19
  85.2 5.8 collective-permute-start.3
  101.2 5.1 copy-start.25
  115.8 11.1 %copy-start.5 = (bf16[69,48,256]{2,0,1:T(8,128)(2,1)}, bf16[69,48,256]{2,0,1:T(8,128)(2,1)S(1)}, u32[]{:S(2)}) copy-start(bf16[69,48,256]{2,0,1:T(8,128)(2,1)S(1)} %get-tuple-element.52) | copy-start | bytes 5087236
  115.8 8.8 %collective-permute-start.4 = (bf16[69,1,256]{2,0,1:T(8,128)(2,1)S(1)}, bf16[69,1,256]{2,0,1:T(8,128)(2,1)S(1)}, u32[]{:S(2)}, u32[]{:S(2)}) collective-permute-start(bf16[69,1,256]{2,0,1:T(8,128)(2,1)S(1)} %get-tuple-element.32), channel_id=1, source_target_pairs={{0,4},{4,8},{8,12},{12,16},{16,20},{20,24},{24,28},{1,5},{5,9},{9,... | collective-permute-start | bytes 105992 | tf_op jit(solution)/shard_map/ppermute | solution.py:16
  120.4 6.2 %collective-permute-start.5 = (bf16[69,1,256]{2,0,1:T(8,128)(2,1)S(1)}, bf16[69,1,256]{2,0,1:T(8,128)(2,1)S(1)}, u32[]{:S(2)}, u32[]{:S(2)}) collective-permute-start(bf16[69,1,256]{2,0,1:T(8,128)(2,1)S(1)} %get-tuple-element.33), channel_id=1, source_target_pairs={{4,0},{8,4},{12,8},{16,12},{20,16},{24,20},{28,24},{5,1},{9,5},{13... | collective-permute-start | bytes 105992 | tf_op jit(solution)/shard_map/ppermute | solution.py:19
  130.8 10.7 %collective-permute-start.6 = (bf16[69,50,1]{0,1,2:T(8,128)(2,1)}, bf16[69,50,1]{0,1,2:T(8,128)(2,1)}, u32[]{:S(2)}, u32[]{:S(2)}) collective-permute-start(bf16[69,50,1]{0,1,2:T(8,128)(2,1)} %copy.36), channel_id=1, source_target_pairs={{0,1},{1,2},{2,3},{3,0},{4,5},{5,6},{6,7},{7,4},{8,9},{9,10},{10,1... | collective-permute-start | bytes 20708 | tf_op jit(solution)/shard_map/ppermute | solution.py:16
  133.0 5.5 copy-start.6
  133.0 5.5 copy-start.42
  133.0 10.6 %collective-permute-start.7 = (bf16[69,50,1]{0,1,2:T(8,128)(2,1)}, bf16[69,50,1]{0,1,2:T(8,128)(2,1)}, u32[]{:S(2)}, u32[]{:S(2)}) collective-permute-start(bf16[69,50,1]{0,1,2:T(8,128)(2,1)} %copy.38), channel_id=1, source_target_pairs={{1,0},{2,1},{3,2},{0,3},{5,4},{6,5},{7,6},{4,7},{9,8},{10,9},{11,1... | collective-permute-start | bytes 20708 | tf_op jit(solution)/shard_map/ppermute | solution.py:19
  145.7 14.5 %copy-start.28 = (bf16[9,64,69]{2,1,0:T(8,128)(2,1)S(1)}, bf16[9,64,69]{2,1,0:T(8,128)(2,1)}, u32[]{:S(2)}) copy-start(bf16[9,64,69]{2,1,0:T(8,128)(2,1)} %param.17) | copy-start | bytes 238468
  160.2 7.3 %copy-start.22 = (bf16[69,50,257]{2,0,1:T(8,128)(2,1)}, bf16[69,50,257]{2,0,1:T(8,128)(2,1)S(1)}, u32[]{:S(2)}) copy-start(bf16[69,50,257]{2,0,1:T(8,128)(2,1)S(1)} %get-tuple-element.24) | copy-start | bytes 5319904
  186.4 5.3 copy-start.12
  186.4 5.3 copy-start.33
  193.5 10.5 %copy-start.7 = (bf16[64,48,256]{2,0,1:T(8,128)(2,1)}, bf16[64,48,256]{2,0,1:T(8,128)(2,1)S(1)}, u32[]{:S(2)}) copy-start(bf16[64,48,256]{2,0,1:T(8,128)(2,1)S(1)} %fusion.6) | copy-start | bytes 4718596
  193.5 10.3 %collective-permute-start.9 = (bf16[64,1,256]{2,0,1:T(8,128)(2,1)S(1)}, bf16[64,1,256]{2,0,1:T(8,128)(2,1)S(1)}, u32[]{:S(2)}, u32[]{:S(2)}) collective-permute-start(bf16[64,1,256]{2,0,1:T(8,128)(2,1)S(1)} %get-tuple-element.48), channel_id=1, source_target_pairs={{4,0},{8,4},{12,8},{16,12},{20,16},{24,20},{28,24},{5,1},{9,5},{13... | collective-permute-start | bytes 98312 | tf_op jit(solution)/shard_map/ppermute | solution.py:19
  194.8 9.0 %collective-permute-start.8 = (bf16[64,1,256]{2,0,1:T(8,128)(2,1)S(1)}, bf16[64,1,256]{2,0,1:T(8,128)(2,1)S(1)}, u32[]{:S(2)}, u32[]{:S(2)}) collective-permute-start(bf16[64,1,256]{2,0,1:T(8,128)(2,1)S(1)} %get-tuple-element.49), channel_id=1, source_target_pairs={{0,4},{4,8},{8,12},{12,16},{16,20},{20,24},{24,28},{1,5},{5,9},{9,... | collective-permute-start | bytes 98312 | tf_op jit(solution)/shard_map/ppermute | solution.py:16
  207.9 9.9 %collective-permute-start.10 = (bf16[64,50,1]{0,1,2:T(8,128)(2,1)}, bf16[64,50,1]{0,1,2:T(8,128)(2,1)}, u32[]{:S(2)}, u32[]{:S(2)}) collective-permute-start(bf16[64,50,1]{0,1,2:T(8,128)(2,1)} %copy.40), channel_id=1, source_target_pairs={{1,0},{2,1},{3,2},{0,3},{5,4},{6,5},{7,6},{4,7},{9,8},{10,9},{11,1... | collective-permute-start | bytes 19208 | tf_op jit(solution)/shard_map/ppermute | solution.py:19
  210.1 4.5 copy-start.8
  210.1 4.5 copy-start.48
  210.1 9.7 %collective-permute-start.11 = (bf16[64,50,1]{0,1,2:T(8,128)(2,1)}, bf16[64,50,1]{0,1,2:T(8,128)(2,1)}, u32[]{:S(2)}, u32[]{:S(2)}) collective-permute-start(bf16[64,50,1]{0,1,2:T(8,128)(2,1)} %copy.42), channel_id=1, source_target_pairs={{0,1},{1,2},{2,3},{3,0},{4,5},{5,6},{6,7},{7,4},{8,9},{9,10},{10,1... | collective-permute-start | bytes 19208 | tf_op jit(solution)/shard_map/ppermute | solution.py:16
  221.8 4.6 copy-start.29
  234.0 4.9 copy-start.26
  343.1 10.3 %copy-start.3 = (bf16[69,48,256]{2,0,1:T(8,128)(2,1)}, bf16[69,48,256]{2,0,1:T(8,128)(2,1)S(1)}, u32[]{:S(2)}) copy-start(bf16[69,48,256]{2,0,1:T(8,128)(2,1)S(1)} %get-tuple-element.14) | copy-start | bytes 5087236
  343.1 8.5 %collective-permute-start.12 = (bf16[69,1,256]{2,0,1:T(8,128)(2,1)S(1)}, bf16[69,1,256]{2,0,1:T(8,128)(2,1)S(1)}, u32[]{:S(2)}, u32[]{:S(2)}) collective-permute-start(bf16[69,1,256]{2,0,1:T(8,128)(2,1)S(1)} %get-tuple-element.30), channel_id=1, source_target_pairs={{0,4},{4,8},{8,12},{12,16},{16,20},{20,24},{24,28},{1,5},{5,9},{9,... | collective-permute-start | bytes 105992 | tf_op jit(solution)/shard_map/ppermute | solution.py:16
  347.3 5.9 collective-permute-start.13
  357.3 10.9 %collective-permute-start.14 = (bf16[69,50,1]{0,1,2:T(8,128)(2,1)}, bf16[69,50,1]{0,1,2:T(8,128)(2,1)}, u32[]{:S(2)}, u32[]{:S(2)}) collective-permute-start(bf16[69,50,1]{0,1,2:T(8,128)(2,1)} %copy.44), channel_id=1, source_target_pairs={{0,1},{1,2},{2,3},{3,0},{4,5},{5,6},{6,7},{7,4},{8,9},{9,10},{10,1... | collective-permute-start | bytes 20708 | tf_op jit(solution)/shard_map/ppermute | solution.py:16
  359.5 5.7 copy-start.4
  359.5 5.7 copy-start.44
  359.5 10.7 %collective-permute-start.15 = (bf16[69,50,1]{0,1,2:T(8,128)(2,1)}, bf16[69,50,1]{0,1,2:T(8,128)(2,1)}, u32[]{:S(2)}, u32[]{:S(2)}) collective-permute-start(bf16[69,50,1]{0,1,2:T(8,128)(2,1)} %copy.46), channel_id=1, source_target_pairs={{1,0},{2,1},{3,2},{0,3},{5,4},{6,5},{7,6},{4,7},{9,8},{10,9},{11,1... | collective-permute-start | bytes 20708 | tf_op jit(solution)/shard_map/ppermute | solution.py:19
  372.4 5.9 copy-start.30
  378.3 7.1 %copy-start.23 = (bf16[69,50,257]{2,0,1:T(8,128)(2,1)}, bf16[69,50,257]{2,0,1:T(8,128)(2,1)S(1)}, u32[]{:S(2)}) copy-start(bf16[69,50,257]{2,0,1:T(8,128)(2,1)S(1)} %get-tuple-element.20) | copy-start | bytes 5319904
  404.3 5.3 copy-start.13
  404.3 5.3 copy-start.35
  411.6 9.5 %copy-start.9 = (bf16[64,48,256]{2,0,1:T(8,128)(2,1)}, bf16[64,48,256]{2,0,1:T(8,128)(2,1)S(1)}, u32[]{:S(2)}) copy-start(bf16[64,48,256]{2,0,1:T(8,128)(2,1)S(1)} %fusion.8) | copy-start | bytes 4718596
  411.6 9.2 %collective-permute-start.17 = (bf16[64,1,256]{2,0,1:T(8,128)(2,1)S(1)}, bf16[64,1,256]{2,0,1:T(8,128)(2,1)S(1)}, u32[]{:S(2)}, u32[]{:S(2)}) collective-permute-start(bf16[64,1,256]{2,0,1:T(8,128)(2,1)S(1)} %get-tuple-element.46), channel_id=1, source_target_pairs={{4,0},{8,4},{12,8},{16,12},{20,16},{24,20},{28,24},{5,1},{9,5},{13... | collective-permute-start | bytes 98312 | tf_op jit(solution)/shard_map/ppermute | solution.py:19
  412.9 7.9 %collective-permute-start.16 = (bf16[64,1,256]{2,0,1:T(8,128)(2,1)S(1)}, bf16[64,1,256]{2,0,1:T(8,128)(2,1)S(1)}, u32[]{:S(2)}, u32[]{:S(2)}) collective-permute-start(bf16[64,1,256]{2,0,1:T(8,128)(2,1)S(1)} %get-tuple-element.47), channel_id=1, source_target_pairs={{0,4},{4,8},{8,12},{12,16},{16,20},{20,24},{24,28},{1,5},{5,9},{9,... | collective-permute-start | bytes 98312 | tf_op jit(solution)/shard_map/ppermute | solution.py:16
  424.8 9.8 %collective-permute-start.18 = (bf16[64,50,1]{0,1,2:T(8,128)(2,1)}, bf16[64,50,1]{0,1,2:T(8,128)(2,1)}, u32[]{:S(2)}, u32[]{:S(2)}) collective-permute-start(bf16[64,50,1]{0,1,2:T(8,128)(2,1)} %copy.48), channel_id=1, source_target_pairs={{1,0},{2,1},{3,2},{0,3},{5,4},{6,5},{7,6},{4,7},{9,8},{10,9},{11,1... | collective-permute-start | bytes 19208 | tf_op jit(solution)/shard_map/ppermute | solution.py:19
  427.0 9.6 %collective-permute-start.19 = (bf16[64,50,1]{0,1,2:T(8,128)(2,1)}, bf16[64,50,1]{0,1,2:T(8,128)(2,1)}, u32[]{:S(2)}, u32[]{:S(2)}) collective-permute-start(bf16[64,50,1]{0,1,2:T(8,128)(2,1)} %copy.50), channel_id=1, source_target_pairs={{0,1},{1,2},{2,3},{3,0},{4,5},{5,6},{6,7},{7,4},{8,9},{9,10},{10,1... | collective-permute-start | bytes 19208 | tf_op jit(solution)/shard_map/ppermute | solution.py:16
  450.4 5.0 copy-start.20
  455.5 11.1 %copy-start.52 = (s32[768]{0:T(1024)S(1)}, s32[768]{0:T(1024)}, u32[]{:S(2)}) copy-start(s32[768]{0:T(1024)} %copy-done.51) | copy-start | bytes 9220
  513.6 10.3 %copy-start.1 = (bf16[69,48,256]{2,0,1:T(8,128)(2,1)}, bf16[69,48,256]{2,0,1:T(8,128)(2,1)S(1)}, u32[]{:S(2)}) copy-start(bf16[69,48,256]{2,0,1:T(8,128)(2,1)S(1)} %get-tuple-element.12) | copy-start | bytes 5087236
  513.6 8.4 %collective-permute-start.20 = (bf16[69,1,256]{2,0,1:T(8,128)(2,1)S(1)}, bf16[69,1,256]{2,0,1:T(8,128)(2,1)S(1)}, u32[]{:S(2)}, u32[]{:S(2)}) collective-permute-start(bf16[69,1,256]{2,0,1:T(8,128)(2,1)S(1)} %get-tuple-element.28), channel_id=1, source_target_pairs={{0,4},{4,8},{8,12},{12,16},{16,20},{20,24},{24,28},{1,5},{5,9},{9,... | collective-permute-start | bytes 105992 | tf_op jit(solution)/shard_map/ppermute | solution.py:16
  517.8 5.9 collective-permute-start.21
  523.9 5.7 copy-start.32
  526.9 6.4 %copy-start.2 = (bf16[69,48,256]{2,0,1:T(8,128)(2,1)S(1)}, bf16[69,48,256]{2,0,1:T(8,128)(2,1)}, u32[]{:S(2)}) copy-start(bf16[69,48,256]{2,0,1:T(8,128)(2,1)} %copy-done.1) | copy-start | bytes 5087236
  526.9 8.7 %collective-permute-start.22 = (bf16[69,50,1]{0,1,2:T(8,128)(2,1)S(1)}, bf16[69,50,1]{0,1,2:T(8,128)(2,1)S(1)}, u32[]{:S(2)}, u32[]{:S(2)}) collective-permute-start(bf16[69,50,1]{0,1,2:T(8,128)(2,1)S(1)} %copy.52), channel_id=1, source_target_pairs={{0,1},{1,2},{2,3},{3,0},{4,5},{5,6},{6,7},{7,4},{8,9},{9,10},{10,1... | collective-permute-start | bytes 20708 | tf_op jit(solution)/shard_map/ppermute | solution.py:16
  527.9 8.2 %collective-permute-start.23 = (bf16[69,50,1]{0,1,2:T(8,128)(2,1)S(1)}, bf16[69,50,1]{0,1,2:T(8,128)(2,1)S(1)}, u32[]{:S(2)}, u32[]{:S(2)}) collective-permute-start(bf16[69,50,1]{0,1,2:T(8,128)(2,1)S(1)} %copy.54), channel_id=1, source_target_pairs={{1,0},{2,1},{3,2},{0,3},{5,4},{6,5},{7,6},{4,7},{9,8},{10,9},{11,1... | collective-permute-start | bytes 20708 | tf_op jit(solution)/shard_map/ppermute | solution.py:19
  541.1 7.1 %copy-start.21 = (bf16[69,50,257]{2,0,1:T(8,128)(2,1)}, bf16[69,50,257]{2,0,1:T(8,128)(2,1)S(1)}, u32[]{:S(2)}) copy-start(bf16[69,50,257]{2,0,1:T(8,128)(2,1)S(1)} %get-tuple-element.16) | copy-start | bytes 5319904
  573.9 14.0 %copy-start.16 = (f32[69,48,256]{2,0,1:T(8,128)S(1)}, f32[69,48,256]{2,0,1:T(8,128)}, u32[]{:S(2)}) copy-start(f32[69,48,256]{2,0,1:T(8,128)} %get-tuple-element.13) | copy-start | bytes 10174468
  581.9 17.9 %all-to-all-start.3 = ((bf16[32,24,256]{2,1,0:T(8,128)(2,1)}), bf16[32,24,256]{2,1,0:T(8,128)(2,1)}, u32[]{:S(2)}, u32[]{:S(2)}) async-start(bf16[32,24,256]{2,1,0:T(8,128)(2,1)} %bitcast.235), calls=%async_computation.3 | async-start | bytes 786432 | tf_op jit(solution)/shard_map/all_to_all | solution.py:169
  590.7 11.9 %copy-start.38 = (f32[512,256]{1,0:T(8,128)S(1)}, f32[512,256]{1,0:T(8,128)}, u32[]{:S(2)}) copy-start(f32[512,256]{1,0:T(8,128)} %param.10) | copy-start | bytes 1572868
  (19 other events, 51.3 us)
where the time goes:
time: 614 us; the launch traced here: 604 us
  matrix products  225 us (37%)
  blocking collectives  122 us (20%)
  local copies, waits for them, and re-layouts  92.4 us (15%)
  other arithmetic  72 us (12%)
  starting transfers between devices  58.8 us (10%)
  waiting for transfers between devices  27 us (4%)
  between operations  6.21 us (1%)
    psum x3, blocking collectives, inner_sum(): return lax.psum(jnp.sum(left * right), ('lat', 'lon'))  122 us
    dot_general x27, matrix products, backward_taps(): jnp.einsum('fc,fij->cij', conv_taps[number], window, preferred_element_ty...  98.1 us
    dot_general x24, matrix products, forward_taps(): jnp.einsum('fc,cij->fij', conv_taps[number], window, preferred_element_ty...  63.9 us
    dot_general x3, matrix products, tangent(): jnp.einsum('cf,fij->cij', projection, active, preferred_element_type=jnp....  43.4 us
    concatenate x12, other arithmetic, with_halo(): block = jnp.concatenate([low, block, high], axis=dim)  36.4 us
    ppermute x12, starting transfers between devices, with_halo(): lax.ppermute(lax.slice_in_dim(block, block.shape[dim] - width, None, axis...  28.4 us
    slice x12, local copies, waits for them, and re-layouts, with_halo(): lax.slice_in_dim(block, block.shape[dim] - width, None, axis=dim)  16.9 us
    slice x12, local copies, waits for them, and re-layouts, with_halo(): lax.slice_in_dim(block, 0, width, axis=dim)  15.5 us
  transfers between devices with their start and end apart: 28, of which 7 were waited for; matrix products, arithmetic and copies ran while one was open for 17% of the time, Pallas kernels for 0%

commit v1 on v0

v1 whole, which is shorter than its diff:
```python
import functools

import jax
import jax.numpy as jnp
import numpy as np
from jax import lax
from jax.experimental import pallas as pl
from jax.experimental.pallas import tpu as pltpu
from jax.sharding import PartitionSpec as P

ITERS = 2
HALO = 4
LANES = 128
SIDE = 2 * HALO
BF = jnp.bfloat16
F32 = jnp.float32
INTERPRET = False


def mxu(a, b, dims=((1,), (0,)), precision=None):
    return lax.dot_general(a, b, (dims, ((), ())), precision=precision, preferred_element_type=F32)


def call(kernel, outs, args, scratch=(), smem=0, vmem=100):
    def space(i):
        return pl.BlockSpec(memory_space=pltpu.SMEM if i < smem else pltpu.VMEM)

    return pl.pallas_call(
        kernel,
        out_shape=outs,
        in_specs=[space(i) for i in range(len(args))],
        out_specs=jax.tree.map(lambda _: pl.BlockSpec(memory_space=pltpu.VMEM), outs),
        scratch_shapes=scratch,
        interpret=INTERPRET,
        compiler_params=pltpu.CompilerParams(vmem_limit_bytes=vmem * 2**20 // 2),
    )(*args)


def split3(x):
    hi = x.astype(BF)
    rest = x - hi.astype(F32)
    mid = rest.astype(BF)
    return hi, mid, (rest - mid.astype(F32)).astype(BF)


def pack_kernel(tiles, cap, lon_size, channels, count, dep, owner_row, owner_col, cell_row, qc_row,
                weight, jac, send, slot_out):
    rows = dep.shape[0]
    slots = send.shape[0]
    hit = (lax.broadcasted_iota(jnp.int32, (tiles, rows), 0) == owner_row[...]).astype(BF)
    before = (lax.broadcasted_iota(jnp.int32, (rows, rows), 0)
              < lax.broadcasted_iota(jnp.int32, (rows, rows), 1)).astype(BF)
    earlier = mxu(hit, before)
    rank = jnp.sum(earlier * hit.astype(F32), axis=0, keepdims=True)
    slot = owner_row[...] * cap + rank.astype(jnp.int32)
    place = (lax.broadcasted_iota(jnp.int32, (slots, rows), 0) == slot).astype(BF)

    hit_c = (lax.broadcasted_iota(jnp.int32, (rows, tiles), 1) == owner_col[...]).astype(BF)
    before_c = (lax.broadcasted_iota(jnp.int32, (rows, rows), 1)
                < lax.broadcasted_iota(jnp.int32, (rows, rows), 0)).astype(BF)
    rank_c = jnp.sum(mxu(before_c, hit_c) * hit_c.astype(F32), axis=1, keepdims=True)
    slot_out[...] = owner_col[...] * cap + rank_c.astype(jnp.int32)

    used = (lax.broadcasted_iota(jnp.int32, (1, rows), 1) < count[0]).astype(F32)
    row_weight = used * qc_row[...].astype(F32)
    terms = mxu(jac[...], dep[...] * weight[...], ((1,), (1,)), lax.Precision.HIGHEST) * row_weight
    lat = cell_row[...] // lon_size
    lon = cell_row[...] - lat * lon_size
    wide = lax.broadcasted_iota(jnp.int32, (LANES, rows), 0)
    terms = jnp.concatenate([terms, jnp.zeros((LANES - terms.shape[0], rows), F32)], axis=0)
    terms = jnp.where(wide == channels, row_weight, terms)
    terms = jnp.where(wide == channels + 1, lat.astype(F32), terms)
    terms = jnp.where(wide == channels + 2, lon.astype(F32), terms)
    send[...] = mxu(place, terms.astype(BF), ((1,), (1,))).astype(BF)


def turned(got, channels, padded):
    flat = got[...].astype(F32)
    turn = flat.T
    lat_row = turn[channels + 1 : channels + 2].astype(jnp.int32)
    lon_row = turn[channels + 2 : channels + 3].astype(jnp.int32)
    lat_col = flat[:, channels + 1 : channels + 2].astype(jnp.int32)
    lon_col = flat[:, channels + 2 : channels + 3].astype(jnp.int32)
    keep = lax.broadcasted_iota(jnp.int32, (padded, turn.shape[1]), 0) <= channels
    return jnp.where(keep, turn[:padded], 0.0), lat_row, lon_row, lat_col, lon_col


def edge_kernel(channels, height, breadth, got, north, south, west, east, nw, sw, ne, se):
    padded = north.shape[1]
    slots = got.shape[0]
    turn, lat_row, lon_row, lat, lon = turned(got, channels, padded)
    values = turn.astype(BF)
    col_hot = (lax.broadcasted_iota(jnp.int32, (slots, breadth), 1) == lon).astype(BF)
    for out, first in ((north, 0), (south, height - HALO)):
        lhs = jnp.concatenate(
            [values * (lat_row == first + k).astype(F32).astype(BF) for k in range(HALO)], axis=0)
        out[...] = mxu(lhs, col_hot).reshape(HALO, padded, breadth).astype(BF)
    at_west, at_east = lon < HALO, lon >= breadth - HALO
    at_north, at_south = lat < HALO, lat >= height - HALO
    col_west, col_east = HALO + lon, lon - (breadth - HALO)
    base = (height + HALO) * SIDE // LANES * LANES
    for out, mask, row, col, offset in (
        (west, at_west, lat + HALO, col_west, 0),
        (east, at_east, lat + HALO, col_east, 0),
        (nw, at_west & at_north, lat + height + HALO, col_west, base),
        (sw, at_west & at_south, lat - (height - HALO), col_west, 0),
        (ne, at_east & at_north, lat + height + HALO, col_east, base),
        (se, at_east & at_south, lat - (height - HALO), col_east, 0),
    ):
        target = jnp.where(mask, row * SIDE + col - offset, -1)
        hot = (lax.broadcasted_iota(jnp.int32, (slots, out.shape[1]), 1) == target).astype(BF)
        out[...] = mxu(values, hot).astype(BF)


def grid_kernel(channels, got, out):
    height, padded, breadth = out.shape
    slots = got.shape[0]
    turn, lat_row, _, _, lon = turned(got, channels, padded)
    values = turn.astype(BF)
    col_hot = (lax.broadcasted_iota(jnp.int32, (slots, breadth), 1) == lon).astype(BF)
    step = 8

    def body(block, _):
        lhs = jnp.concatenate(
            [values * (lat_row == block * step + k).astype(F32).astype(BF) for k in range(step)], axis=0)
        out[pl.ds(block * step, step)] = mxu(lhs, col_hot).reshape(step, padded, breadth)
        return 0

    lax.fori_loop(0, height // step, body, 0)


def main_kernel(channels, hidden, flags, got, inner, north, south, from_east, from_west, from_ne, from_se,
                from_nw, from_sw, slope, w_n, w_m, p_t, p_j, g3, first_out, second_out, reply,
                field, strip, ga, xb, vec, hi, y1):
    height, padded, breadth = inner.shape
    wide = breadth + LANES
    ext = height + 2 * HALO

    def is_in(i):
        above = (i >= HALO) | (flags[0] == 1)
        below = (i < height + HALO) | (flags[1] == 1)
        return (above & below).astype(F32)

    blocks = strip.shape[0]
    last = (height + HALO) * SIDE // LANES
    for k in range(blocks):
        part = pl.ds(k * LANES, LANES)
        q = from_east[:, part].astype(F32) + from_west[:, part].astype(F32)
        if k == 0:
            q = q + from_nw[...].astype(F32) + from_ne[...].astype(F32)
        if k == last:
            q = q + from_sw[...].astype(F32) + from_se[...].astype(F32)
        strip[k] = q

    per = LANES // SIDE

    def pull(i, y):
        u = mxu(p_t[...], y.astype(BF))
        ga[i] = (slope[i].astype(F32) * u).astype(BF)

    def begin(i, main):
        shift = LANES - (i % per) * SIDE - HALO
        shift = jnp.where(shift < 0, shift + LANES, shift)
        edge = pltpu.roll(strip[i // per], shift, 1)
        whole = jnp.concatenate([main, edge], axis=1)
        field[i] = whole
        pull(i, whole)

    def from_north(i, _):
        begin(i, north[i].astype(F32))
        return 0

    def from_inner(i, _):
        begin(i, inner[i - HALO])
        return 0

    def from_south(i, _):
        begin(i, south[i - (HALO + height)].astype(F32))
        return 0

    lax.fori_loop(0, HALO, from_north, 0, unroll=True)
    lax.fori_loop(HALO, HALO + height, from_inner, 0, unroll=2)
    lax.fori_loop(HALO + height, ext, from_south, 0, unroll=True)

    def spread(i, y):
        rows = ga[pl.ds(i - 1, 3)].reshape(3 * hidden, wide)
        o = mxu(w_n[...], rows)
        return (y + o[padded : 2 * padded] + pltpu.roll(o[:padded], wide - 1, 1)
                + pltpu.roll(o[2 * padded :], 1, 1))

    def tangent(i, v):
        rows = xb[pl.ds(i - 1, 3)].reshape(3 * padded, wide)
        o = mxu(w_m[...], rows)
        h = (o[hidden : 2 * hidden] + pltpu.roll(o[:hidden], 1, 1)
             + pltpu.roll(o[2 * hidden :], wide - 1, 1))
        act = (slope[i].astype(F32) * h).astype(BF)
        return v + mxu(p_j[...], act)

    def gram_of(s):
        s_hi = s.astype(BF)
        s_lo = (s - s_hi.astype(F32)).astype(BF)
        return mxu(g3[...], jnp.concatenate([s_hi, s_hi, s_lo], axis=0))

    def n_first(i, _):
        v = spread(i, field[i])
        vec[i] = v
        xb[i] = (v * is_in(i)).astype(BF)
        return 0

    lax.fori_loop(1, ext - 1, n_first, 0, unroll=2)

    def m_first(i, _):
        s = tangent(i, vec[i])
        cell_weight = field[i][channels : channels + 1]
        y = cell_weight * gram_of(s)
        hi[i, :padded] = s[:, :breadth].astype(BF)
        y1[i] = y
        pull(i, y)
        return 0

    lax.fori_loop(2, ext - 2, m_first, 0, unroll=2)

    def keep_first(i, _):
        first_out[i] = vec[i + HALO][:, :breadth]
        return 0

    lax.fori_loop(0, height, keep_first, 0, unroll=2)

    def n_second(i, _):
        v = spread(i, y1[i])
        vec[i] = v
        xb[i] = (v * is_in(i)).astype(BF)
        return 0

    lax.fori_loop(3, ext - 3, n_second, 0, unroll=2)

    turn, lat_row, lon_row, _, _ = turned(got, channels, padded)
    slots = got.shape[0]
    col_hot = (lax.broadcasted_iota(jnp.int32, (breadth, slots), 0) == lon_row).astype(BF)

    def m_second(i, rows):
        v = vec[i]
        s = tangent(i, v)
        second_out[i - HALO] = v[:, :breadth]
        hi[i, padded:] = s[:, :breadth].astype(BF)
        return rows + mxu(hi[i], col_hot) * (lat_row == i - HALO).astype(F32)

    rows = lax.fori_loop(HALO, HALO + height, m_second, jnp.zeros((2 * padded, slots), F32))
    row0, row1 = rows[:padded], rows[padded:]
    weight = turn[channels : channels + 1]
    curved0 = gram_of(row0) * weight
    curved1 = gram_of(row1) * weight
    real = lax.broadcasted_iota(jnp.int32, (padded, slots), 0) < channels
    first = jnp.where(real, turn, 0.0)

    def total(x):
        return jnp.sum(jnp.sum(x, axis=0, keepdims=True), axis=1, keepdims=True)

    sums = (total(first * row0), total(curved0 * row0), total(curved0 * row1), total(curved1 * row1))
    lane = lax.broadcasted_iota(jnp.int32, (1, LANES), 1)
    pieces = jnp.zeros((1, LANES), F32)
    for number, value in enumerate(sums):
        for part, piece in enumerate(split3(value)):
            pieces = jnp.where(lane == channels + 3 + 3 * number + part, piece.astype(F32), pieces)
    filler = jnp.zeros((LANES - padded, slots), F32)
    turned0 = jnp.concatenate([row0, filler], axis=0).T
    turned1 = jnp.concatenate([row1, filler], axis=0).T
    cap = reply_cap(slots, flags)
    leads = lax.broadcasted_iota(jnp.int32, (slots, LANES), 0)
    is_lead = (leads - (leads // cap) * cap) == 0
    lanes = lax.broadcasted_iota(jnp.int32, (slots, LANES), 1)
    reply[:, :LANES] = jnp.where(lanes < channels, turned0, jnp.where(is_lead, pieces, 0.0)).astype(BF)
    reply[:, LANES:] = turned1.astype(BF)


def reply_cap(slots, flags):
    return flags[2]


def scalars(reply, channels):
    sums = jnp.sum(reply[:, :LANES].astype(F32), axis=0, keepdims=True)

    def value(number):
        at = channels + 3 + 3 * number
        return sums[:, at : at + 1] + sums[:, at + 1 : at + 2] + sums[:, at + 2 : at + 3]

    a00, a01, a11, d11 = (value(n) for n in range(4))
    step0 = a00 / (a00 + a01)
    keep = 1.0 - step0
    norm1 = keep * keep * a00 - 2.0 * step0 * keep * a01 + step0 * step0 * a11
    c0 = keep + norm1 / a00
    c1 = -step0
    curve = (c0 * c0 * (a00 + a01) + 2.0 * c0 * c1 * (a01 + a11) + c1 * c1 * (a11 + d11))
    step1 = norm1 / curve
    return step0 + step1 * c0, step1 * c1


def final_kernel(channels, back, slot, dep, jac, first, second, increment, departures):
    slots = back.shape[0]
    rows = dep.shape[0]
    a, b = scalars(back, channels)
    place = (lax.broadcasted_iota(jnp.int32, (rows, slots), 1) == slot[...]).astype(BF)
    own = mxu(place, back[...])
    padded = jac.shape[0]
    state = a * own[:, :padded] + b * own[:, LANES : LANES + padded]
    departures[...] = dep[...] - mxu(state, jac[...], precision=lax.Precision.HIGHEST)
    increment[...] = a[None] * first[...] + b[None] * second[...]


def neighbours(axis, by, periodic):
    count = lax.axis_size(axis)
    pairs = [(i, (i + by)) for i in range(count)]
    return [(i, j % count) for i, j in pairs if periodic or 0 <= j < count]


def shift2(x, by_lat, by_lon):
    n_lat, n_lon = lax.axis_size("lat"), lax.axis_size("lon")
    pairs = [(i * n_lon + j, (i + by_lat) * n_lon + (j + by_lon) % n_lon)
             for i in range(n_lat) for j in range(n_lon) if 0 <= i + by_lat < n_lat]
    return lax.ppermute(x, ("lat", "lon"), pairs)


def wide_slope(slope):
    x = jnp.transpose(slope, (1, 0, 2))
    low = shift2(x[-HALO:], 1, 0)
    high = shift2(x[:HALO], -1, 0)
    x = jnp.concatenate([low, x, high], axis=0)
    left = shift2(x[:, :, -HALO:], 0, 1)
    right = shift2(x[:, :, :HALO], 0, -1)
    gap = jnp.zeros(x.shape[:2] + (LANES - 2 * HALO,), x.dtype)
    return jnp.concatenate([x, right, gap, left], axis=2)


def on_device(departure_in, obs_owner, obs_cell, obs_count, qc_mask, channel_weight, jacobian,
              conv_taps, projection, slope):
    channels, hidden = projection.shape
    height, breadth = slope.shape[1], slope.shape[2]
    tiles = lax.axis_size(("lat", "lon"))
    rows, radiances = departure_in.shape
    cap = max(2, 3 * rows // (2 * tiles))
    slots = tiles * cap
    padded = -(-channels // 16) * 16
    wide = breadth + LANES
    ext = height + 2 * HALO
    strip = -(-(ext * SIDE) // LANES) * LANES
    more = padded - channels

    def shape(dims, kind=F32):
        return jax.ShapeDtypeStruct(dims, kind)

    jac = jnp.pad(jacobian, ((0, more), (0, 0)))
    weight = channel_weight[None, :]
    send, slot = call(
        functools.partial(pack_kernel, tiles, cap, breadth, channels),
        (shape((slots, LANES), BF), shape((rows, 1), jnp.int32)),
        (obs_count, departure_in, obs_owner.reshape(1, rows), obs_owner, obs_cell[None, :],
         qc_mask[None, :], weight, jac),
        smem=1,
    )

    def swap(x):
        return lax.all_to_all(x.reshape(tiles, cap, -1), ("lat", "lon"), split_axis=0, concat_axis=0,
                              tiled=True).reshape(slots, -1)

    got = swap(send)

    gram = jnp.dot(jac * weight, jac.T, precision=lax.Precision.HIGHEST)
    gram_hi = gram.astype(BF)
    gram_lo = (gram - gram_hi.astype(F32)).astype(BF)
    g3 = jnp.concatenate([gram_hi, gram_lo, gram_hi], axis=1)
    taps = jnp.pad(conv_taps, ((0, 0), (0, 0), (0, more))).reshape(3, 3, hidden, padded)
    w_m = jnp.transpose(taps, (1, 2, 0, 3)).reshape(3 * hidden, 3 * padded)
    w_n = jnp.transpose(taps[::-1], (1, 3, 0, 2)).reshape(3 * padded, 3 * hidden)
    p_j = jnp.pad(projection, ((0, more), (0, 0)))
    p_t = p_j.T
    slope_wide = wide_slope(slope)

    edge = (HALO, padded, breadth)
    north, south, west, east, nw, sw, ne, se = call(
        functools.partial(edge_kernel, channels, height, breadth),
        (shape(edge, BF),) * 2 + (shape((padded, strip), BF),) * 2 + (shape((padded, LANES), BF),) * 4,
        (got,),
    )
    from_south = shift2(north, -1, 0)
    from_north = shift2(south, 1, 0)
    from_east = shift2(west, 0, -1)
    from_west = shift2(east, 0, 1)
    from_se = shift2(nw, -1, -1)
    from_ne = shift2(sw, 1, -1)
    from_sw = shift2(ne, -1, 1)
    from_nw = shift2(se, 1, 1)
    inner = call(functools.partial(grid_kernel, channels), shape((height, padded, breadth)), (got,))

    at = lax.axis_index("lat")
    flags = jnp.stack([at > 0, at < lax.axis_size("lat") - 1, cap]).astype(jnp.int32)
    first, second, reply = call(
        functools.partial(main_kernel, channels, hidden),
        (shape((height, padded, breadth)),) * 2 + (shape((slots, 2 * LANES), BF),),
        (flags, got, inner, from_north, from_south, from_east, from_west, from_ne, from_se, from_nw,
         from_sw, slope_wide, w_n, w_m, p_t, p_j, g3),
        scratch=[
            pltpu.VMEM((ext, padded, wide), F32),
            pltpu.VMEM((strip // LANES, padded, LANES), F32),
            pltpu.VMEM((ext, hidden, wide), BF),
            pltpu.VMEM((ext, padded, wide), BF),
            pltpu.VMEM((ext, padded, wide), F32),
            pltpu.VMEM((ext, 2 * padded, breadth), BF),
            pltpu.VMEM((ext, padded, wide), F32),
        ],
        smem=1,
        vmem=116,
    )
    back = swap(reply)
    first = jnp.transpose(first, (1, 0, 2))[:channels]
    second = jnp.transpose(second, (1, 0, 2))[:channels]
    return call(
        functools.partial(final_kernel, channels),
        (shape((channels, height, breadth)), shape((rows, radiances))),
        (back, slot, departure_in, jac, first, second),
    )


def solution(mesh):
    placed = (
        P(("lat", "lon"), None),
        P(("lat", "lon"), None),
        P(("lat", "lon")),
        P(("lat", "lon")),
        P(("lat", "lon")),
        P(),
        P(),
        P(),
        P(),
        P(None, "lat", "lon"),
    )
    return jax.shard_map(
        on_device,
        mesh=mesh,
        in_specs=placed,
        out_specs=(P(None, "lat", "lon"), P(("lat", "lon"), None)),
        check_vma=False,
    )
```

time: 614 us -> 202 us (0.33); the launches traced: 604 us -> 201 us
  matrix products: 225 us -> 0.23 us
  blocking collectives: 122 us -> 0 us
  Pallas kernels: 0 us -> 114 us
  other arithmetic: 72 us -> 5.15 us
  local copies, waits for them, and re-layouts: 92.4 us -> 35 us
  waiting for transfers between devices: 27 us -> 5.14 us
  starting transfers between devices: 58.8 us -> 40.7 us
    dot_general x62 -> x1, matrix products: 225 us -> 0.23 us  [on_device(): gram = jnp.dot(jac * weight, jac.T, precision=lax.Precision.HIGHEST)]
    psum x3 -> x0, blocking collectives: 122 us -> none  [inner_sum(): return lax.psum(jnp.sum(left * right), ('lat', 'lon'))]
    pallas_call x0 -> x5, Pallas kernels: none -> 114 us  [call(): pl.pallas_call(kernel, out_shape=outs, in_specs=[space(i) for i in range(...]
    concatenate x12 -> x3, other arithmetic: 36.4 us -> 4.56 us  [the longest x1 3.63 us: wide_slope(): return jnp.concatenate([x, right, gap, left], axis=2)]
    slice x25 -> x6, local copies, waits for them, and re-layouts: 32.7 us -> 8.57 us  [the longest x2 3.61 us: wide_slope(): right = shift2(x[:, :, :HALO], 0, -1)]
    all_to_all x4 -> x2, waiting for transfers between devices: 21.9 us -> 1.2 us  [swap(): lax.all_to_all(x.reshape(tiles, cap, -1), ('lat', 'lon'), split_axis=0, c...]
    reshape x4 -> x5, local copies, waits for them, and re-layouts: 17.6 us -> 1.93 us  [the longest x2 0.9 us: on_device(): jnp.transpose(taps[::-1], (1, 3, 0, 2)).reshape(3 * padded, 3 * hidden)]
    ppermute x24 -> x12, starting transfers between devices: 41.6 us -> 26.1 us  [shift2(): return lax.ppermute(x, ('lat', 'lon'), pairs)]
  transfers between devices with their start and end apart: 28 -> 14, of which waited for: 7 -> 2; matrix products, arithmetic and copies ran while one was open for 17% -> 16% of each run, Pallas kernels for 0% -> 2%
where the time goes in v1:
time: 202 us; the launch traced here: 201 us
  Pallas kernels  114 us (56%)
  starting transfers between devices  40.7 us (20%)
  local copies, waits for them, and re-layouts  35 us (17%)
  other arithmetic  5.15 us (3%)
  waiting for transfers between devices  5.14 us (3%)
    pallas_call x5, Pallas kernels, call(): pl.pallas_call(kernel, out_shape=outs, in_specs=[space(i) for i in range(...  114 us
    ppermute x12, starting transfers between devices, shift2(): return lax.ppermute(x, ('lat', 'lon'), pairs)  26.1 us
    all_to_all x2, starting transfers between devices, swap(): lax.all_to_all(x.reshape(tiles, cap, -1), ('lat', 'lon'), split_axis=0, c...  14.6 us
    unnamed x43, local copies, waits for them, and re-layouts  9.89 us
    transpose x1, local copies, waits for them, and re-layouts, on_device(): second = jnp.transpose(second, (1, 0, 2))[:channels]  7.87 us
    ppermute x2, local copies, waits for them, and re-layouts, shift2(): return lax.ppermute(x, ('lat', 'lon'), pairs)  4.34 us
  transfers between devices with their start and end apart: 14, of which 2 were waited for; matrix products, arithmetic and copies ran while one was open for 16% of the time, Pallas kernels for 2%

profile of v1, /device:TPU:0, one launch (start us, length us, event | category | flops | bytes accessed | tf_op | source)
XLA Modules:
  0.0 201.5 jit_solution(8614215619941496823)
XLA Ops:
  0.6 0.0 copy-start.9
  0.6 0.0 copy-start.6
  1.4 0.8 copy.29.owner_col
  2.2 0.9 pad.12.jac
  3.1 1.0 copy-done.2
  4.1 0.7 copy-done.4
  4.8 0.7 copy-done.5
  5.5 0.7 copy-done.7
  6.2 0.7 copy-done.8
  6.9 1.9 shard_map.113
  8.7 7.3 %all-to-all-start = ((bf16[32,24,128]{2,1,0:T(8,128)(2,1)}), bf16[32,24,128]{2,1,0:T(8,128)(2,1)S(1)}, u32[]{:S(2)}, u32[]{:S(2)}) async-start(bf16[32,24,128]{2,1,0:T(8,128)(2,1)} %bitcast.6), calls=%async_computation | async-start | bytes 393216 | tf_op jit(solution)/shard_map/all_to_all | solution.py:362
  16.0 1.9 copy.46
  18.0 3.7 %collective-permute-start.8 = (bf16[4,64,256]{2,1,0:T(8,128)(2,1)S(1)}, bf16[4,64,256]{2,1,0:T(8,128)(2,1)S(1)}, u32[]{:S(2)}, u32[]{:S(2)}) collective-permute-start(bf16[4,64,256]{2,1,0:T(8,128)(2,1)S(1)} %get-tuple-element.32), channel_id=1, source_target_pairs={{0,4},{1,5},{2,6},{3,7},{4,8},{5,9},{6,10},{7,11},{8,12},{9,13},{1... | collective-permute-start | bytes 393224 | tf_op jit(solution)/shard_map/ppermute | solution.py:320
  21.7 1.3 collective-permute-start.9
  23.0 0.2 subtract_convert_fusion
  23.2 0.1 copy.37
  23.4 0.6 fusion.6
  24.0 0.7 pad_maximum_fusion.2.g3
  24.7 0.1 copy.35
  24.9 0.1 reverse_bitcast_fusion
  24.9 0.0 collective-permute-done.8
  25.0 3.9 %collective-permute-done.9 = bf16[4,64,256]{2,1,0:T(8,128)(2,1)S(1)} collective-permute-done((bf16[4,64,256]{2,1,0:T(8,128)(2,1)S(1)}, bf16[4,64,256]{2,1,0:T(8,128)(2,1)S(1)}, u32[]{:S(2)}, u32[]{:S(2)}) %collective-permute-start.9) | collective-permute-done | bytes 131104 | tf_op jit(solution)/shard_map/ppermute | solution.py:320
  28.9 0.6 copy-done.10
  29.5 0.2 pad_maximum_fusion.1
  29.7 1.4 fusion.4
  31.1 2.2 %copy.31 = bf16[56,64,4]{1,0,2:T(8,128)(2,1)} copy(bf16[56,64,4]{2,1,0:T(8,128)(2,1)} %get-tuple-element.30) | data formatting | bytes 57344 | tf_op jit(solution)/shard_map/slice | solution.py:329
  33.3 1.0 copy.32
  34.4 1.7 collective-permute-start.10
  36.1 2.2 %shard_map.115 = (bf16[4,80,256]{2,1,0:T(8,128)(2,1)S(1)}, bf16[4,80,256]{2,1,0:T(8,128)(2,1)S(1)}, bf16[80,512]{1,0:T(8,128)(2,1)S(1)}, bf16[80,512]{1,0:T(8,12...) custom-call(bf16[768,128]{1,0:T(8,128)(2,1)S(1)} %bitcast.27), custom_call_target="tpu_custom_call" | custom-call | tf_op jit(solution)/shard_map/pallas_call | solution.py:28
  38.3 3.7 %collective-permute-start.4 = (bf16[80,128]{1,0:T(8,128)(2,1)S(1)}, bf16[80,128]{1,0:T(8,128)(2,1)S(1)}, u32[]{:S(2)}, u32[]{:S(2)}) collective-permute-start(bf16[80,128]{1,0:T(8,128)(2,1)S(1)} %get-tuple-element.20), channel_id=1, source_target_pairs={{0,7},{1,4},{2,5},{3,6},{4,11},{5,8},{6,9},{7,10},{8,15},{9,12},{1... | collective-permute-start | bytes 61448 | tf_op jit(solution)/shard_map/ppermute | solution.py:320
  42.1 1.3 collective-permute-start.5
  43.4 4.9 %collective-permute-start.6 = (bf16[80,128]{1,0:T(8,128)(2,1)S(1)}, bf16[80,128]{1,0:T(8,128)(2,1)}, u32[]{:S(2)}, u32[]{:S(2)}) collective-permute-start(bf16[80,128]{1,0:T(8,128)(2,1)S(1)} %get-tuple-element.22), channel_id=1, source_target_pairs={{0,5},{1,6},{2,7},{3,4},{4,9},{5,10},{6,11},{7,8},{8,13},{9,14},{1... | collective-permute-start | bytes 61448 | tf_op jit(solution)/shard_map/ppermute | solution.py:320
  48.2 0.6 pad_add_fusion.flags
  48.8 0.1 copy.47
  48.9 0.7 copy.39.p_t
  49.6 0.8 reshape.34.w_m
  50.4 0.1 reshape.33
  50.5 0.8 copy.38.w_n
  51.3 0.1 pad.22.clone
  51.4 2.2 %copy.33 = bf16[56,64,4]{2,1,0:T(8,128)(2,1)} copy(bf16[56,64,4]{1,0,2:T(8,128)(2,1)} %collective-permute-done.10) | data formatting | bytes 57344 | tf_op jit(solution)/shard_map/ppermute | solution.py:320
  53.6 0.0 collective-permute-done.11
  53.6 2.2 %copy.34 = bf16[56,64,4]{2,1,0:T(8,128)(2,1)} copy(bf16[56,64,4]{1,0,2:T(8,128)(2,1)} %collective-permute-done.11) | data formatting | bytes 57344 | tf_op jit(solution)/shard_map/ppermute | solution.py:320
  55.7 1.3 collective-permute-start.7
  57.0 2.7 %collective-permute-start.2 = (bf16[80,512]{1,0:T(8,128)(2,1)S(1)}, bf16[80,512]{1,0:T(8,128)(2,1)S(1)}, u32[]{:S(2)}, u32[]{:S(2)}) collective-permute-start(bf16[80,512]{1,0:T(8,128)(2,1)S(1)} %get-tuple-element.18), channel_id=1, source_target_pairs={{0,3},{1,0},{2,1},{3,2},{4,7},{5,4},{6,5},{7,6},{8,11},{9,8},{10,9... | collective-permute-start | bytes 245768 | tf_op jit(solution)/shard_map/ppermute | solution.py:320
  59.7 0.0 collective-permute-done.4.from_ne
  59.7 0.0 collective-permute-done.5.from_se
  59.7 4.0 %collective-permute-start = (bf16[4,80,256]{2,1,0:T(8,128)(2,1)S(1)}, bf16[4,80,256]{2,1,0:T(8,128)(2,1)S(1)}, u32[]{:S(2)}, u32[]{:S(2)}) collective-permute-start(bf16[4,80,256]{2,1,0:T(8,128)(2,1)S(1)} %get-tuple-element.16), channel_id=1, source_target_pairs={{0,4},{1,5},{2,6},{3,7},{4,8},{5,9},{6,10},{7,11},{8,12},{9,13},{1... | collective-permute-start | bytes 491528 | tf_op jit(solution)/shard_map/ppermute | solution.py:320
  63.8 1.5 collective-permute-start.1
  65.3 3.6 %pad_maximum_fusion.slope = bf16[56,64,384]{2,1,0:T(8,128)(2,1)} fusion(bf16[56,64,4]{2,1,0:T(8,128)(2,1)} %copy.34, bf16[56,64,4]{2,1,0:T(8,128)(2,1)} %copy.33, bf16[4,64,256]{2,1,0:T(8,128)(2,1)S(1)} %copy-done.11, bf16[48,64,256]{2,1,0:T(8,128)(2,1)S(1)} %bitcast.37, bf16[4,64,256]{2,1,0:T(8,128)(2,1)S(1)} %collective-permute-done.8, ...), kind=kLoop, calls=%fused_computation.2 | loop fusion | flops 16515072 | bytes 4645632 | tf_op jit(solution)/shard_map/concatenate | solution.py:331
  68.9 2.8 %shard_map.114.inner = f32[48,80,256]{2,1,0:T(8,128)S(1)} custom-call(bf16[768,128]{1,0:T(8,128)(2,1)S(1)} %bitcast.28), custom_call_target="tpu_custom_call" | custom-call | tf_op jit(solution)/shard_map/pallas_call | solution.py:28
  71.8 1.9 copy-done
  73.6 0.0 collective-permute-done.2.from_east
  73.7 0.5 copy-done.18
  74.2 0.0 copy-done.15
  74.3 0.0 copy-done.16
  74.3 0.1 copy-done.12
  74.4 0.1 copy-done.13
  74.4 100.4 %shard_map.116 = (f32[48,80,256]{2,1,0:T(8,128)}, f32[48,80,256]{2,1,0:T(8,128)}, bf16[768,256]{1,0:T(8,128)(2,1)}) custom-call(s32[3]{0:T(128)} %pad_add_fusion.flags, bf16[768,128]{1,0:T(8,128)(2,1)} %bitcast.29, f32[48,80,256]{2,1,0:T(8,128)} %copy-done, bf16[4,80,256]{2,1,0:T(8,128)(2,1)} %copy-done.12, bf16[4,80,256]{2,1,0:T(8,128)(2,1)} %copy-done.13, ...), custom_call_target="tpu_custom_call" | custom-call | tf_op jit(solution)/shard_map/pallas_call | solution.py:28
  174.9 7.4 %all-to-all-start.1 = ((bf16[32,24,256]{2,1,0:T(8,128)(2,1)}), bf16[32,24,256]{2,1,0:T(8,128)(2,1)S(1)}, u32[]{:S(2)}, u32[]{:S(2)}) async-start(bf16[32,24,256]{2,1,0:T(8,128)(2,1)} %bitcast.41), calls=%async_computation.1 | async-start | bytes 786432 | tf_op jit(solution)/shard_map/all_to_all | solution.py:362
  182.2 7.9 %copy_bitcast_fusion = (f32[80,48,256]{2,1,0:T(8,128)S(1)}, f32[80,48,256]{2,1,0:T(8,128)S(1)}) fusion(f32[48,80,256]{2,1,0:T(8,128)} %get-tuple-element.27, f32[48,80,256]{2,1,0:T(8,128)} %get-tuple-element.26), kind=kLoop, calls=%fused_computation | loop fusion | bytes 15728640 | tf_op jit(solution)/shard_map/transpose | solution.py:415
  190.1 2.0 slice.29.second
  192.0 1.9 slice.28.first
  194.0 1.2 all-to-all-done.1
  195.2 6.3 %shard_map.117 = (f32[69,48,256]{2,1,0:T(8,128)}, f32[512,256]{1,0:T(8,128)}) custom-call(bf16[768,256]{1,0:T(8,128)(2,1)S(1)} %bitcast.30, s32[512,1]{1,0:T(8,128)S(1)} %get-tuple-element.25.slot, f32[512,256]{1,0:T(8,128)S(1)} %copy-done.3, f32[80,256]{1,0:T(8,128)S(1)} %pad.12.jac, f32[69,48,256]{2,1,0:T(8,128)} %slice.28.first, f32[69,48,256]{2,1,0:T(8,128)} %slice.29.second), custom_call_target="tpu_custom_call" | custom-call | tf_op jit(solution)/shard_map/pallas_call | solution.py:28
  (38 shorter events, 0.1 us)
Async XLA Ops:
  0.6 22.4 %copy-start.9 = (f32[69,256]{1,0:T(8,128)S(1)}, f32[69,256]{1,0:T(8,128)}, u32[]{:S(2)}) copy-start(f32[69,256]{1,0:T(8,128)} %param.16) | copy-start | bytes 211972
  0.6 22.4 %copy-start.6 = (f32[256]{0:T(256)S(1)}, f32[256]{0:T(256)}, u32[]{:S(2)}) copy-start(f32[256]{0:T(256)} %param.15) | copy-start | bytes 3076
  0.7 22.6 %copy-start.19 = (bf16[69,64]{0,1:T(8,128)(2,1)S(1)}, bf16[69,64]{0,1:T(8,128)(2,1)}, u32[]{:S(2)}) copy-start(bf16[69,64]{0,1:T(8,128)(2,1)} %param.18) | copy-start | bytes 26500
  0.7 24.0 %copy-start.14 = (bf16[9,64,69]{2,1,0:T(8,128)(2,1)S(1)}, bf16[9,64,69]{2,1,0:T(8,128)(2,1)}, u32[]{:S(2)}) copy-start(bf16[9,64,69]{2,1,0:T(8,128)(2,1)} %param.17) | copy-start | bytes 238468
  3.1 1.0 copy-start.2
  4.1 0.7 copy-start.4
  4.8 0.7 copy-start.5
  5.5 0.7 copy-start.7
  6.2 0.7 copy-start.8
  8.7 27.4 %all-to-all-start = ((bf16[32,24,128]{2,1,0:T(8,128)(2,1)}), bf16[32,24,128]{2,1,0:T(8,128)(2,1)S(1)}, u32[]{:S(2)}, u32[]{:S(2)}) async-start(bf16[32,24,128]{2,1,0:T(8,128)(2,1)} %bitcast.6), calls=%async_computation | async-start | bytes 393216 | tf_op jit(solution)/shard_map/all_to_all | solution.py:362
  18.0 6.9 %collective-permute-start.8 = (bf16[4,64,256]{2,1,0:T(8,128)(2,1)S(1)}, bf16[4,64,256]{2,1,0:T(8,128)(2,1)S(1)}, u32[]{:S(2)}, u32[]{:S(2)}) collective-permute-start(bf16[4,64,256]{2,1,0:T(8,128)(2,1)S(1)} %get-tuple-element.32), channel_id=1, source_target_pairs={{0,4},{1,5},{2,6},{3,7},{4,8},{5,9},{6,10},{7,11},{8,12},{9,13},{1... | collective-permute-start | bytes 393224 | tf_op jit(solution)/shard_map/ppermute | solution.py:320
  21.7 7.2 %collective-permute-start.9 = (bf16[4,64,256]{2,1,0:T(8,128)(2,1)S(1)}, bf16[4,64,256]{2,1,0:T(8,128)(2,1)S(1)}, u32[]{:S(2)}, u32[]{:S(2)}) collective-permute-start(bf16[4,64,256]{2,1,0:T(8,128)(2,1)S(1)} %get-tuple-element.33), channel_id=1, source_target_pairs={{4,0},{5,1},{6,2},{7,3},{8,4},{9,5},{10,6},{11,7},{12,8},{13,9},{1... | collective-permute-start | bytes 393224 | tf_op jit(solution)/shard_map/ppermute | solution.py:320
  28.9 0.6 copy-start.10
  34.4 30.9 %copy-start.11 = (bf16[4,64,256]{2,1,0:T(8,128)(2,1)S(1)}, bf16[4,64,256]{2,1,0:T(8,128)(2,1)}, u32[]{:S(2)}) copy-start(bf16[4,64,256]{2,1,0:T(8,128)(2,1)} %copy-done.10) | copy-start | bytes 393220
  34.4 19.2 %collective-permute-start.11 = (bf16[56,64,4]{1,0,2:T(8,128)(2,1)}, bf16[56,64,4]{1,0,2:T(8,128)(2,1)}, u32[]{:S(2)}, u32[]{:S(2)}) collective-permute-start(bf16[56,64,4]{1,0,2:T(8,128)(2,1)} %copy.32), channel_id=1, source_target_pairs={{0,1},{1,2},{2,3},{3,0},{4,5},{5,6},{6,7},{7,4},{8,9},{9,10},{10,1... | collective-permute-start | bytes 86024 | tf_op jit(solution)/shard_map/ppermute | solution.py:320
  34.4 17.0 %collective-permute-start.10 = (bf16[56,64,4]{1,0,2:T(8,128)(2,1)}, bf16[56,64,4]{1,0,2:T(8,128)(2,1)}, u32[]{:S(2)}, u32[]{:S(2)}) collective-permute-start(bf16[56,64,4]{1,0,2:T(8,128)(2,1)} %copy.31), channel_id=1, source_target_pairs={{0,3},{1,0},{2,1},{3,2},{4,7},{5,4},{6,5},{7,6},{8,11},{9,8},{10,9... | collective-permute-start | bytes 86024 | tf_op jit(solution)/shard_map/ppermute | solution.py:320
  36.1 32.8 %copy-start.1 = (bf16[32,24,128]{2,1,0:T(8,128)(2,1)}, bf16[32,24,128]{2,1,0:T(8,128)(2,1)S(1)}, u32[]{:S(2)}) copy-start(bf16[32,24,128]{2,1,0:T(8,128)(2,1)S(1)} %all-to-all-done) | copy-start | bytes 589828
  38.3 21.4 %collective-permute-start.4 = (bf16[80,128]{1,0:T(8,128)(2,1)S(1)}, bf16[80,128]{1,0:T(8,128)(2,1)S(1)}, u32[]{:S(2)}, u32[]{:S(2)}) collective-permute-start(bf16[80,128]{1,0:T(8,128)(2,1)S(1)} %get-tuple-element.20), channel_id=1, source_target_pairs={{0,7},{1,4},{2,5},{3,6},{4,11},{5,8},{6,9},{7,10},{8,15},{9,12},{1... | collective-permute-start | bytes 61448 | tf_op jit(solution)/shard_map/ppermute | solution.py:320
  42.1 17.7 %collective-permute-start.5 = (bf16[80,128]{1,0:T(8,128)(2,1)S(1)}, bf16[80,128]{1,0:T(8,128)(2,1)}, u32[]{:S(2)}, u32[]{:S(2)}) collective-permute-start(bf16[80,128]{1,0:T(8,128)(2,1)S(1)} %get-tuple-element.21), channel_id=1, source_target_pairs={{4,3},{5,0},{6,1},{7,2},{8,7},{9,4},{10,5},{11,6},{12,11},{13,8},{... | collective-permute-start | bytes 61448 | tf_op jit(solution)/shard_map/ppermute | solution.py:320
  43.4 20.4 %collective-permute-start.6 = (bf16[80,128]{1,0:T(8,128)(2,1)S(1)}, bf16[80,128]{1,0:T(8,128)(2,1)}, u32[]{:S(2)}, u32[]{:S(2)}) collective-permute-start(bf16[80,128]{1,0:T(8,128)(2,1)S(1)} %get-tuple-element.22), channel_id=1, source_target_pairs={{0,5},{1,6},{2,7},{3,4},{4,9},{5,10},{6,11},{7,8},{8,13},{9,14},{1... | collective-permute-start | bytes 61448 | tf_op jit(solution)/shard_map/ppermute | solution.py:320
  55.7 17.9 %collective-permute-start.7 = (bf16[80,128]{1,0:T(8,128)(2,1)S(1)}, bf16[80,128]{1,0:T(8,128)(2,1)S(1)}, u32[]{:S(2)}, u32[]{:S(2)}) collective-permute-start(bf16[80,128]{1,0:T(8,128)(2,1)S(1)} %get-tuple-element.23), channel_id=1, source_target_pairs={{4,1},{5,2},{6,3},{7,0},{8,5},{9,6},{10,7},{11,4},{12,9},{13,10},{... | collective-permute-start | bytes 61448 | tf_op jit(solution)/shard_map/ppermute | solution.py:320
  57.0 16.6 %collective-permute-start.2 = (bf16[80,512]{1,0:T(8,128)(2,1)S(1)}, bf16[80,512]{1,0:T(8,128)(2,1)S(1)}, u32[]{:S(2)}, u32[]{:S(2)}) collective-permute-start(bf16[80,512]{1,0:T(8,128)(2,1)S(1)} %get-tuple-element.18), channel_id=1, source_target_pairs={{0,3},{1,0},{2,1},{3,2},{4,7},{5,4},{6,5},{7,6},{8,11},{9,8},{10,9... | collective-permute-start | bytes 245768 | tf_op jit(solution)/shard_map/ppermute | solution.py:320
  59.7 12.0 %copy-start.17 = (bf16[80,128]{1,0:T(8,128)(2,1)}, bf16[80,128]{1,0:T(8,128)(2,1)S(1)}, u32[]{:S(2)}) copy-start(bf16[80,128]{1,0:T(8,128)(2,1)S(1)} %collective-permute-done.4.from_ne) | copy-start | bytes 61444
  59.7 13.9 %collective-permute-start.3 = (bf16[80,512]{1,0:T(8,128)(2,1)S(1)}, bf16[80,512]{1,0:T(8,128)(2,1)S(1)}, u32[]{:S(2)}, u32[]{:S(2)}) collective-permute-start(bf16[80,512]{1,0:T(8,128)(2,1)S(1)} %get-tuple-element.19), channel_id=1, source_target_pairs={{0,1},{1,2},{2,3},{3,0},{4,5},{5,6},{6,7},{7,4},{8,9},{9,10},{10,1... | collective-permute-start | bytes 245768 | tf_op jit(solution)/shard_map/ppermute | solution.py:320
  59.7 13.9 %collective-permute-start = (bf16[4,80,256]{2,1,0:T(8,128)(2,1)S(1)}, bf16[4,80,256]{2,1,0:T(8,128)(2,1)S(1)}, u32[]{:S(2)}, u32[]{:S(2)}) collective-permute-start(bf16[4,80,256]{2,1,0:T(8,128)(2,1)S(1)} %get-tuple-element.16), channel_id=1, source_target_pairs={{0,4},{1,5},{2,6},{3,7},{4,8},{5,9},{6,10},{7,11},{8,12},{9,13},{1... | collective-permute-start | bytes 491528 | tf_op jit(solution)/shard_map/ppermute | solution.py:320
  63.8 9.9 %collective-permute-start.1 = (bf16[4,80,256]{2,1,0:T(8,128)(2,1)S(1)}, bf16[4,80,256]{2,1,0:T(8,128)(2,1)S(1)}, u32[]{:S(2)}, u32[]{:S(2)}) collective-permute-start(bf16[4,80,256]{2,1,0:T(8,128)(2,1)S(1)} %get-tuple-element.17), channel_id=1, source_target_pairs={{4,0},{5,1},{6,2},{7,3},{8,4},{9,5},{10,6},{11,7},{12,8},{13,9},{1... | collective-permute-start | bytes 491528 | tf_op jit(solution)/shard_map/ppermute | solution.py:320
  71.8 1.9 copy-start
  73.6 0.6 copy-start.18
  73.6 0.6 copy-start.15
  73.7 0.7 copy-start.16
  73.7 0.7 copy-start.12
  73.7 0.7 copy-start.13
  174.9 20.3 %all-to-all-start.1 = ((bf16[32,24,256]{2,1,0:T(8,128)(2,1)}), bf16[32,24,256]{2,1,0:T(8,128)(2,1)S(1)}, u32[]{:S(2)}, u32[]{:S(2)}) async-start(bf16[32,24,256]{2,1,0:T(8,128)(2,1)} %bitcast.41), calls=%async_computation.1 | async-start | bytes 786432 | tf_op jit(solution)/shard_map/all_to_all | solution.py:362
  192.0 3.1 %copy-start.3 = (f32[512,256]{1,0:T(8,128)S(1)}, f32[512,256]{1,0:T(8,128)}, u32[]{:S(2)}) copy-start(f32[512,256]{1,0:T(8,128)} %dep.3) | copy-start | bytes 1572868

commit v2 on v1

--- a/solution.py
+++ b/solution.py
@@ -15,6 +15,7 @@
 BF = jnp.bfloat16
 F32 = jnp.float32
 INTERPRET = False
+G = (9, 13, 10, 12, 16)
 
 
 def mxu(a, b, dims=((1,), (0,)), precision=None):
@@ -85,7 +86,7 @@
     return jnp.where(keep, turn[:padded], 0.0), lat_row, lon_row, lat_col, lon_col
 
 
-def edge_kernel(channels, height, breadth, got, north, south, west, east, nw, sw, ne, se):
+def edge_kernel(channels, height, breadth, got, north, south, west, east):
     padded = north.shape[1]
     slots = got.shape[0]
     turn, lat_row, lon_row, lat, lon = turned(got, channels, padded)
@@ -94,22 +95,22 @@
     for out, first in ((north, 0), (south, height - HALO)):
         lhs = jnp.concatenate(
             [values * (lat_row == first + k).astype(F32).astype(BF) for k in range(HALO)], axis=0)
-        out[...] = mxu(lhs, col_hot).reshape(HALO, padded, breadth).astype(BF)
+        out[:HALO] = mxu(lhs, col_hot).reshape(HALO, padded, breadth).astype(BF)
     at_west, at_east = lon < HALO, lon >= breadth - HALO
     at_north, at_south = lat < HALO, lat >= height - HALO
     col_west, col_east = HALO + lon, lon - (breadth - HALO)
-    base = (height + HALO) * SIDE // LANES * LANES
-    for out, mask, row, col, offset in (
-        (west, at_west, lat + HALO, col_west, 0),
-        (east, at_east, lat + HALO, col_east, 0),
-        (nw, at_west & at_north, lat + height + HALO, col_west, base),
-        (sw, at_west & at_south, lat - (height - HALO), col_west, 0),
-        (ne, at_east & at_north, lat + height + HALO, col_east, base),
-        (se, at_east & at_south, lat - (height - HALO), col_east, 0),
-    ):
-        target = jnp.where(mask, row * SIDE + col - offset, -1)
-        hot = (lax.broadcasted_iota(jnp.int32, (slots, out.shape[1]), 1) == target).astype(BF)
-        out[...] = mxu(values, hot).astype(BF)
+
+    def place(mask, row, col, lanes):
+        target = jnp.where(mask, row * SIDE + col, -1)
+        hot = (lax.broadcasted_iota(jnp.int32, (slots, lanes), 1) == target).astype(BF)
+        return mxu(values, hot).astype(BF)
+
+    west[...] = place(at_west, lat + HALO, col_west, west.shape[1])
+    east[...] = place(at_east, lat + HALO, col_east, east.shape[1])
+    below = (height + HALO) % (LANES // SIDE)
+    for out, mask, row in ((north, at_north, lat + below), (south, at_south, lat - (height - HALO))):
+        out[HALO, :, :LANES] = place(mask & at_west, row, col_west, LANES)
+        out[HALO, :, LANES : 2 * LANES] = place(mask & at_east, row, col_east, LANES)
 
 
 def grid_kernel(channels, got, out):
@@ -129,124 +130,190 @@
     lax.fori_loop(0, height // step, body, 0)
 
 
-def main_kernel(channels, hidden, flags, got, inner, north, south, from_east, from_west, from_ne, from_se,
-                from_nw, from_sw, slope, w_n, w_m, p_t, p_j, g3, first_out, second_out, reply,
-                field, strip, ga, xb, vec, hi, y1):
+def strip_kernel(inner, north, south, west, east):
+    height, hidden, breadth = inner.shape
+    per = LANES // SIDE
+    lane = lax.broadcasted_iota(jnp.int32, (hidden, LANES), 1)
+    for block in range(west.shape[1] // LANES):
+        left = jnp.zeros((hidden, LANES), F32)
+        right = jnp.zeros((hidden, LANES), F32)
+        for k in range(per):
+            i = block * per + k
+            if i < HALO:
+                row = north[i]
+            elif i < HALO + height:
+                row = inner[i - HALO]
+            elif i < height + 2 * HALO:
+                row = south[i - HALO - height]
+            else:
+                break
+            row = row.astype(F32)
+            mine = (lane >= k * SIDE) & (lane < (k + 1) * SIDE)
+            left = jnp.where(mine, pltpu.roll(row[:, :LANES], (k * SIDE + HALO) % LANES, 1), left)
+            right = jnp.where(mine, pltpu.roll(row[:, breadth - LANES :], (k * SIDE + HALO) % LANES, 1), right)
+        west[:, block * LANES : (block + 1) * LANES] = left.astype(BF)
+        east[:, block * LANES : (block + 1) * LANES] = right.astype(BF)
+
+
+def join_kernel(height, west, east, from_north, from_south, slope_west, slope_east, to_west, to_east):
+    padded, strip = west.shape
+    last = (height + HALO) * SIDE // LANES
+    for k, own, slope, out in ((0, west, slope_west, to_west), (1, east, slope_east, to_east)):
+        corner = pl.ds(k * LANES, LANES)
+        for block in range(strip // LANES):
+            part = pl.ds(block * LANES, LANES)
+            q = own[:, part]
+            if block == 0:
+                q = q + from_north[HALO, :, corner]
+            if block == last:
+                q = q + from_south[HALO, :, corner]
+            out[:padded, part] = q
+        out[padded:] = slope[...]
+
+
+def main_kernel(channels, hidden, cap, flags, got, inner, north, south, from_east, from_west, slope_inner,
+                slope_north, slope_south, w_n, w_m, p_t, p_j, g3, first_out, second_out, reply,
+                field, slope, ga, xb, vec, hi, y1, found):
     height, padded, breadth = inner.shape
     wide = breadth + LANES
     ext = height + 2 * HALO
+    per = LANES // SIDE
 
     def is_in(i):
         above = (i >= HALO) | (flags[0] == 1)
         below = (i < height + HALO) | (flags[1] == 1)
         return (above & below).astype(F32)
 
-    blocks = strip.shape[0]
-    last = (height + HALO) * SIDE // LANES
-    for k in range(blocks):
-        part = pl.ds(k * LANES, LANES)
-        q = from_east[:, part].astype(F32) + from_west[:, part].astype(F32)
-        if k == 0:
-            q = q + from_nw[...].astype(F32) + from_ne[...].astype(F32)
-        if k == last:
-            q = q + from_sw[...].astype(F32) + from_se[...].astype(F32)
-        strip[k] = q
-
-    per = LANES // SIDE
-
-    def pull(i, y):
-        u = mxu(p_t[...], y.astype(BF))
-        ga[i] = (slope[i].astype(F32) * u).astype(BF)
-
-    def begin(i, main):
-        shift = LANES - (i % per) * SIDE - HALO
-        shift = jnp.where(shift < 0, shift + LANES, shift)
-        edge = pltpu.roll(strip[i // per], shift, 1)
-        whole = jnp.concatenate([main, edge], axis=1)
-        field[i] = whole
-        pull(i, whole)
-
-    def from_north(i, _):
-        begin(i, north[i].astype(F32))
+    def join(parts):
+        return jnp.concatenate(parts, axis=1)
+
+    def part(x, k):
+        return x[:, k * wide : (k + 1) * wide]
+
+    def pull(i, ys):
+        u = mxu(p_t[...], join([y.astype(BF) for y in ys]))
+        for k in range(len(ys)):
+            ga[i + k] = (slope[i + k].astype(F32) * part(u, k)).astype(BF)
+
+    lane = lax.broadcasted_iota(jnp.int32, (padded + hidden, LANES), 1)
+    from_the_west = lane % SIDE < HALO
+
+    def begin(i, mains, slopes, count):
+        at = pl.ds(pl.multiple_of(i // per * LANES, LANES), LANES)
+        both = jnp.where(from_the_west, from_west[:, at].astype(F32), from_east[:, at].astype(F32))
+        ys = []
+        for k in range(count):
+            shift = 2 * LANES - ((i % per) + k) * SIDE - HALO
+            edge = pltpu.roll(both, shift % LANES, 1)
+            y = join([mains[k].astype(F32), edge[:padded]])
+            field[i + k] = y
+            slope[i + k] = join([slopes[k], edge[padded:].astype(BF)])
+            ys.append(y)
+        pull(i, ys)
+
+    begin(0, [north[k] for k in range(HALO)], [slope_north[k] for k in range(HALO)], HALO)
+    begin(HALO + height, [south[k] for k in range(HALO)], [slope_south[k] for k in range(HALO)], HALO)
+
+    def middle(n, _):
+        i = n * HALO
+        begin(i + HALO, [inner[i + k] for k in range(HALO)], [slope_inner[i + k] for k in range(HALO)], HALO)
         return 0
 
-    def from_inner(i, _):
-        begin(i, inner[i - HALO])
-        return 0
-
-    def from_south(i, _):
-        begin(i, south[i - (HALO + height)].astype(F32))
-        return 0
-
-    lax.fori_loop(0, HALO, from_north, 0, unroll=True)
-    lax.fori_loop(HALO, HALO + height, from_inner, 0, unroll=2)
-    lax.fori_loop(HALO + height, ext, from_south, 0, unroll=True)
-
-    def spread(i, y):
-        rows = ga[pl.ds(i - 1, 3)].reshape(3 * hidden, wide)
-        o = mxu(w_n[...], rows)
-        return (y + o[padded : 2 * padded] + pltpu.roll(o[:padded], wide - 1, 1)
-                + pltpu.roll(o[2 * padded :], 1, 1))
-
-    def tangent(i, v):
-        rows = xb[pl.ds(i - 1, 3)].reshape(3 * padded, wide)
-        o = mxu(w_m[...], rows)
-        h = (o[hidden : 2 * hidden] + pltpu.roll(o[:hidden], 1, 1)
-             + pltpu.roll(o[2 * hidden :], wide - 1, 1))
-        act = (slope[i].astype(F32) * h).astype(BF)
-        return v + mxu(p_j[...], act)
+    lax.fori_loop(0, height // HALO, middle, 0)
+
+    def spread(i, ys):
+        o = mxu(w_n[...], join([ga[pl.ds(i + k - 1, 3)].reshape(3 * hidden, wide) for k in range(len(ys))]))
+        out = []
+        for k, y in enumerate(ys):
+            p = part(o, k)
+            out.append(y + p[padded : 2 * padded] + pltpu.roll(p[:padded], wide - 1, 1)
+                       + pltpu.roll(p[2 * padded :], 1, 1))
+        return out
+
+    def tangent(i, vs):
+        o = mxu(w_m[...], join([xb[pl.ds(i + k - 1, 3)].reshape(3 * padded, wide) for k in range(len(vs))]))
+        acts = []
+        for k in range(len(vs)):
+            p = part(o, k)
+            h = (p[hidden : 2 * hidden] + pltpu.roll(p[:hidden], 1, 1)
+                 + pltpu.roll(p[2 * hidden :], wide - 1, 1))
+            acts.append((slope[i + k].astype(F32) * h).astype(BF))
+        back = mxu(p_j[...], join(acts))
+        return [v + part(back, k) for k, v in enumerate(vs)]
 
     def gram_of(s):
         s_hi = s.astype(BF)
         s_lo = (s - s_hi.astype(F32)).astype(BF)
         return mxu(g3[...], jnp.concatenate([s_hi, s_hi, s_lo], axis=0))
 
-    def n_first(i, _):
-        v = spread(i, field[i])
-        vec[i] = v
-        xb[i] = (v * is_in(i)).astype(BF)
-        return 0
-
-    lax.fori_loop(1, ext - 1, n_first, 0, unroll=2)
-
-    def m_first(i, _):
-        s = tangent(i, vec[i])
-        cell_weight = field[i][channels : channels + 1]
-        y = cell_weight * gram_of(s)
-        hi[i, :padded] = s[:, :breadth].astype(BF)
-        y1[i] = y
-        pull(i, y)
-        return 0
-
-    lax.fori_loop(2, ext - 2, m_first, 0, unroll=2)
-
-    def keep_first(i, _):
+    def loop(first, last, size, body):
+        assert (last - first) % size == 0
+
+        def step(n, _):
+            body(first + n * size)
+            return 0
+
+        lax.fori_loop(0, (last - first) // size, step, 0)
+
+    def n_first(i):
+        for k, v in enumerate(spread(i, [field[i + k] for k in range(G[0])])):
+            vec[i + k] = v
+            xb[i + k] = (v * is_in(i + k)).astype(BF)
+
+    loop(1, ext - 1, G[0], n_first)
+
+    def m_first(i):
+        ss = tangent(i, [vec[i + k] for k in range(G[1])])
+        gs = gram_of(join(ss))
+        ys = []
+        for k, s in enumerate(ss):
+            y = field[i + k][channels : channels + 1] * part(gs, k)
+            hi[i + k, :padded] = s[:, :breadth].astype(BF)
+            y1[i + k] = y
+            ys.append(y)
+        pull(i, ys)
+
+    loop(2, ext - 2, G[1], m_first)
+
+    def keep_first(i):
         first_out[i] = vec[i + HALO][:, :breadth]
-        return 0
-
-    lax.fori_loop(0, height, keep_first, 0, unroll=2)
-
-    def n_second(i, _):
-        v = spread(i, y1[i])
-        vec[i] = v
-        xb[i] = (v * is_in(i)).astype(BF)
-        return 0
-
-    lax.fori_loop(3, ext - 3, n_second, 0, unroll=2)
+
+    loop(0, height, 1, keep_first)
+
+    def n_second(i):
+        for k, v in enumerate(spread(i, [y1[i + k] for k in range(G[2])])):
+            vec[i + k] = v
+            xb[i + k] = (v * is_in(i + k)).astype(BF)
+
+    loop(3, ext - 3, G[2], n_second)
+
+    def m_second(i):
+        vs = [vec[i + k] for k in range(G[3])]
+        for k, s in enumerate(tangent(i, vs)):
+            second_out[i + k - HALO] = vs[k][:, :breadth]
+            hi[i + k, padded:] = s[:, :breadth].astype(BF)
+
+    loop(HALO, ext - HALO, G[3], m_second)
 
     turn, lat_row, lon_row, _, _ = turned(got, channels, padded)
     slots = got.shape[0]
-    col_hot = (lax.broadcasted_iota(jnp.int32, (breadth, slots), 0) == lon_row).astype(BF)
-
-    def m_second(i, rows):
-        v = vec[i]
-        s = tangent(i, v)
-        second_out[i - HALO] = v[:, :breadth]
-        hi[i, padded:] = s[:, :breadth].astype(BF)
-        return rows + mxu(hi[i], col_hot) * (lat_row == i - HALO).astype(F32)
-
-    rows = lax.fori_loop(HALO, HALO + height, m_second, jnp.zeros((2 * padded, slots), F32))
-    row0, row1 = rows[:padded], rows[padded:]
+    piece = 256
+    for c in range(slots // piece):
+        here = slice(c * piece, (c + 1) * piece)
+        col_hot = (lax.broadcasted_iota(jnp.int32, (breadth, piece), 0) == lon_row[:, here]).astype(BF)
+        found[:, here] = jnp.zeros((2 * padded, piece), F32)
+
+        def gather(i, col_hot=col_hot, here=here):
+            out = mxu(hi[pl.ds(i, G[4])].reshape(G[4] * 2 * padded, breadth), col_hot)
+            total = found[:, here]
+            for k in range(G[4]):
+                mine = (lat_row[:, here] == i + k - HALO)
+                total = total + jnp.where(mine, out[k * 2 * padded : (k + 1) * 2 * padded], 0.0)
+            found[:, here] = total
+
+        loop(HALO, ext - HALO, G[4], gather)
+
+    row0, row1 = found[:padded], found[padded:]
     weight = turn[channels : channels + 1]
     curved0 = gram_of(row0) * weight
     curved1 = gram_of(row1) * weight
@@ -260,21 +327,16 @@
     lane = lax.broadcasted_iota(jnp.int32, (1, LANES), 1)
     pieces = jnp.zeros((1, LANES), F32)
     for number, value in enumerate(sums):
-        for part, piece in enumerate(split3(value)):
-            pieces = jnp.where(lane == channels + 3 + 3 * number + part, piece.astype(F32), pieces)
+        for third, piece in enumerate(split3(value)):
+            pieces = jnp.where(lane == channels + 3 + 3 * number + third, piece.astype(F32), pieces)
     filler = jnp.zeros((LANES - padded, slots), F32)
     turned0 = jnp.concatenate([row0, filler], axis=0).T
     turned1 = jnp.concatenate([row1, filler], axis=0).T
-    cap = reply_cap(slots, flags)
     leads = lax.broadcasted_iota(jnp.int32, (slots, LANES), 0)
-    is_lead = (leads - (leads // cap) * cap) == 0
+    is_lead = leads % cap == 0
     lanes = lax.broadcasted_iota(jnp.int32, (slots, LANES), 1)
     reply[:, :LANES] = jnp.where(lanes < channels, turned0, jnp.where(is_lead, pieces, 0.0)).astype(BF)
     reply[:, LANES:] = turned1.astype(BF)
-
-
-def reply_cap(slots, flags):
-    return flags[2]
 
 
 def scalars(reply, channels):
@@ -307,28 +369,11 @@
     increment[...] = a[None] * first[...] + b[None] * second[...]
 
 
-def neighbours(axis, by, periodic):
-    count = lax.axis_size(axis)
-    pairs = [(i, (i + by)) for i in range(count)]
-    return [(i, j % count) for i, j in pairs if periodic or 0 <= j < count]
-
-
 def shift2(x, by_lat, by_lon):
     n_lat, n_lon = lax.axis_size("lat"), lax.axis_size("lon")
     pairs = [(i * n_lon + j, (i + by_lat) * n_lon + (j + by_lon) % n_lon)
              for i in range(n_lat) for j in range(n_lon) if 0 <= i + by_lat < n_lat]
     return lax.ppermute(x, ("lat", "lon"), pairs)
-
-
-def wide_slope(slope):
-    x = jnp.transpose(slope, (1, 0, 2))
-    low = shift2(x[-HALO:], 1, 0)
-    high = shift2(x[:HALO], -1, 0)
-    x = jnp.concatenate([low, x, high], axis=0)
-    left = shift2(x[:, :, -HALO:], 0, 1)
-    right = shift2(x[:, :, :HALO], 0, -1)
-    gap = jnp.zeros(x.shape[:2] + (LANES - 2 * HALO,), x.dtype)
-    return jnp.concatenate([x, right, gap, left], axis=2)
 
 
 def on_device(departure_in, obs_owner, obs_cell, obs_count, qc_mask, channel_weight, jacobian,
@@ -373,42 +418,49 @@
     w_n = jnp.transpose(taps[::-1], (1, 3, 0, 2)).reshape(3 * padded, 3 * hidden)
     p_j = jnp.pad(projection, ((0, more), (0, 0)))
     p_t = p_j.T
-    slope_wide = wide_slope(slope)
-
-    edge = (HALO, padded, breadth)
-    north, south, west, east, nw, sw, ne, se = call(
+
+    slope_inner = jnp.transpose(slope, (1, 0, 2))
+    slope_north = shift2(slope_inner[-HALO:], 1, 0)
+    slope_south = shift2(slope_inner[:HALO], -1, 0)
+    slope_west, slope_east = call(strip_kernel, (shape((hidden, strip), BF),) * 2,
+                                  (slope_inner, slope_north, slope_south))
+
+    edge = (HALO + 1, padded, breadth)
+    north, south, west, east = call(
         functools.partial(edge_kernel, channels, height, breadth),
-        (shape(edge, BF),) * 2 + (shape((padded, strip), BF),) * 2 + (shape((padded, LANES), BF),) * 4,
+        (shape(edge, BF),) * 2 + (shape((padded, strip), BF),) * 2,
         (got,),
     )
     from_south = shift2(north, -1, 0)
     from_north = shift2(south, 1, 0)
-    from_east = shift2(west, 0, -1)
-    from_west = shift2(east, 0, 1)
-    from_se = shift2(nw, -1, -1)
-    from_ne = shift2(sw, 1, -1)
-    from_sw = shift2(ne, -1, 1)
-    from_nw = shift2(se, 1, 1)
+    to_west, to_east = call(
+        functools.partial(join_kernel, height),
+        (shape((padded + hidden, strip), BF),) * 2,
+        (west, east, from_north, from_south, slope_west, slope_east),
+    )
+    from_east = shift2(to_west, 0, -1)
+    from_west = shift2(to_east, 0, 1)
     inner = call(functools.partial(grid_kernel, channels), shape((height, padded, breadth)), (got,))
 
     at = lax.axis_index("lat")
-    flags = jnp.stack([at > 0, at < lax.axis_size("lat") - 1, cap]).astype(jnp.int32)
+    flags = jnp.stack([at > 0, at < lax.axis_size("lat") - 1]).astype(jnp.int32)
     first, second, reply = call(
-        functools.partial(main_kernel, channels, hidden),
+        functools.partial(main_kernel, channels, hidden, cap),
         (shape((height, padded, breadth)),) * 2 + (shape((slots, 2 * LANES), BF),),
-        (flags, got, inner, from_north, from_south, from_east, from_west, from_ne, from_se, from_nw,
-         from_sw, slope_wide, w_n, w_m, p_t, p_j, g3),
+        (flags, got, inner, from_north, from_south, from_east, from_west, slope_inner, slope_north,
+         slope_south, w_n, w_m, p_t, p_j, g3),
         scratch=[
             pltpu.VMEM((ext, padded, wide), F32),
-            pltpu.VMEM((strip // LANES, padded, LANES), F32),
+            pltpu.VMEM((ext, hidden, wide), BF),
             pltpu.VMEM((ext, hidden, wide), BF),
             pltpu.VMEM((ext, padded, wide), BF),
             pltpu.VMEM((ext, padded, wide), F32),
             pltpu.VMEM((ext, 2 * padded, breadth), BF),
             pltpu.VMEM((ext, padded, wide), F32),
+            pltpu.VMEM((2 * padded, slots), F32),
         ],
         smem=1,
-        vmem=116,
+        vmem=120,
     )
     back = swap(reply)
     first = jnp.transpose(first, (1, 0, 2))[:channels]

time: 202 us -> 116 us (0.57)
  Pallas kernels: 114 us -> 49.7 us
  starting transfers between devices: 40.7 us -> 26.2 us
  local copies, waits for them, and re-layouts: 35 us -> 27.6 us
  other arithmetic: 5.15 us -> 2.09 us
    pallas_call x5 -> x7, Pallas kernels: 114 us -> 49.7 us  [call(): pl.pallas_call(kernel, out_shape=outs, in_specs=[space(i) for i in range(...]
    ppermute x12 -> x6, starting transfers between devices: 26.1 us -> 12.2 us  [shift2(): return lax.ppermute(x, ('lat', 'lon'), pairs)]
    ppermute x2 -> x0, local copies, waits for them, and re-layouts: 4.34 us -> none  [shift2(): return lax.ppermute(x, ('lat', 'lon'), pairs)]
    slice x4 -> x1, local copies, waits for them, and re-layouts: 4.68 us -> 0.77 us  [on_device(): slope_south = shift2(slope_inner[:HALO], -1, 0)]
    concatenate x2 -> x0, other arithmetic: 3.86 us -> none  [the longest x1 3.63 us: wide_slope(): return jnp.concatenate([x, right, gap, left], axis=2)]
    ppermute x12 -> x6, waiting for transfers between devices: 3.95 us -> 5.7 us  [shift2(): return lax.ppermute(x, ('lat', 'lon'), pairs)]
    unnamed x43 -> x37, local copies, waits for them, and re-layouts: 9.89 us -> 8.54 us
  transfers between devices with their start and end apart: 14 -> 8, of which waited for: 2 -> 2; matrix products, arithmetic and copies ran while one was open for 16% -> 20% of each run, Pallas kernels for 2% -> 4%
where the time goes in v2:
time: 116 us; the launch traced here: 115 us
  Pallas kernels  49.7 us (43%)
  local copies, waits for them, and re-layouts  27.6 us (24%)
  starting transfers between devices  26.2 us (23%)
  waiting for transfers between devices  6.89 us (6%)
  other arithmetic  2.09 us (2%)
  between operations  1.59 us (1%)
    pallas_call x7, Pallas kernels, call(): pl.pallas_call(kernel, out_shape=outs, in_specs=[space(i) for i in range(...  49.7 us
    all_to_all x2, starting transfers between devices, swap(): lax.all_to_all(x.reshape(tiles, cap, -1), ('lat', 'lon'), split_axis=0, c...  14 us
    ppermute x6, starting transfers between devices, shift2(): return lax.ppermute(x, ('lat', 'lon'), pairs)  12.2 us
    unnamed x37, local copies, waits for them, and re-layouts  8.54 us
    transpose x1, local copies, waits for them, and re-layouts, on_device(): second = jnp.transpose(second, (1, 0, 2))[:channels]  7.87 us
    ppermute x6, waiting for transfers between devices, shift2(): return lax.ppermute(x, ('lat', 'lon'), pairs)  5.7 us
  transfers between devices with their start and end apart: 8, of which 2 were waited for; matrix products, arithmetic and copies ran while one was open for 20% of the time, Pallas kernels for 4%

profile of v2, /device:TPU:0, one launch (start us, length us, event | category | flops | bytes accessed | tf_op | source)
XLA Modules:
  0.0 115.0 jit_solution(6607989579929959958)
XLA Ops:
  0.6 0.0 copy-start.14
  0.6 0.0 copy-start.11
  0.7 0.0 copy-start.16
  0.7 0.0 copy-start.15
  1.4 0.8 copy.20.owner_col
  2.2 0.9 pad.12.jac
  3.1 1.0 copy-done.3
  4.1 0.7 copy-done.9
  4.8 0.7 copy-done.10
  5.5 0.7 copy-done.12
  6.2 0.7 copy-done.13
  6.9 1.9 %shard_map.113 = (bf16[768,128]{1,0:T(8,128)(2,1)}, s32[512,1]{1,0:T(8,128)S(1)}) custom-call(s32[1]{0:T(128)S(6)} %copy.35.count, f32[512,256]{1,0:T(8,128)S(1)} %copy-done.3, s32[1,512]{1,0:T(1,128)S(1)} %bitcast.34, s32[512,1]{1,0:T(8,128)S(1)} %copy.20.owner_col, s32[1,512]{1,0:T(1,128)S(1)} %bitcast.36, s32[1,512]{1,0:T(1,128)S(1)} %bitcast.37, ...), custom_call_target="tpu_custom_call" | custom-call | tf_op jit(solution)/shard_map/pallas_call | solution.py:29
  8.7 7.3 %all-to-all-start = ((bf16[32,24,128]{2,1,0:T(8,128)(2,1)}), bf16[32,24,128]{2,1,0:T(8,128)(2,1)S(1)}, u32[]{:S(2)}, u32[]{:S(2)}) async-start(bf16[32,24,128]{2,1,0:T(8,128)(2,1)} %bitcast.6), calls=%async_computation | async-start | bytes 393216 | tf_op jit(solution)/shard_map/all_to_all | solution.py:407
  16.0 1.9 %copy.33 = bf16[64,48,256]{2,0,1:T(8,128)(2,1)S(1)} copy(bf16[64,48,256]{2,1,0:T(8,128)(2,1)} %param.19) | data formatting | bytes 3145728 | tf_op args[9]
  18.0 0.0 copy-start
  18.0 0.8 fusion.4
  18.8 1.3 %collective-permute-start.3 = (bf16[4,64,256]{2,1,0:T(8,128)(2,1)}, bf16[4,64,256]{2,1,0:T(8,128)(2,1)S(1)}, u32[]{:S(2)}, u32[]{:S(2)}) collective-permute-start(bf16[4,64,256]{2,1,0:T(8,128)(2,1)} %get-tuple-element.30), channel_id=1, source_target_pairs={{4,0},{5,1},{6,2},{7,3},{8,4},{9,5},{10,6},{11,7},{12,8},{13,9},{1... | collective-permute-start | bytes 393224 | tf_op jit(solution)/shard_map/ppermute | solution.py:376
  20.0 4.6 %collective-permute-start.2 = (bf16[4,64,256]{2,1,0:T(8,128)(2,1)}, bf16[4,64,256]{2,1,0:T(8,128)(2,1)S(1)}, u32[]{:S(2)}, u32[]{:S(2)}) collective-permute-start(bf16[4,64,256]{2,1,0:T(8,128)(2,1)} %get-tuple-element.31), channel_id=1, source_target_pairs={{0,4},{1,5},{2,6},{3,7},{4,8},{5,9},{6,10},{7,11},{8,12},{9,13},{1... | collective-permute-start | bytes 393224 | tf_op jit(solution)/shard_map/ppermute | solution.py:376
  24.6 0.0 copy-done.16
  24.6 0.1 copy.24
  24.7 0.0 copy-done.14
  24.7 0.0 copy-done.11
  24.7 0.8 subtract_convert_fusion
  25.6 0.0 all-to-all-done
  25.6 1.8 %shard_map.115 = (bf16[5,80,256]{2,1,0:T(8,128)(2,1)S(1)}, bf16[5,80,256]{2,1,0:T(8,128)(2,1)S(1)}, bf16[80,512]{1,0:T(8,128)(2,1)S(1)}, bf16[80,512]{1,0:T(8,128)(2,1)S(1)}) custom-call(bf16[768,128]{1,0:T(8,128)(2,1)S(1)} %bitcast.30), custom_call_target="tpu_custom_call" | custom-call | tf_op jit(solution)/shard_map/pallas_call | solution.py:29
  27.4 4.6 %collective-permute-start = (bf16[5,80,256]{2,1,0:T(8,128)(2,1)S(1)}, bf16[5,80,256]{2,1,0:T(8,128)(2,1)S(1)}, u32[]{:S(2)}, u32[]{:S(2)}) collective-permute-start(bf16[5,80,256]{2,1,0:T(8,128)(2,1)S(1)} %get-tuple-element.16), channel_id=1, source_target_pairs={{0,4},{1,5},{2,6},{3,7},{4,8},{5,9},{6,10},{7,11},{8,12},{9,13},{1... | collective-permute-start | bytes 614408 | tf_op jit(solution)/shard_map/ppermute | solution.py:376
  31.9 1.3 %collective-permute-start.1 = (bf16[5,80,256]{2,1,0:T(8,128)(2,1)S(1)}, bf16[5,80,256]{2,1,0:T(8,128)(2,1)S(1)}, u32[]{:S(2)}, u32[]{:S(2)}) collective-permute-start(bf16[5,80,256]{2,1,0:T(8,128)(2,1)S(1)} %get-tuple-element.17), channel_id=1, source_target_pairs={{4,0},{5,1},{6,2},{7,3},{8,4},{9,5},{10,6},{11,7},{12,8},{13,9},{1... | collective-permute-start | bytes 614408 | tf_op jit(solution)/shard_map/ppermute | solution.py:376
  33.2 0.6 fusion.5
  33.9 0.0 copy-done.15
  33.9 0.1 copy.22
  34.0 0.1 reverse_bitcast_fusion
  34.1 0.0 collective-permute-done.3.south.slope_south
  34.1 0.0 copy-start.7
  34.1 0.0 collective-permute-done.2.north.slope_north
  34.1 0.0 copy-start.8
  34.2 0.5 shard_map.116
  34.7 5.7 %collective-permute-done.from_north.north = bf16[5,80,256]{2,1,0:T(8,128)(2,1)S(1)} collective-permute-done((bf16[5,80,256]{2,1,0:T(8,128)(2,1)S(1)}, bf16[5,80,256]{2,1,0:T(8,128)(2,1)S(1)}, u32[]{:S(2)}, u32[]{:S(2)}) %collective-permute-start) | collective-permute-done | bytes 204832 | tf_op jit(solution)/shard_map/ppermute | solution.py:376
  40.4 0.0 collective-permute-done.1.from_south.south
  40.4 0.1 collective-permute-start.4
  40.5 0.5 collective-permute-start.5
  41.0 0.6 add_convert_fusion.flags
  41.6 0.8 copy.34
  42.4 1.4 %copy.26.p_t = bf16[64,80]{1,0:T(8,128)(2,1)} copy(bf16[64,80]{0,1:T(8,128)(2,1)} %get-tuple-element.33) | data formatting | bytes 20480 | tf_op jit(solution)/shard_map/transpose | solution.py:420
  43.8 1.7 %reshape.34.w_m = bf16[192,240]{1,0:T(8,128)(2,1)} reshape(bf16[3,64,3,80]{3,2,1,0:T(4,128)(2,1)} %bitcast.40) | data formatting | bytes 184320 | tf_op jit(solution)/shard_map/reshape | solution.py:417
  45.5 0.1 reshape.33
  45.7 0.7 copy.25.w_n
  46.4 1.5 %pad_maximum_fusion.g3 = bf16[80,240]{1,0:T(8,128)(2,1)} fusion(bf16[80,80]{1,0:T(8,128)(2,1)} %get-tuple-element.29, bf16[80,80]{1,0:T(8,128)(2,1)} %get-tuple-element.28), kind=kLoop, calls=%fused_computation.7 | loop fusion | flops 115200 | bytes 64000 | tf_op jit(solution)/shard_map/concatenate | solution.py:415
  47.9 2.8 %shard_map.114.inner = f32[48,80,256]{2,1,0:T(8,128)S(1)} custom-call(bf16[768,128]{1,0:T(8,128)(2,1)S(1)} %bitcast.31), custom_call_target="tpu_custom_call" | custom-call | tf_op jit(solution)/shard_map/pallas_call | solution.py:29
  50.7 0.0 copy-done
  50.8 0.0 copy-done.2
  50.8 0.0 copy-done.7
  50.8 0.0 copy-done.8
  50.8 0.0 copy-start.1
  50.8 1.9 %copy-done.1 = f32[48,80,256]{2,1,0:T(8,128)} copy-done((f32[48,80,256]{2,1,0:T(8,128)}, f32[48,80,256]{2,1,0:T(8,128)S(1)}, u32[]{:S(2)}) %copy-start.1) | copy-done | bytes 3932184
  52.7 0.0 collective-permute-done.4.from_east
  52.7 0.0 collective-permute-done.5.from_west
  52.7 36.4 %shard_map.118 = (f32[48,80,256]{2,1,0:T(8,128)}, f32[48,80,256]{2,1,0:T(8,128)}, bf16[768,256]{1,0:T(8,128)(2,1)}) custom-call(s32[2]{0:T(128)} %add_convert_fusion.flags, bf16[768,128]{1,0:T(8,128)(2,1)} %bitcast.32, f32[48,80,256]{2,1,0:T(8,128)} %copy-done.1, bf16[5,80,256]{2,1,0:T(8,128)(2,1)} %copy-done.5, bf16[5,80,256]{2,1,0:T(8,128)(2,1)} %copy-done.6, ...), custom_call_target="tpu_custom_call" | custom-call | tf_op jit(solution)/shard_map/pallas_call | solution.py:29
  89.1 6.7 %all-to-all-start.1 = ((bf16[32,24,256]{2,1,0:T(8,128)(2,1)}), bf16[32,24,256]{2,1,0:T(8,128)(2,1)S(1)}, u32[]{:S(2)}, u32[]{:S(2)}) async-start(bf16[32,24,256]{2,1,0:T(8,128)(2,1)} %bitcast.41), calls=%async_computation.1 | async-start | bytes 786432 | tf_op jit(solution)/shard_map/all_to_all | solution.py:407
  95.8 7.9 %copy_bitcast_fusion = (f32[80,48,256]{2,1,0:T(8,128)S(1)}, f32[80,48,256]{2,1,0:T(8,128)S(1)}) fusion(f32[48,80,256]{2,1,0:T(8,128)} %get-tuple-element.27, f32[48,80,256]{2,1,0:T(8,128)} %get-tuple-element.26), kind=kLoop, calls=%fused_computation | loop fusion | bytes 15728640 | tf_op jit(solution)/shard_map/transpose | solution.py:467
  103.6 2.0 %slice.19.second = f32[69,48,256]{2,1,0:T(8,128)} slice(f32[80,48,256]{2,1,0:T(8,128)S(1)} %get-tuple-element.34), slice={[0:69], [0:48], [0:256]} | slice | bytes 6782976 | tf_op jit(solution)/shard_map/slice | solution.py:467
  105.6 1.9 %slice.18.first = f32[69,48,256]{2,1,0:T(8,128)} slice(f32[80,48,256]{2,1,0:T(8,128)S(1)} %get-tuple-element.35), slice={[0:69], [0:48], [0:256]} | slice | bytes 6782976 | tf_op jit(solution)/shard_map/slice | solution.py:466
  107.5 1.2 %all-to-all-done.1 = bf16[32,24,256]{2,1,0:T(8,128)(2,1)S(1)} async-done(((bf16[32,24,256]{2,1,0:T(8,128)(2,1)}), bf16[32,24,256]{2,1,0:T(8,128)(2,1)S(1)}, u32[]{:S(2)}, u32[]{:S(2)}) %all-to-all-start.1) | async-done | bytes 393248 | tf_op jit(solution)/shard_map/all_to_all | solution.py:407
  108.7 0.0 copy-done.4
  108.7 6.3 %shard_map.119 = (f32[69,48,256]{2,1,0:T(8,128)}, f32[512,256]{1,0:T(8,128)}) custom-call(bf16[768,256]{1,0:T(8,128)(2,1)S(1)} %bitcast.33, s32[512,1]{1,0:T(8,128)S(1)} %get-tuple-element.25.slot, f32[512,256]{1,0:T(8,128)S(1)} %copy-done.4, f32[80,256]{1,0:T(8,128)S(1)} %pad.12.jac, f32[69,48,256]{2,1,0:T(8,128)} %slice.18.first, f32[69,48,256]{2,1,0:T(8,128)} %slice.19.second), custom_call_target="tpu_custom_call" | custom-call | tf_op jit(solution)/shard_map/pallas_call | solution.py:29
  (13 shorter events, 0.1 us)
Async XLA Ops:
  0.6 24.1 %copy-start.14 = (f32[69,256]{1,0:T(8,128)S(1)}, f32[69,256]{1,0:T(8,128)}, u32[]{:S(2)}) copy-start(f32[69,256]{1,0:T(8,128)} %param.16) | copy-start | bytes 211972
  0.6 24.1 %copy-start.11 = (f32[256]{0:T(256)S(1)}, f32[256]{0:T(256)}, u32[]{:S(2)}) copy-start(f32[256]{0:T(256)} %param.15) | copy-start | bytes 3076
  0.7 24.0 %copy-start.16 = (bf16[69,64]{0,1:T(8,128)(2,1)S(1)}, bf16[69,64]{0,1:T(8,128)(2,1)}, u32[]{:S(2)}) copy-start(bf16[69,64]{0,1:T(8,128)(2,1)} %param.18) | copy-start | bytes 26500
  0.7 33.2 %copy-start.15 = (bf16[9,64,69]{2,1,0:T(8,128)(2,1)S(1)}, bf16[9,64,69]{2,1,0:T(8,128)(2,1)}, u32[]{:S(2)}) copy-start(bf16[9,64,69]{2,1,0:T(8,128)(2,1)} %param.17) | copy-start | bytes 238468
  3.1 1.0 copy-start.3
  4.1 0.7 copy-start.9
  4.8 0.7 copy-start.10
  5.5 0.7 copy-start.12
  6.2 0.7 copy-start.13
  8.7 16.8 %all-to-all-start = ((bf16[32,24,128]{2,1,0:T(8,128)(2,1)}), bf16[32,24,128]{2,1,0:T(8,128)(2,1)S(1)}, u32[]{:S(2)}, u32[]{:S(2)}) async-start(bf16[32,24,128]{2,1,0:T(8,128)(2,1)} %bitcast.6), calls=%async_computation | async-start | bytes 393216 | tf_op jit(solution)/shard_map/all_to_all | solution.py:407
  18.0 32.8 %copy-start = (bf16[64,48,256]{2,0,1:T(8,128)(2,1)}, bf16[64,48,256]{2,0,1:T(8,128)(2,1)S(1)}, u32[]{:S(2)}) copy-start(bf16[64,48,256]{2,0,1:T(8,128)(2,1)S(1)} %copy.33) | copy-start | bytes 4718596
  18.8 15.4 %collective-permute-start.3 = (bf16[4,64,256]{2,1,0:T(8,128)(2,1)}, bf16[4,64,256]{2,1,0:T(8,128)(2,1)S(1)}, u32[]{:S(2)}, u32[]{:S(2)}) collective-permute-start(bf16[4,64,256]{2,1,0:T(8,128)(2,1)} %get-tuple-element.30), channel_id=1, source_target_pairs={{4,0},{5,1},{6,2},{7,3},{8,4},{9,5},{10,6},{11,7},{12,8},{13,9},{1... | collective-permute-start | bytes 393224 | tf_op jit(solution)/shard_map/ppermute | solution.py:376
  20.0 14.1 %collective-permute-start.2 = (bf16[4,64,256]{2,1,0:T(8,128)(2,1)}, bf16[4,64,256]{2,1,0:T(8,128)(2,1)S(1)}, u32[]{:S(2)}, u32[]{:S(2)}) collective-permute-start(bf16[4,64,256]{2,1,0:T(8,128)(2,1)} %get-tuple-element.31), channel_id=1, source_target_pairs={{0,4},{1,5},{2,6},{3,7},{4,8},{5,9},{6,10},{7,11},{8,12},{9,13},{1... | collective-permute-start | bytes 393224 | tf_op jit(solution)/shard_map/ppermute | solution.py:376
  25.6 25.2 %copy-start.2 = (bf16[32,24,128]{2,1,0:T(8,128)(2,1)}, bf16[32,24,128]{2,1,0:T(8,128)(2,1)S(1)}, u32[]{:S(2)}) copy-start(bf16[32,24,128]{2,1,0:T(8,128)(2,1)S(1)} %all-to-all-done) | copy-start | bytes 589828
  27.4 13.0 %collective-permute-start = (bf16[5,80,256]{2,1,0:T(8,128)(2,1)S(1)}, bf16[5,80,256]{2,1,0:T(8,128)(2,1)S(1)}, u32[]{:S(2)}, u32[]{:S(2)}) collective-permute-start(bf16[5,80,256]{2,1,0:T(8,128)(2,1)S(1)} %get-tuple-element.16), channel_id=1, source_target_pairs={{0,4},{1,5},{2,6},{3,7},{4,8},{5,9},{6,10},{7,11},{8,12},{9,13},{1... | collective-permute-start | bytes 614408 | tf_op jit(solution)/shard_map/ppermute | solution.py:376
  31.9 8.5 %collective-permute-start.1 = (bf16[5,80,256]{2,1,0:T(8,128)(2,1)S(1)}, bf16[5,80,256]{2,1,0:T(8,128)(2,1)S(1)}, u32[]{:S(2)}, u32[]{:S(2)}) collective-permute-start(bf16[5,80,256]{2,1,0:T(8,128)(2,1)S(1)} %get-tuple-element.17), channel_id=1, source_target_pairs={{4,0},{5,1},{6,2},{7,3},{8,4},{9,5},{10,6},{11,7},{12,8},{13,9},{1... | collective-permute-start | bytes 614408 | tf_op jit(solution)/shard_map/ppermute | solution.py:376
  34.1 16.6 %copy-start.7 = (bf16[4,64,256]{2,1,0:T(8,128)(2,1)}, bf16[4,64,256]{2,1,0:T(8,128)(2,1)S(1)}, u32[]{:S(2)}) copy-start(bf16[4,64,256]{2,1,0:T(8,128)(2,1)S(1)} %collective-permute-done.3.south.slope_south) | copy-start | bytes 393220
  34.1 16.6 %copy-start.8 = (bf16[4,64,256]{2,1,0:T(8,128)(2,1)}, bf16[4,64,256]{2,1,0:T(8,128)(2,1)S(1)}, u32[]{:S(2)}) copy-start(bf16[4,64,256]{2,1,0:T(8,128)(2,1)S(1)} %collective-permute-done.2.north.slope_north) | copy-start | bytes 393220
  40.4 12.3 %copy-start.5 = (bf16[5,80,256]{2,1,0:T(8,128)(2,1)}, bf16[5,80,256]{2,1,0:T(8,128)(2,1)S(1)}, u32[]{:S(2)}) copy-start(bf16[5,80,256]{2,1,0:T(8,128)(2,1)S(1)} %collective-permute-done.from_north.north) | copy-start | bytes 614404
  40.4 12.3 %copy-start.6 = (bf16[5,80,256]{2,1,0:T(8,128)(2,1)}, bf16[5,80,256]{2,1,0:T(8,128)(2,1)S(1)}, u32[]{:S(2)}) copy-start(bf16[5,80,256]{2,1,0:T(8,128)(2,1)S(1)} %collective-permute-done.1.from_south.south) | copy-start | bytes 614404
  40.4 12.2 %collective-permute-start.4 = (bf16[144,512]{1,0:T(8,128)(2,1)S(1)}, bf16[144,512]{1,0:T(8,128)(2,1)}, u32[]{:S(2)}, u32[]{:S(2)}) collective-permute-start(bf16[144,512]{1,0:T(8,128)(2,1)S(1)} %get-tuple-element.22), channel_id=1, source_target_pairs={{0,3},{1,0},{2,1},{3,2},{4,7},{5,4},{6,5},{7,6},{8,11},{9,8},{10,9... | collective-permute-start | bytes 442376 | tf_op jit(solution)/shard_map/ppermute | solution.py:376
  40.5 12.2 %collective-permute-start.5 = (bf16[144,512]{1,0:T(8,128)(2,1)S(1)}, bf16[144,512]{1,0:T(8,128)(2,1)}, u32[]{:S(2)}, u32[]{:S(2)}) collective-permute-start(bf16[144,512]{1,0:T(8,128)(2,1)S(1)} %get-tuple-element.23), channel_id=1, source_target_pairs={{0,1},{1,2},{2,3},{3,0},{4,5},{5,6},{6,7},{7,4},{8,9},{9,10},{10,1... | collective-permute-start | bytes 442376 | tf_op jit(solution)/shard_map/ppermute | solution.py:376
  50.8 1.9 %copy-start.1 = (f32[48,80,256]{2,1,0:T(8,128)}, f32[48,80,256]{2,1,0:T(8,128)S(1)}, u32[]{:S(2)}) copy-start(f32[48,80,256]{2,1,0:T(8,128)S(1)} %shard_map.114.inner) | copy-start | bytes 11796484
  89.1 19.7 %all-to-all-start.1 = ((bf16[32,24,256]{2,1,0:T(8,128)(2,1)}), bf16[32,24,256]{2,1,0:T(8,128)(2,1)S(1)}, u32[]{:S(2)}, u32[]{:S(2)}) async-start(bf16[32,24,256]{2,1,0:T(8,128)(2,1)} %bitcast.41), calls=%async_computation.1 | async-start | bytes 786432 | tf_op jit(solution)/shard_map/all_to_all | solution.py:407
  105.6 3.1 %copy-start.4 = (f32[512,256]{1,0:T(8,128)S(1)}, f32[512,256]{1,0:T(8,128)}, u32[]{:S(2)}) copy-start(f32[512,256]{1,0:T(8,128)} %dep.3) | copy-start | bytes 1572868

commit v3 on v2

--- a/solution.py
+++ b/solution.py
@@ -22,15 +22,24 @@
     return lax.dot_general(a, b, (dims, ((), ())), precision=precision, preferred_element_type=F32)
 
 
-def call(kernel, outs, args, scratch=(), smem=0, vmem=100):
-    def space(i):
-        return pl.BlockSpec(memory_space=pltpu.SMEM if i < smem else pltpu.VMEM)
-
+def call(kernel, outs, args, scratch=(), smem=0, vmem=24, unread=0, staged=False, away=()):
+    def space(i, x):
+        if i < smem:
+            return pl.BlockSpec(memory_space=pltpu.SMEM)
+        if i >= len(args) - unread:
+            return pl.BlockSpec(memory_space=pl.ANY)
+        if staged:
+            return pl.BlockSpec(x.shape, lambda _: (0,) * x.ndim)
+        return pl.BlockSpec(memory_space=pltpu.VMEM)
+
+    leaves, tree = jax.tree.flatten(outs)
+    out_specs = [pl.BlockSpec(memory_space=pl.ANY if i in away else pltpu.VMEM) for i in range(len(leaves))]
     return pl.pallas_call(
         kernel,
         out_shape=outs,
-        in_specs=[space(i) for i in range(len(args))],
-        out_specs=jax.tree.map(lambda _: pl.BlockSpec(memory_space=pltpu.VMEM), outs),
+        grid=(1,) if staged else (),
+        in_specs=[space(i, x) for i, x in enumerate(args)],
+        out_specs=jax.tree.unflatten(tree, out_specs),
         scratch_shapes=scratch,
         interpret=INTERPRET,
         compiler_params=pltpu.CompilerParams(vmem_limit_bytes=vmem * 2**20 // 2),
@@ -44,7 +53,7 @@
     return hi, mid, (rest - mid.astype(F32)).astype(BF)
 
 
-def pack_kernel(tiles, cap, lon_size, channels, count, dep, owner_row, owner_col, cell_row, qc_row,
+def pack_kernel(tiles, cap, lon_size, channels, count, dep, owner_row, cell_row, qc_row,
                 weight, jac, send, slot_out):
     rows = dep.shape[0]
     slots = send.shape[0]
@@ -54,13 +63,8 @@
     earlier = mxu(hit, before)
     rank = jnp.sum(earlier * hit.astype(F32), axis=0, keepdims=True)
     slot = owner_row[...] * cap + rank.astype(jnp.int32)
+    slot_out[...] = slot
     place = (lax.broadcasted_iota(jnp.int32, (slots, rows), 0) == slot).astype(BF)
-
-    hit_c = (lax.broadcasted_iota(jnp.int32, (rows, tiles), 1) == owner_col[...]).astype(BF)
-    before_c = (lax.broadcasted_iota(jnp.int32, (rows, rows), 1)
-                < lax.broadcasted_iota(jnp.int32, (rows, rows), 0)).astype(BF)
-    rank_c = jnp.sum(mxu(before_c, hit_c) * hit_c.astype(F32), axis=1, keepdims=True)
-    slot_out[...] = owner_col[...] * cap + rank_c.astype(jnp.int32)
 
     used = (lax.broadcasted_iota(jnp.int32, (1, rows), 1) < count[0]).astype(F32)
     row_weight = used * qc_row[...].astype(F32)
@@ -68,11 +72,41 @@
     lat = cell_row[...] // lon_size
     lon = cell_row[...] - lat * lon_size
     wide = lax.broadcasted_iota(jnp.int32, (LANES, rows), 0)
-    terms = jnp.concatenate([terms, jnp.zeros((LANES - terms.shape[0], rows), F32)], axis=0)
+    terms = jnp.concatenate([terms, jnp.zeros((LANES - channels, rows), F32)], axis=0)
     terms = jnp.where(wide == channels, row_weight, terms)
     terms = jnp.where(wide == channels + 1, lat.astype(F32), terms)
     terms = jnp.where(wide == channels + 2, lon.astype(F32), terms)
     send[...] = mxu(place, terms.astype(BF), ((1,), (1,))).astype(BF)
+
+
+def weights_kernel(taps, projection, jac, weight, w_m, w_n, p_t, p_j, g3):
+    _, hidden, channels = taps.shape
+    padded = p_j.shape[0]
+
+    def shifted(rows, columns, by):
+        return (lax.broadcasted_iota(jnp.int32, (rows, columns), 0) + by
+                == lax.broadcasted_iota(jnp.int32, (rows, columns), 1)).astype(BF)
+
+    wider = shifted(channels, padded, 0)
+    for b in range(3):
+        total_m, total_n = 0.0, 0.0
+        for a in range(3):
+            tap = taps[3 * a + b]
+            total_m = total_m + mxu(tap, shifted(channels, 3 * padded, a * padded))
+            turned_tap = mxu(wider, tap, ((0,), (1,))).astype(BF)
+            total_n = total_n + mxu(turned_tap, shifted(hidden, 3 * hidden, (2 - a) * hidden))
+        w_m[b * hidden : (b + 1) * hidden] = total_m.astype(BF)
+        w_n[b * padded : (b + 1) * padded] = total_n.astype(BF)
+    p_j[...] = mxu(wider, projection[...], ((0,), (0,))).astype(BF)
+    p_t[...] = mxu(projection[...], wider, ((0,), (0,))).astype(BF)
+    tall = jnp.concatenate([jac[...], jnp.zeros((padded - channels, jac.shape[1]), F32)], axis=0)
+    gram = mxu(tall * weight[...], tall, ((1,), (1,)), lax.Precision.HIGHEST)
+    hi = gram.astype(BF)
+    lo = (gram - hi.astype(F32)).astype(BF)
+    total = 0.0
+    for k, value in enumerate((hi, lo, hi)):
+        total = total + mxu(value, shifted(padded, 3 * padded, k * padded))
+    g3[...] = total.astype(BF)
 
 
 def turned(got, channels, padded):
@@ -155,7 +189,8 @@
         east[:, block * LANES : (block + 1) * LANES] = right.astype(BF)
 
 
-def join_kernel(height, west, east, from_north, from_south, slope_west, slope_east, to_west, to_east):
+def join_kernel(height, west, east, from_north, from_south, slope_west, slope_east, _inner, _weights,
+                to_west, to_east):
     padded, strip = west.shape
     last = (height + HALO) * SIDE // LANES
     for k, own, slope, out in ((0, west, slope_west, to_west), (1, east, slope_east, to_east)):
@@ -173,7 +208,7 @@
 
 def main_kernel(channels, hidden, cap, flags, got, inner, north, south, from_east, from_west, slope_inner,
                 slope_north, slope_south, w_n, w_m, p_t, p_j, g3, first_out, second_out, reply,
-                field, slope, ga, xb, vec, hi, y1, found):
+                field, slope, ga, xb, vec, hi, found):
     height, padded, breadth = inner.shape
     wide = breadth + LANES
     ext = height + 2 * HALO
@@ -269,7 +304,7 @@
         for k, s in enumerate(ss):
             y = field[i + k][channels : channels + 1] * part(gs, k)
             hi[i + k, :padded] = s[:, :breadth].astype(BF)
-            y1[i + k] = y
+            field[i + k] = y
             ys.append(y)
         pull(i, ys)
 
@@ -281,7 +316,7 @@
     loop(0, height, 1, keep_first)
 
     def n_second(i):
-        for k, v in enumerate(spread(i, [y1[i + k] for k in range(G[2])])):
+        for k, v in enumerate(spread(i, [field[i + k] for k in range(G[2])])):
             vec[i + k] = v
             xb[i + k] = (v * is_in(i + k)).astype(BF)
 
@@ -357,16 +392,25 @@
     return step0 + step1 * c0, step1 * c1
 
 
-def final_kernel(channels, back, slot, dep, jac, first, second, increment, departures):
+def final_kernel(channels, back, slot, dep, jac, first, second, increment, departures, mixed, sems):
     slots = back.shape[0]
     rows = dep.shape[0]
+    height = mixed.shape[0]
     a, b = scalars(back, channels)
-    place = (lax.broadcasted_iota(jnp.int32, (rows, slots), 1) == slot[...]).astype(BF)
-    own = mxu(place, back[...])
-    padded = jac.shape[0]
-    state = a * own[:, :padded] + b * own[:, LANES : LANES + padded]
+
+    def copy(i):
+        return pltpu.make_async_copy(mixed.at[i], increment.at[:, i], sems.at[i])
+
+    for i in range(height):
+        mixed[i] = a * first[i, :channels] + b * second[i, :channels]
+        copy(i).start()
+    slots_of = lax.broadcasted_iota(jnp.int32, (slots, rows), 0)
+    place = (slots_of == slot[...]).astype(BF)
+    own = mxu(place, back[...], ((0,), (0,)))
+    state = a * own[:, :channels] + b * own[:, LANES : LANES + channels]
     departures[...] = dep[...] - mxu(state, jac[...], precision=lax.Precision.HIGHEST)
-    increment[...] = a[None] * first[...] + b[None] * second[...]
+    for i in range(height):
+        copy(i).wait()
 
 
 def shift2(x, by_lat, by_lon):
@@ -388,19 +432,18 @@
     wide = breadth + LANES
     ext = height + 2 * HALO
     strip = -(-(ext * SIDE) // LANES) * LANES
-    more = padded - channels
 
     def shape(dims, kind=F32):
         return jax.ShapeDtypeStruct(dims, kind)
 
-    jac = jnp.pad(jacobian, ((0, more), (0, 0)))
     weight = channel_weight[None, :]
     send, slot = call(
         functools.partial(pack_kernel, tiles, cap, breadth, channels),
-        (shape((slots, LANES), BF), shape((rows, 1), jnp.int32)),
-        (obs_count, departure_in, obs_owner.reshape(1, rows), obs_owner, obs_cell[None, :],
-         qc_mask[None, :], weight, jac),
+        (shape((slots, LANES), BF), shape((1, rows), jnp.int32)),
+        (obs_count, departure_in, obs_owner.reshape(1, rows), obs_cell[None, :],
+         qc_mask[None, :], weight, jacobian),
         smem=1,
+        staged=True,
     )
 
     def swap(x):
@@ -409,15 +452,13 @@
 
     got = swap(send)
 
-    gram = jnp.dot(jac * weight, jac.T, precision=lax.Precision.HIGHEST)
-    gram_hi = gram.astype(BF)
-    gram_lo = (gram - gram_hi.astype(F32)).astype(BF)
-    g3 = jnp.concatenate([gram_hi, gram_lo, gram_hi], axis=1)
-    taps = jnp.pad(conv_taps, ((0, 0), (0, 0), (0, more))).reshape(3, 3, hidden, padded)
-    w_m = jnp.transpose(taps, (1, 2, 0, 3)).reshape(3 * hidden, 3 * padded)
-    w_n = jnp.transpose(taps[::-1], (1, 3, 0, 2)).reshape(3 * padded, 3 * hidden)
-    p_j = jnp.pad(projection, ((0, more), (0, 0)))
-    p_t = p_j.T
+    w_m, w_n, p_t, p_j, g3 = call(
+        weights_kernel,
+        (shape((3 * hidden, 3 * padded), BF), shape((3 * padded, 3 * hidden), BF), shape((hidden, padded), BF),
+         shape((padded, hidden), BF), shape((padded, 3 * padded), BF)),
+        (conv_taps, projection, jacobian, weight),
+        staged=True,
+    )
 
     slope_inner = jnp.transpose(slope, (1, 0, 2))
     slope_north = shift2(slope_inner[-HALO:], 1, 0)
@@ -433,14 +474,15 @@
     )
     from_south = shift2(north, -1, 0)
     from_north = shift2(south, 1, 0)
+    inner = call(functools.partial(grid_kernel, channels), shape((height, padded, breadth)), (got,))
     to_west, to_east = call(
         functools.partial(join_kernel, height),
         (shape((padded + hidden, strip), BF),) * 2,
-        (west, east, from_north, from_south, slope_west, slope_east),
+        (west, east, from_north, from_south, slope_west, slope_east, inner, w_m),
+        unread=2,
     )
     from_east = shift2(to_west, 0, -1)
     from_west = shift2(to_east, 0, 1)
-    inner = call(functools.partial(grid_kernel, channels), shape((height, padded, breadth)), (got,))
 
     at = lax.axis_index("lat")
     flags = jnp.stack([at > 0, at < lax.axis_size("lat") - 1]).astype(jnp.int32)
@@ -456,19 +498,19 @@
             pltpu.VMEM((ext, padded, wide), BF),
             pltpu.VMEM((ext, padded, wide), F32),
             pltpu.VMEM((ext, 2 * padded, breadth), BF),
-            pltpu.VMEM((ext, padded, wide), F32),
             pltpu.VMEM((2 * padded, slots), F32),
         ],
         smem=1,
-        vmem=120,
+        vmem=64,
     )
     back = swap(reply)
-    first = jnp.transpose(first, (1, 0, 2))[:channels]
-    second = jnp.transpose(second, (1, 0, 2))[:channels]
     return call(
         functools.partial(final_kernel, channels),
         (shape((channels, height, breadth)), shape((rows, radiances))),
-        (back, slot, departure_in, jac, first, second),
+        (back, slot, departure_in, jacobian, first, second),
+        scratch=[pltpu.VMEM((height, channels, breadth), F32), pltpu.SemaphoreType.DMA((height,))],
+        away=(0,),
+        vmem=32,
     )
 
 

time: 116 us -> 113 us (0.974)
  blocking collectives: 0 us -> 18.4 us
  local copies, waits for them, and re-layouts: 27.6 us -> 11.4 us
  waiting for transfers between devices: 6.89 us -> 17.2 us
  starting transfers between devices: 26.2 us -> 18.4 us
  Pallas kernels: 49.7 us -> 45.3 us
  other arithmetic: 2.09 us -> 0.07 us
    all_to_all x0 -> x1, blocking collectives: none -> 18.4 us  [swap(): lax.all_to_all(x.reshape(tiles, cap, -1), ('lat', 'lon'), split_axis=0, c...]
    transpose x3 -> x0, local copies, waits for them, and re-layouts: 9.35 us -> none  [the longest x1 7.87 us: on_device(): second = jnp.transpose(second, (1, 0, 2))[:channels]]
    all_to_all x2 -> x1, starting transfers between devices: 14 us -> 7.3 us  [swap(): lax.all_to_all(x.reshape(tiles, cap, -1), ('lat', 'lon'), split_axis=0, c...]
    all_to_all x2 -> x1, waiting for transfers between devices: 1.19 us -> 6.95 us  [swap(): lax.all_to_all(x.reshape(tiles, cap, -1), ('lat', 'lon'), split_axis=0, c...]
    ppermute x6, waiting for transfers between devices: 5.7 us -> 10.3 us  [shift2(): return lax.ppermute(x, ('lat', 'lon'), pairs)]
    pallas_call x7 -> x8, Pallas kernels: 49.7 us -> 45.3 us  [call(): pl.pallas_call(kernel, out_shape=outs, grid=(1,) if staged else (), in_sp...]
    slice x2 -> x0, local copies, waits for them, and re-layouts: 3.9 us -> none  [the longest x1 1.98 us: on_device(): second = jnp.transpose(second, (1, 0, 2))[:channels]]
    reshape x5 -> x0, local copies, waits for them, and re-layouts: 3.52 us -> none  [the longest x1 1.71 us: on_device(): w_m = jnp.transpose(taps, (1, 2, 0, 3)).reshape(3 * hidden, 3 * padded)]
  transfers between devices with their start and end apart: 8 -> 7, of which waited for: 2 -> 5; matrix products, arithmetic and copies ran while one was open for 20% -> 2% of each run, Pallas kernels for 4% -> 4%
where the time goes in v3:
time: 113 us; the launch traced here: 112 us
  Pallas kernels  45.3 us (40%)
  starting transfers between devices  18.4 us (16%)
  blocking collectives  18.4 us (16%)
  waiting for transfers between devices  17.2 us (15%)
  local copies, waits for them, and re-layouts  11.4 us (10%)
  between operations  1.62 us (1%)
    pallas_call x8, Pallas kernels, call(): pl.pallas_call(kernel, out_shape=outs, grid=(1,) if staged else (), in_sp...  45.3 us
    all_to_all x1, blocking collectives, swap(): lax.all_to_all(x.reshape(tiles, cap, -1), ('lat', 'lon'), split_axis=0, c...  18.4 us
    ppermute x6, starting transfers between devices, shift2(): return lax.ppermute(x, ('lat', 'lon'), pairs)  11.1 us
    unnamed x28, local copies, waits for them, and re-layouts  10.7 us
    ppermute x6, waiting for transfers between devices, shift2(): return lax.ppermute(x, ('lat', 'lon'), pairs)  10.3 us
    all_to_all x1, starting transfers between devices, swap(): lax.all_to_all(x.reshape(tiles, cap, -1), ('lat', 'lon'), split_axis=0, c...  7.3 us
    all_to_all x1, waiting for transfers between devices, swap(): lax.all_to_all(x.reshape(tiles, cap, -1), ('lat', 'lon'), split_axis=0, c...  6.95 us
  transfers between devices with their start and end apart: 7, of which 5 were waited for; matrix products, arithmetic and copies ran while one was open for 2% of the time, Pallas kernels for 4%

profile of v3, /device:TPU:0, one launch (start us, length us, event | category | flops | bytes accessed | tf_op | source)
XLA Modules:
  0.0 112.4 jit_solution(842393398439052422)
XLA Ops:
  0.6 0.0 copy-start.8
  1.3 0.0 copy-start.2
  1.3 1.0 copy-done.2
  2.3 0.0 copy-start.4
  2.3 0.9 copy-done.4
  3.2 0.0 copy-start.7
  3.2 0.7 copy-done.7
  3.9 0.0 copy-start.9
  3.9 0.7 copy-done.9
  4.6 0.0 copy-start.10
  4.6 0.7 copy-done.10
  5.3 0.0 copy-start.11
  5.3 0.7 copy-done.11
  6.0 0.0 copy-start.12
  6.0 0.0 copy-start.5
  6.0 0.0 copy-start.6
  6.0 1.6 %shard_map.113 = (bf16[768,128]{1,0:T(8,128)(2,1)}, s32[1,512]{1,0:T(1,128)S(1)}) custom-call(s32[1]{0:T(128)S(6)} %copy.16.count, f32[512,256]{1,0:T(8,128)S(1)} %copy-done.2, s32[1,512]{1,0:T(1,128)S(1)} %bitcast.23, s32[1,512]{1,0:T(1,128)S(1)} %bitcast.24, s32[1,512]{1,0:T(1,128)S(1)} %bitcast.25, f32[1,256]{1,0:T(1,128)S(1)} %bitcast.21, ...), custom_call_target="tpu_custom_call" | custom-call | tf_op jit(solution)/shard_map/pallas_call | solution.py:37
  7.6 7.3 %all-to-all-start = ((bf16[32,24,128]{2,1,0:T(8,128)(2,1)}), bf16[32,24,128]{2,1,0:T(8,128)(2,1)S(1)}, u32[]{:S(2)}, u32[]{:S(2)}) async-start(bf16[32,24,128]{2,1,0:T(8,128)(2,1)} %bitcast.6), calls=%async_computation | async-start | bytes 393216 | tf_op jit(solution)/shard_map/all_to_all | solution.py:450
  14.9 1.9 %copy.15 = bf16[64,48,256]{2,0,1:T(8,128)(2,1)S(1)} copy(bf16[64,48,256]{2,1,0:T(8,128)(2,1)} %param.19) | data formatting | bytes 3145728 | tf_op args[9]
  16.9 6.9 %all-to-all-done = bf16[32,24,128]{2,1,0:T(8,128)(2,1)S(1)} async-done(((bf16[32,24,128]{2,1,0:T(8,128)(2,1)}), bf16[32,24,128]{2,1,0:T(8,128)(2,1)S(1)}, u32[]{:S(2)}, u32[]{:S(2)}) %all-to-all-start) | async-done | bytes 196640 | tf_op jit(solution)/shard_map/all_to_all | solution.py:450
  23.8 2.5 %shard_map.115 = (bf16[5,80,256]{2,1,0:T(8,128)(2,1)S(1)}, bf16[5,80,256]{2,1,0:T(8,128)(2,1)}, bf16[80,512]{1,0:T(8,128)(2,1)S(1)}, bf16[80,512]{1,0:T(8,128)(2,1)S(1)}) custom-call(bf16[768,128]{1,0:T(8,128)(2,1)S(1)} %bitcast.16), custom_call_target="tpu_custom_call" | custom-call | tf_op jit(solution)/shard_map/pallas_call | solution.py:37
  26.3 2.8 %collective-permute-start = (bf16[5,80,256]{2,1,0:T(8,128)(2,1)}, bf16[5,80,256]{2,1,0:T(8,128)(2,1)S(1)}, u32[]{:S(2)}, u32[]{:S(2)}) collective-permute-start(bf16[5,80,256]{2,1,0:T(8,128)(2,1)} %get-tuple-element.21), channel_id=1, source_target_pairs={{0,4},{1,5},{2,6},{3,7},{4,8},{5,9},{6,10},{7,11},{8,12},{9,13},{1... | collective-permute-start | bytes 614408 | tf_op jit(solution)/shard_map/ppermute | solution.py:420
  29.1 1.3 %collective-permute-start.1 = (bf16[5,80,256]{2,1,0:T(8,128)(2,1)S(1)}, bf16[5,80,256]{2,1,0:T(8,128)(2,1)S(1)}, u32[]{:S(2)}, u32[]{:S(2)}) collective-permute-start(bf16[5,80,256]{2,1,0:T(8,128)(2,1)S(1)} %get-tuple-element.22), channel_id=1, source_target_pairs={{4,0},{5,1},{6,2},{7,3},{8,4},{9,5},{10,6},{11,7},{12,8},{13,9},{1... | collective-permute-start | bytes 614408 | tf_op jit(solution)/shard_map/ppermute | solution.py:420
  30.4 0.7 fusion
  31.1 1.3 %collective-permute-start.3 = (bf16[4,64,256]{2,1,0:T(8,128)(2,1)}, bf16[4,64,256]{2,1,0:T(8,128)(2,1)S(1)}, u32[]{:S(2)}, u32[]{:S(2)}) collective-permute-start(bf16[4,64,256]{2,1,0:T(8,128)(2,1)} %get-tuple-element.38), channel_id=1, source_target_pairs={{4,0},{5,1},{6,2},{7,3},{8,4},{9,5},{10,6},{11,7},{12,8},{13,9},{1... | collective-permute-start | bytes 393224 | tf_op jit(solution)/shard_map/ppermute | solution.py:420
  32.4 5.2 %collective-permute-start.2 = (bf16[4,64,256]{2,1,0:T(8,128)(2,1)S(1)}, bf16[4,64,256]{2,1,0:T(8,128)(2,1)S(1)}, u32[]{:S(2)}, u32[]{:S(2)}) collective-permute-start(bf16[4,64,256]{2,1,0:T(8,128)(2,1)S(1)} %get-tuple-element.39), channel_id=1, source_target_pairs={{0,4},{1,5},{2,6},{3,7},{4,8},{5,9},{6,10},{7,11},{8,12},{9,13},{1... | collective-permute-start | bytes 393224 | tf_op jit(solution)/shard_map/ppermute | solution.py:420
  37.6 0.0 copy-done.12
  37.6 0.1 copy.13.projection
  37.7 0.0 copy-done.8
  37.7 0.0 copy-done.5
  37.7 0.0 copy-done.6
  37.7 0.9 shard_map.117
  38.6 1.6 %collective-permute-done.3.south.slope_south = bf16[4,64,256]{2,1,0:T(8,128)(2,1)S(1)} collective-permute-done((bf16[4,64,256]{2,1,0:T(8,128)(2,1)}, bf16[4,64,256]{2,1,0:T(8,128)(2,1)S(1)}, u32[]{:S(2)}, u32[]{:S(2)}) %collective-permute-start.3) | collective-permute-done | bytes 131104 | tf_op jit(solution)/shard_map/ppermute | solution.py:420
  40.2 3.3 %collective-permute-done.2.north.slope_north = bf16[4,64,256]{2,1,0:T(8,128)(2,1)S(1)} collective-permute-done((bf16[4,64,256]{2,1,0:T(8,128)(2,1)S(1)}, bf16[4,64,256]{2,1,0:T(8,128)(2,1)S(1)}, u32[]{:S(2)}, u32[]{:S(2)}) %collective-permute-start.2) | collective-permute-done | bytes 131104 | tf_op jit(solution)/shard_map/ppermute | solution.py:420
  43.5 0.6 shard_map.116
  44.0 2.8 %shard_map.114._inner.inner = f32[48,80,256]{2,1,0:T(8,128)S(1)} custom-call(bf16[768,128]{1,0:T(8,128)(2,1)S(1)} %bitcast.17), custom_call_target="tpu_custom_call" | custom-call | tf_op jit(solution)/shard_map/pallas_call | solution.py:37
  46.9 0.0 collective-permute-done.from_north.north
  46.9 0.0 collective-permute-done.1.from_south.south
  46.9 0.0 copy-start
  46.9 1.9 %copy-done = f32[48,80,256]{2,1,0:T(8,128)} copy-done((f32[48,80,256]{2,1,0:T(8,128)}, f32[48,80,256]{2,1,0:T(8,128)S(1)}, u32[]{:S(2)}) %copy-start) | copy-done | bytes 3932184
  48.8 0.5 collective-permute-start.4
  49.3 0.0 collective-permute-start.5
  49.3 0.1 add_convert_fusion.flags
  49.4 3.8 %collective-permute-done.4.from_east = bf16[144,512]{1,0:T(8,128)(2,1)S(1)} collective-permute-done((bf16[144,512]{1,0:T(8,128)(2,1)S(1)}, bf16[144,512]{1,0:T(8,128)(2,1)S(1)}, u32[]{:S(2)}, u32[]{:S(2)}) %collective-permute-start.4) | collective-permute-done | bytes 147488 | tf_op jit(solution)/shard_map/ppermute | solution.py:420
  53.2 1.6 %collective-permute-done.5.from_west = bf16[144,512]{1,0:T(8,128)(2,1)S(1)} collective-permute-done((bf16[144,512]{1,0:T(8,128)(2,1)S(1)}, bf16[144,512]{1,0:T(8,128)(2,1)S(1)}, u32[]{:S(2)}, u32[]{:S(2)}) %collective-permute-start.5) | collective-permute-done | bytes 147488 | tf_op jit(solution)/shard_map/ppermute | solution.py:420
  54.8 0.0 copy-start.1
  54.8 2.1 %copy-done.1 = f32[48,80,256]{2,1,0:T(8,128)S(1)} copy-done((f32[48,80,256]{2,1,0:T(8,128)S(1)}, f32[48,80,256]{2,1,0:T(8,128)}, u32[]{:S(2)}) %copy-start.1) | copy-done | bytes 3932184
  56.9 0.0 copy-start.3
  56.9 33.1 %shard_map.119 = (f32[48,80,256]{2,1,0:T(8,128)S(1)}, f32[48,80,256]{2,1,0:T(8,128)S(1)}, bf16[768,256]{1,0:T(8,128)(2,1)S(1)}) custom-call(s32[2]{0:T(128)S(1)} %add_convert_fusion.flags, bf16[768,128]{1,0:T(8,128)(2,1)S(1)} %bitcast.18, f32[48,80,256]{2,1,0:T(8,128)S(1)} %copy-done.1, bf16[5,80,256]{2,1,0:T(8,128)(2,1)S(1)} %collective-permute-done.from_north.north, ...), custom_call_target="tpu_custom_call" | custom-call | tf_op jit(solution)/shard_map/pallas_call | solution.py:37
  90.0 18.4 %all_to_all.10 = bf16[32,24,256]{2,1,0:T(8,128)(2,1)S(1)} all-to-all(bf16[32,24,256]{2,1,0:T(8,128)(2,1)S(1)} %bitcast.20), channel_id=1, replica_groups=mesh['lat'=8,'lon'=4] {'lat','lon'}, dimensions={0} | all-to-all | bytes 786432 | tf_op jit(solution)/shard_map/all_to_all | solution.py:450
  108.4 0.0 copy-done.3
  108.4 3.8 %shard_map.120 = (f32[69,48,256]{2,1,0:T(8,128)}, f32[512,256]{1,0:T(8,128)}) custom-call(bf16[768,256]{1,0:T(8,128)(2,1)S(1)} %bitcast.19, s32[1,512]{1,0:T(1,128)S(1)} %get-tuple-element.35.slot, f32[512,256]{1,0:T(8,128)S(1)} %copy-done.3, f32[69,256]{1,0:T(8,128)S(1)} %copy-done.5, f32[48,80,256]{2,1,0:T(8,128)S(1)} %get-tuple-element.36.first, ...), custom_call_target="tpu_custom_call" | custom-call | tf_op jit(solution)/shard_map/pallas_call | solution.py:37
  (1 shorter events, 0.0 us)
Async XLA Ops:
  0.6 37.1 %copy-start.8 = (f32[256]{0:T(256)S(1)}, f32[256]{0:T(256)}, u32[]{:S(2)}) copy-start(f32[256]{0:T(256)} %param.15) | copy-start | bytes 3076
  1.3 1.0 copy-start.2
  2.3 0.9 copy-start.4
  3.2 0.7 copy-start.7
  3.9 0.7 copy-start.9
  4.6 0.7 copy-start.10
  5.3 0.7 copy-start.11
  6.0 31.6 %copy-start.12 = (bf16[69,64]{0,1:T(8,128)(2,1)S(1)}, bf16[69,64]{0,1:T(8,128)(2,1)}, u32[]{:S(2)}) copy-start(bf16[69,64]{0,1:T(8,128)(2,1)} %param.18) | copy-start | bytes 26500
  6.0 31.7 %copy-start.5 = (f32[69,256]{1,0:T(8,128)S(1)}, f32[69,256]{1,0:T(8,128)}, u32[]{:S(2)}) copy-start(f32[69,256]{1,0:T(8,128)} %jac.5) | copy-start | bytes 211972
  6.0 31.7 %copy-start.6 = (bf16[9,64,69]{2,1,0:T(8,128)(2,1)S(1)}, bf16[9,64,69]{2,1,0:T(8,128)(2,1)}, u32[]{:S(2)}) copy-start(bf16[9,64,69]{2,1,0:T(8,128)(2,1)} %taps.1) | copy-start | bytes 238468
  7.6 16.2 %all-to-all-start = ((bf16[32,24,128]{2,1,0:T(8,128)(2,1)}), bf16[32,24,128]{2,1,0:T(8,128)(2,1)S(1)}, u32[]{:S(2)}, u32[]{:S(2)}) async-start(bf16[32,24,128]{2,1,0:T(8,128)(2,1)} %bitcast.6), calls=%async_computation | async-start | bytes 393216 | tf_op jit(solution)/shard_map/all_to_all | solution.py:450
  26.3 20.6 %collective-permute-start = (bf16[5,80,256]{2,1,0:T(8,128)(2,1)}, bf16[5,80,256]{2,1,0:T(8,128)(2,1)S(1)}, u32[]{:S(2)}, u32[]{:S(2)}) collective-permute-start(bf16[5,80,256]{2,1,0:T(8,128)(2,1)} %get-tuple-element.21), channel_id=1, source_target_pairs={{0,4},{1,5},{2,6},{3,7},{4,8},{5,9},{6,10},{7,11},{8,12},{9,13},{1... | collective-permute-start | bytes 614408 | tf_op jit(solution)/shard_map/ppermute | solution.py:420
  29.1 17.8 %collective-permute-start.1 = (bf16[5,80,256]{2,1,0:T(8,128)(2,1)S(1)}, bf16[5,80,256]{2,1,0:T(8,128)(2,1)S(1)}, u32[]{:S(2)}, u32[]{:S(2)}) collective-permute-start(bf16[5,80,256]{2,1,0:T(8,128)(2,1)S(1)} %get-tuple-element.22), channel_id=1, source_target_pairs={{4,0},{5,1},{6,2},{7,3},{8,4},{9,5},{10,6},{11,7},{12,8},{13,9},{1... | collective-permute-start | bytes 614408 | tf_op jit(solution)/shard_map/ppermute | solution.py:420
  31.1 9.1 %collective-permute-start.3 = (bf16[4,64,256]{2,1,0:T(8,128)(2,1)}, bf16[4,64,256]{2,1,0:T(8,128)(2,1)S(1)}, u32[]{:S(2)}, u32[]{:S(2)}) collective-permute-start(bf16[4,64,256]{2,1,0:T(8,128)(2,1)} %get-tuple-element.38), channel_id=1, source_target_pairs={{4,0},{5,1},{6,2},{7,3},{8,4},{9,5},{10,6},{11,7},{12,8},{13,9},{1... | collective-permute-start | bytes 393224 | tf_op jit(solution)/shard_map/ppermute | solution.py:420
  32.4 11.1 %collective-permute-start.2 = (bf16[4,64,256]{2,1,0:T(8,128)(2,1)S(1)}, bf16[4,64,256]{2,1,0:T(8,128)(2,1)S(1)}, u32[]{:S(2)}, u32[]{:S(2)}) collective-permute-start(bf16[4,64,256]{2,1,0:T(8,128)(2,1)S(1)} %get-tuple-element.39), channel_id=1, source_target_pairs={{0,4},{1,5},{2,6},{3,7},{4,8},{5,9},{6,10},{7,11},{8,12},{9,13},{1... | collective-permute-start | bytes 393224 | tf_op jit(solution)/shard_map/ppermute | solution.py:420
  46.9 1.9 %copy-start = (f32[48,80,256]{2,1,0:T(8,128)}, f32[48,80,256]{2,1,0:T(8,128)S(1)}, u32[]{:S(2)}) copy-start(f32[48,80,256]{2,1,0:T(8,128)S(1)} %shard_map.114._inner.inner) | copy-start | bytes 11796484
  48.8 4.4 %collective-permute-start.4 = (bf16[144,512]{1,0:T(8,128)(2,1)S(1)}, bf16[144,512]{1,0:T(8,128)(2,1)S(1)}, u32[]{:S(2)}, u32[]{:S(2)}) collective-permute-start(bf16[144,512]{1,0:T(8,128)(2,1)S(1)} %get-tuple-element.28), channel_id=1, source_target_pairs={{0,3},{1,0},{2,1},{3,2},{4,7},{5,4},{6,5},{7,6},{8,11},{9,8},{10,9... | collective-permute-start | bytes 442376 | tf_op jit(solution)/shard_map/ppermute | solution.py:420
  49.3 5.5 %collective-permute-start.5 = (bf16[144,512]{1,0:T(8,128)(2,1)S(1)}, bf16[144,512]{1,0:T(8,128)(2,1)S(1)}, u32[]{:S(2)}, u32[]{:S(2)}) collective-permute-start(bf16[144,512]{1,0:T(8,128)(2,1)S(1)} %get-tuple-element.29), channel_id=1, source_target_pairs={{0,1},{1,2},{2,3},{3,0},{4,5},{5,6},{6,7},{7,4},{8,9},{9,10},{10,1... | collective-permute-start | bytes 442376 | tf_op jit(solution)/shard_map/ppermute | solution.py:420
  54.8 2.1 %copy-start.1 = (f32[48,80,256]{2,1,0:T(8,128)S(1)}, f32[48,80,256]{2,1,0:T(8,128)}, u32[]{:S(2)}) copy-start(f32[48,80,256]{2,1,0:T(8,128)} %copy-done) | copy-start | bytes 11796484
  56.9 51.5 %copy-start.3 = (f32[512,256]{1,0:T(8,128)S(1)}, f32[512,256]{1,0:T(8,128)}, u32[]{:S(2)}) copy-start(f32[512,256]{1,0:T(8,128)} %dep.3) | copy-start | bytes 1572868

commit v4 on v3

--- a/solution.py
+++ b/solution.py
@@ -27,7 +27,7 @@
         if i < smem:
             return pl.BlockSpec(memory_space=pltpu.SMEM)
         if i >= len(args) - unread:
-            return pl.BlockSpec(memory_space=pl.ANY)
+            return pl.BlockSpec(memory_space=pltpu.HBM if scratch else pl.ANY)
         if staged:
             return pl.BlockSpec(x.shape, lambda _: (0,) * x.ndim)
         return pl.BlockSpec(memory_space=pltpu.VMEM)
@@ -53,8 +53,14 @@
     return hi, mid, (rest - mid.astype(F32)).astype(BF)
 
 
-def pack_kernel(tiles, cap, lon_size, channels, count, dep, owner_row, cell_row, qc_row,
-                weight, jac, send, slot_out):
+def pack_kernel(tiles, cap, lon_size, channels, count, *refs):
+    sources, (send, slot_out), held, sems = refs[:6], refs[6:8], refs[8:14], refs[14]
+    copies = [pltpu.make_async_copy(src, dst, sems.at[k]) for k, (src, dst) in enumerate(zip(sources, held))]
+    for copy in copies:
+        copy.start()
+    for copy in copies:
+        copy.wait()
+    dep, owner_row, cell_row, qc_row, weight, jac = held
     rows = dep.shape[0]
     slots = send.shape[0]
     hit = (lax.broadcasted_iota(jnp.int32, (tiles, rows), 0) == owner_row[...]).astype(BF)
@@ -120,31 +126,38 @@
     return jnp.where(keep, turn[:padded], 0.0), lat_row, lon_row, lat_col, lon_col
 
 
-def edge_kernel(channels, height, breadth, got, north, south, west, east):
-    padded = north.shape[1]
+def edge_kernel(channels, height, got, _slope_north, _slope_south, north, south):
+    tall, breadth = north.shape
+    trim = tall // HALO
     slots = got.shape[0]
-    turn, lat_row, lon_row, lat, lon = turned(got, channels, padded)
+    turn, lat_row, _, _, lon = turned(got, channels, -(-trim // 16) * 16)
     values = turn.astype(BF)
     col_hot = (lax.broadcasted_iota(jnp.int32, (slots, breadth), 1) == lon).astype(BF)
     for out, first in ((north, 0), (south, height - HALO)):
         lhs = jnp.concatenate(
             [values * (lat_row == first + k).astype(F32).astype(BF) for k in range(HALO)], axis=0)
-        out[:HALO] = mxu(lhs, col_hot).reshape(HALO, padded, breadth).astype(BF)
-    at_west, at_east = lon < HALO, lon >= breadth - HALO
-    at_north, at_south = lat < HALO, lat >= height - HALO
-    col_west, col_east = HALO + lon, lon - (breadth - HALO)
-
-    def place(mask, row, col, lanes):
-        target = jnp.where(mask, row * SIDE + col, -1)
-        hot = (lax.broadcasted_iota(jnp.int32, (slots, lanes), 1) == target).astype(BF)
-        return mxu(values, hot).astype(BF)
-
-    west[...] = place(at_west, lat + HALO, col_west, west.shape[1])
-    east[...] = place(at_east, lat + HALO, col_east, east.shape[1])
-    below = (height + HALO) % (LANES // SIDE)
-    for out, mask, row in ((north, at_north, lat + below), (south, at_south, lat - (height - HALO))):
-        out[HALO, :, :LANES] = place(mask & at_west, row, col_west, LANES)
-        out[HALO, :, LANES : 2 * LANES] = place(mask & at_east, row, col_east, LANES)
+        rows = mxu(lhs, col_hot).reshape(HALO, values.shape[0], breadth)[:, :trim]
+        out[...] = rows.reshape(tall, breadth).astype(BF)
+
+
+def rows_of(message, padded):
+    tall, breadth = message.shape
+    rows = message[...].astype(F32).reshape(HALO, tall // HALO, breadth)
+    return jnp.concatenate([rows, jnp.zeros((HALO, padded - tall // HALO, breadth), F32)], axis=1)
+
+
+def side_kernel(channels, height, breadth, got, west, east):
+    padded, strip = west.shape
+    slots = got.shape[0]
+    turn, _, _, lat, lon = turned(got, channels, padded)
+    values = turn.astype(BF)
+    for out, mask, col in (
+        (west, lon < HALO, HALO + lon),
+        (east, lon >= breadth - HALO, lon - (breadth - HALO)),
+    ):
+        target = jnp.where(mask, (lat + HALO) * SIDE + col, -1)
+        hot = (lax.broadcasted_iota(jnp.int32, (slots, strip), 1) == target).astype(BF)
+        out[...] = mxu(values, hot).astype(BF)
 
 
 def grid_kernel(channels, got, out):
@@ -164,44 +177,46 @@
     lax.fori_loop(0, height // step, body, 0)
 
 
+def to_strip(rows, base, block):
+    per = LANES // SIDE
+    shape = (rows[0].shape[0], LANES)
+    lane = lax.broadcasted_iota(jnp.int32, shape, 1)
+    left, right = jnp.zeros(shape, F32), jnp.zeros(shape, F32)
+    for k, row in enumerate(rows):
+        at = base + k - block * per
+        if not 0 <= at < per:
+            continue
+        row = row.astype(F32)
+        by = (at * SIDE + HALO) % LANES
+        mine = (lane >= at * SIDE) & (lane < (at + 1) * SIDE)
+        left = jnp.where(mine & (lane % SIDE >= HALO), pltpu.roll(row[:, :LANES], by, 1), left)
+        right = jnp.where(mine & (lane % SIDE < HALO), pltpu.roll(row[:, -LANES:], by, 1), right)
+    return left, right
+
+
 def strip_kernel(inner, north, south, west, east):
-    height, hidden, breadth = inner.shape
-    per = LANES // SIDE
-    lane = lax.broadcasted_iota(jnp.int32, (hidden, LANES), 1)
+    height = inner.shape[0]
+    rows = [north[k] for k in range(HALO)] + [inner[k] for k in range(height)] + [south[k] for k in range(HALO)]
     for block in range(west.shape[1] // LANES):
-        left = jnp.zeros((hidden, LANES), F32)
-        right = jnp.zeros((hidden, LANES), F32)
-        for k in range(per):
-            i = block * per + k
-            if i < HALO:
-                row = north[i]
-            elif i < HALO + height:
-                row = inner[i - HALO]
-            elif i < height + 2 * HALO:
-                row = south[i - HALO - height]
-            else:
-                break
-            row = row.astype(F32)
-            mine = (lane >= k * SIDE) & (lane < (k + 1) * SIDE)
-            left = jnp.where(mine, pltpu.roll(row[:, :LANES], (k * SIDE + HALO) % LANES, 1), left)
-            right = jnp.where(mine, pltpu.roll(row[:, breadth - LANES :], (k * SIDE + HALO) % LANES, 1), right)
+        left, right = to_strip(rows, 0, block)
         west[:, block * LANES : (block + 1) * LANES] = left.astype(BF)
         east[:, block * LANES : (block + 1) * LANES] = right.astype(BF)
 
 
-def join_kernel(height, west, east, from_north, from_south, slope_west, slope_east, _inner, _weights,
-                to_west, to_east):
+def join_kernel(height, west, east, from_north, from_south, slope_west, slope_east, _token, to_west, to_east):
     padded, strip = west.shape
     last = (height + HALO) * SIDE // LANES
+    above, below = rows_of(from_north, padded), rows_of(from_south, padded)
+    above = to_strip([above[k] for k in range(HALO)], 0, 0)
+    below = to_strip([below[k] for k in range(HALO)], HALO + height, last)
     for k, own, slope, out in ((0, west, slope_west, to_west), (1, east, slope_east, to_east)):
-        corner = pl.ds(k * LANES, LANES)
         for block in range(strip // LANES):
             part = pl.ds(block * LANES, LANES)
             q = own[:, part]
             if block == 0:
-                q = q + from_north[HALO, :, corner]
+                q = q + above[k].astype(BF)
             if block == last:
-                q = q + from_south[HALO, :, corner]
+                q = q + below[k].astype(BF)
             out[:padded, part] = q
         out[padded:] = slope[...]
 
@@ -246,8 +261,9 @@
             ys.append(y)
         pull(i, ys)
 
-    begin(0, [north[k] for k in range(HALO)], [slope_north[k] for k in range(HALO)], HALO)
-    begin(HALO + height, [south[k] for k in range(HALO)], [slope_south[k] for k in range(HALO)], HALO)
+    above, below = rows_of(north, padded), rows_of(south, padded)
+    begin(0, [above[k] for k in range(HALO)], [slope_north[k] for k in range(HALO)], HALO)
+    begin(HALO + height, [below[k] for k in range(HALO)], [slope_south[k] for k in range(HALO)], HALO)
 
     def middle(n, _):
         i = n * HALO
@@ -437,13 +453,14 @@
         return jax.ShapeDtypeStruct(dims, kind)
 
     weight = channel_weight[None, :]
+    inputs = (departure_in, obs_owner.reshape(1, rows), obs_cell[None, :], qc_mask[None, :], weight, jacobian)
     send, slot = call(
         functools.partial(pack_kernel, tiles, cap, breadth, channels),
         (shape((slots, LANES), BF), shape((1, rows), jnp.int32)),
-        (obs_count, departure_in, obs_owner.reshape(1, rows), obs_cell[None, :],
-         qc_mask[None, :], weight, jacobian),
+        (obs_count,) + inputs,
+        scratch=[pltpu.VMEM(x.shape, x.dtype) for x in inputs] + [pltpu.SemaphoreType.DMA((len(inputs),))],
         smem=1,
-        staged=True,
+        unread=len(inputs),
     )
 
     def swap(x):
@@ -466,23 +483,26 @@
     slope_west, slope_east = call(strip_kernel, (shape((hidden, strip), BF),) * 2,
                                   (slope_inner, slope_north, slope_south))
 
-    edge = (HALO + 1, padded, breadth)
-    north, south, west, east = call(
-        functools.partial(edge_kernel, channels, height, breadth),
-        (shape(edge, BF),) * 2 + (shape((padded, strip), BF),) * 2,
-        (got,),
+    trim = -(-(channels + 1) // 8) * 8
+    north, south = call(
+        functools.partial(edge_kernel, channels, height),
+        (shape((HALO * trim, breadth), BF),) * 2,
+        (got, slope_north, slope_south),
+        unread=2,
     )
     from_south = shift2(north, -1, 0)
     from_north = shift2(south, 1, 0)
-    inner = call(functools.partial(grid_kernel, channels), shape((height, padded, breadth)), (got,))
+    west, east = call(
+        functools.partial(side_kernel, channels, height, breadth), (shape((padded, strip), BF),) * 2, (got,))
     to_west, to_east = call(
         functools.partial(join_kernel, height),
         (shape((padded + hidden, strip), BF),) * 2,
-        (west, east, from_north, from_south, slope_west, slope_east, inner, w_m),
-        unread=2,
+        (west, east, from_north, from_south, slope_west, slope_east, p_t),
+        unread=1,
     )
     from_east = shift2(to_west, 0, -1)
     from_west = shift2(to_east, 0, 1)
+    inner = call(functools.partial(grid_kernel, channels), shape((height, padded, breadth)), (got,))
 
     at = lax.axis_index("lat")
     flags = jnp.stack([at > 0, at < lax.axis_size("lat") - 1]).astype(jnp.int32)

time: 113 us -> 101 us (0.89)
  waiting for transfers between devices: 17.2 us -> 10.9 us
  local copies, waits for them, and re-layouts: 11.4 us -> 6.72 us
    all_to_all x1, waiting for transfers between devices: 6.95 us -> 0.01 us  [swap(): lax.all_to_all(x.reshape(tiles, cap, -1), ('lat', 'lon'), split_axis=0, c...]
    unnamed x28 -> x24, local copies, waits for them, and re-layouts: 10.7 us -> 6.7 us
    pallas_call x8 -> x9, Pallas kernels: 45.3 us -> 44.6 us  [call(): pl.pallas_call(kernel, out_shape=outs, grid=(1,) if staged else (), in_sp...]
  transfers between devices with their start and end apart: 7 -> 7, of which waited for: 5 -> 4; matrix products, arithmetic and copies ran while one was open for 2% -> 2% of each run, Pallas kernels for 4% -> 5%
where the time goes in v4:
time: 101 us
  Pallas kernels  44.6 us (44%)
  starting transfers between devices  19.4 us (19%)
  blocking collectives  17.5 us (17%)
  waiting for transfers between devices  10.9 us (11%)
  local copies, waits for them, and re-layouts  6.72 us (7%)
  between operations  1.64 us (2%)
    pallas_call x9, Pallas kernels, call(): pl.pallas_call(kernel, out_shape=outs, grid=(1,) if staged else (), in_sp...  44.6 us
    all_to_all x1, blocking collectives, swap(): lax.all_to_all(x.reshape(tiles, cap, -1), ('lat', 'lon'), split_axis=0, c...  17.5 us
    ppermute x6, starting transfers between devices, shift2(): return lax.ppermute(x, ('lat', 'lon'), pairs)  12.1 us
    ppermute x6, waiting for transfers between devices, shift2(): return lax.ppermute(x, ('lat', 'lon'), pairs)  10.9 us
    all_to_all x1, starting transfers between devices, swap(): lax.all_to_all(x.reshape(tiles, cap, -1), ('lat', 'lon'), split_axis=0, c...  7.3 us
    unnamed x24, local copies, waits for them, and re-layouts  6.7 us
  transfers between devices with their start and end apart: 7, of which 4 were waited for; matrix products, arithmetic and copies ran while one was open for 2% of the time, Pallas kernels for 5%

profile of v4, /device:TPU:0, one launch (start us, length us, event | category | flops | bytes accessed | tf_op | source)
XLA Modules:
  0.0 100.7 jit_solution(4098924379678627607)
XLA Ops:
  0.6 0.0 copy-start.6
  1.3 0.0 copy-start
  1.3 1.0 %copy-done = f32[512,256]{1,0:T(8,128)S(1)} copy-done((f32[512,256]{1,0:T(8,128)S(1)}, f32[512,256]{1,0:T(8,128)}, u32[]{:S(2)}) %copy-start) | copy-done | bytes 524312
  2.3 0.0 copy-start.2
  2.3 0.9 copy-done.2
  3.2 0.0 copy-start.5
  3.2 0.7 copy-done.5
  3.9 0.0 copy-start.7
  3.9 0.7 copy-done.7
  4.6 0.0 copy-start.8
  4.6 0.7 copy-done.8
  5.3 0.0 copy-start.9
  5.3 0.7 copy-done.9
  6.0 0.0 copy-start.10
  6.0 0.0 copy-start.3
  6.0 0.0 copy-start.4
  6.0 1.8 %shard_map.113 = (bf16[768,128]{1,0:T(8,128)(2,1)}, s32[1,512]{1,0:T(1,128)S(1)}) custom-call(s32[1]{0:T(128)S(6)} %copy.16.count, f32[512,256]{1,0:T(8,128)S(1)} %copy-done, s32[1,512]{1,0:T(1,128)S(1)} %bitcast.24, s32[1,512]{1,0:T(1,128)S(1)} %bitcast.25, s32[1,512]{1,0:T(1,128)S(1)} %bitcast.26, f32[1,256]{1,0:T(1,128)S(1)} %bitcast.22, ...), custom_call_target="tpu_custom_call" | custom-call | tf_op jit(solution)/shard_map/pallas_call | solution.py:37
  7.8 7.3 %all-to-all-start = ((bf16[32,24,128]{2,1,0:T(8,128)(2,1)}), bf16[32,24,128]{2,1,0:T(8,128)(2,1)S(1)}, u32[]{:S(2)}, u32[]{:S(2)}) async-start(bf16[32,24,128]{2,1,0:T(8,128)(2,1)} %bitcast.6), calls=%async_computation | async-start | bytes 393216 | tf_op jit(solution)/shard_map/all_to_all | solution.py:467
  15.1 1.9 %copy.15 = bf16[64,48,256]{2,0,1:T(8,128)(2,1)S(1)} copy(bf16[64,48,256]{2,1,0:T(8,128)(2,1)} %param.19) | data formatting | bytes 3145728 | tf_op args[9]
  17.1 1.3 %collective-permute-start.1 = (bf16[4,64,256]{2,1,0:T(8,128)(2,1)S(1)}, bf16[4,64,256]{2,1,0:T(8,128)(2,1)S(1)}, u32[]{:S(2)}, u32[]{:S(2)}) collective-permute-start(bf16[4,64,256]{2,1,0:T(8,128)(2,1)S(1)} %get-tuple-element.38), channel_id=1, source_target_pairs={{4,0},{5,1},{6,2},{7,3},{8,4},{9,5},{10,6},{11,7},{12,8},{13,9},{1... | collective-permute-start | bytes 393224 | tf_op jit(solution)/shard_map/ppermute | solution.py:436
  18.4 4.6 %collective-permute-start = (bf16[4,64,256]{2,1,0:T(8,128)(2,1)S(1)}, bf16[4,64,256]{2,1,0:T(8,128)(2,1)S(1)}, u32[]{:S(2)}, u32[]{:S(2)}) collective-permute-start(bf16[4,64,256]{2,1,0:T(8,128)(2,1)S(1)} %get-tuple-element.39), channel_id=1, source_target_pairs={{0,4},{1,5},{2,6},{3,7},{4,8},{5,9},{6,10},{7,11},{8,12},{9,13},{1... | collective-permute-start | bytes 393224 | tf_op jit(solution)/shard_map/ppermute | solution.py:436
  22.9 2.2 %collective-permute-done.1._slope_south.south.slope_south = bf16[4,64,256]{2,1,0:T(8,128)(2,1)S(1)} collective-permute-done((bf16[4,64,256]{2,1,0:T(8,128)(2,1)S(1)}, bf16[4,64,256]{2,1,0:T(8,128)(2,1)S(1)}, u32[]{:S(2)}, u32[]{:S(2)}) %collective-permute-start.1) | collective-permute-done | bytes 131104 | tf_op jit(solution)/shard_map/ppermute | solution.py:436
  25.1 2.5 %collective-permute-done._slope_north.north.slope_north = bf16[4,64,256]{2,1,0:T(8,128)(2,1)S(1)} collective-permute-done((bf16[4,64,256]{2,1,0:T(8,128)(2,1)S(1)}, bf16[4,64,256]{2,1,0:T(8,128)(2,1)S(1)}, u32[]{:S(2)}, u32[]{:S(2)}) %collective-permute-start) | collective-permute-done | bytes 131104 | tf_op jit(solution)/shard_map/ppermute | solution.py:436
  27.6 0.0 all-to-all-done
  27.6 0.5 shard_map.115
  28.2 4.4 %collective-permute-start.2 = (bf16[288,256]{1,0:T(8,128)(2,1)S(1)}, bf16[288,256]{1,0:T(8,128)(2,1)S(1)}, u32[]{:S(2)}, u32[]{:S(2)}) collective-permute-start(bf16[288,256]{1,0:T(8,128)(2,1)S(1)} %get-tuple-element.21), channel_id=1, source_target_pairs={{0,4},{1,5},{2,6},{3,7},{4,8},{5,9},{6,10},{7,11},{8,12},{9,13},{1... | collective-permute-start | bytes 442376 | tf_op jit(solution)/shard_map/ppermute | solution.py:436
  32.6 1.3 %collective-permute-start.3 = (bf16[288,256]{1,0:T(8,128)(2,1)S(1)}, bf16[288,256]{1,0:T(8,128)(2,1)S(1)}, u32[]{:S(2)}, u32[]{:S(2)}) collective-permute-start(bf16[288,256]{1,0:T(8,128)(2,1)S(1)} %get-tuple-element.22), channel_id=1, source_target_pairs={{4,0},{5,1},{6,2},{7,3},{8,4},{9,5},{10,6},{11,7},{12,8},{13,9},{1... | collective-permute-start | bytes 442376 | tf_op jit(solution)/shard_map/ppermute | solution.py:436
  33.9 0.0 copy-done.10
  33.9 0.1 copy.13.projection
  34.0 0.0 copy-done.6
  34.0 0.0 copy-done.3
  34.0 0.0 copy-done.4
  34.0 0.9 shard_map.118
  34.9 0.6 shard_map.117
  35.5 1.0 %shard_map.116 = (bf16[80,512]{1,0:T(8,128)(2,1)S(1)}, bf16[80,512]{1,0:T(8,128)(2,1)S(1)}) custom-call(bf16[768,128]{1,0:T(8,128)(2,1)S(1)} %bitcast.17), custom_call_target="tpu_custom_call" | custom-call | tf_op jit(solution)/shard_map/pallas_call | solution.py:37
  36.5 0.0 collective-permute-done.2.from_north.north
  36.5 3.4 %collective-permute-done.3.from_south.south = bf16[288,256]{1,0:T(8,128)(2,1)S(1)} collective-permute-done((bf16[288,256]{1,0:T(8,128)(2,1)S(1)}, bf16[288,256]{1,0:T(8,128)(2,1)S(1)}, u32[]{:S(2)}, u32[]{:S(2)}) %collective-permute-start.3) | collective-permute-done | bytes 147488 | tf_op jit(solution)/shard_map/ppermute | solution.py:436
  40.0 0.2 shard_map.119
  40.1 0.1 collective-permute-start.4
  40.2 0.5 collective-permute-start.5
  40.7 0.1 add_convert_fusion.flags
  40.8 2.8 %shard_map.114.inner = f32[48,80,256]{2,1,0:T(8,128)S(1)} custom-call(bf16[768,128]{1,0:T(8,128)(2,1)S(1)} %bitcast.18), custom_call_target="tpu_custom_call" | custom-call | tf_op jit(solution)/shard_map/pallas_call | solution.py:37
  43.6 0.0 collective-permute-done.4.from_east
  43.6 2.7 %collective-permute-done.5.from_west = bf16[144,512]{1,0:T(8,128)(2,1)S(1)} collective-permute-done((bf16[144,512]{1,0:T(8,128)(2,1)S(1)}, bf16[144,512]{1,0:T(8,128)(2,1)S(1)}, u32[]{:S(2)}, u32[]{:S(2)}) %collective-permute-start.5) | collective-permute-done | bytes 147488 | tf_op jit(solution)/shard_map/ppermute | solution.py:436
  46.3 0.0 copy-start.1
  46.3 33.0 %shard_map.120 = (f32[48,80,256]{2,1,0:T(8,128)S(1)}, f32[48,80,256]{2,1,0:T(8,128)S(1)}, bf16[768,256]{1,0:T(8,128)(2,1)S(1)}) custom-call(s32[2]{0:T(128)S(1)} %add_convert_fusion.flags, bf16[768,128]{1,0:T(8,128)(2,1)S(1)} %bitcast.19, f32[48,80,256]{2,1,0:T(8,128)S(1)} %shard_map.114.inner, bf16[288,256]{1,0:T(8,128)(2,1)S(1)} %collective-permute-done.2.from_north.north, ...), custom_call_target="tpu_custom_call" | custom-call | tf_op jit(solution)/shard_map/pallas_call | solution.py:37
  79.3 17.5 %all_to_all.10 = bf16[32,24,256]{2,1,0:T(8,128)(2,1)S(1)} all-to-all(bf16[32,24,256]{2,1,0:T(8,128)(2,1)S(1)} %bitcast.21), channel_id=1, replica_groups=mesh['lat'=8,'lon'=4] {'lat','lon'}, dimensions={0} | all-to-all | bytes 786432 | tf_op jit(solution)/shard_map/all_to_all | solution.py:467
  96.8 0.0 copy-done.1
  96.8 3.8 %shard_map.121 = (f32[69,48,256]{2,1,0:T(8,128)}, f32[512,256]{1,0:T(8,128)}) custom-call(bf16[768,256]{1,0:T(8,128)(2,1)S(1)} %bitcast.20, s32[1,512]{1,0:T(1,128)S(1)} %get-tuple-element.35.slot, f32[512,256]{1,0:T(8,128)S(1)} %copy-done.1, f32[69,256]{1,0:T(8,128)S(1)} %copy-done.3, f32[48,80,256]{2,1,0:T(8,128)S(1)} %get-tuple-element.36.first, ...), custom_call_target="tpu_custom_call" | custom-call | tf_op jit(solution)/shard_map/pallas_call | solution.py:37
  (1 shorter events, 0.0 us)
Async XLA Ops:
  0.6 33.4 %copy-start.6 = (f32[256]{0:T(256)S(1)}, f32[256]{0:T(256)}, u32[]{:S(2)}) copy-start(f32[256]{0:T(256)} %param.15) | copy-start | bytes 3076
  1.3 1.0 %copy-start = (f32[512,256]{1,0:T(8,128)S(1)}, f32[512,256]{1,0:T(8,128)}, u32[]{:S(2)}) copy-start(f32[512,256]{1,0:T(8,128)} %dep.1) | copy-start | bytes 1572868
  2.3 0.9 copy-start.2
  3.2 0.7 copy-start.5
  3.9 0.7 copy-start.7
  4.6 0.7 copy-start.8
  5.3 0.7 copy-start.9
  6.0 27.9 %copy-start.10 = (bf16[69,64]{0,1:T(8,128)(2,1)S(1)}, bf16[69,64]{0,1:T(8,128)(2,1)}, u32[]{:S(2)}) copy-start(bf16[69,64]{0,1:T(8,128)(2,1)} %param.18) | copy-start | bytes 26500
  6.0 28.0 %copy-start.3 = (f32[69,256]{1,0:T(8,128)S(1)}, f32[69,256]{1,0:T(8,128)}, u32[]{:S(2)}) copy-start(f32[69,256]{1,0:T(8,128)} %jac.3) | copy-start | bytes 211972
  6.0 28.0 %copy-start.4 = (bf16[9,64,69]{2,1,0:T(8,128)(2,1)S(1)}, bf16[9,64,69]{2,1,0:T(8,128)(2,1)}, u32[]{:S(2)}) copy-start(bf16[9,64,69]{2,1,0:T(8,128)(2,1)} %taps.1) | copy-start | bytes 238468
  7.8 19.8 %all-to-all-start = ((bf16[32,24,128]{2,1,0:T(8,128)(2,1)}), bf16[32,24,128]{2,1,0:T(8,128)(2,1)S(1)}, u32[]{:S(2)}, u32[]{:S(2)}) async-start(bf16[32,24,128]{2,1,0:T(8,128)(2,1)} %bitcast.6), calls=%async_computation | async-start | bytes 393216 | tf_op jit(solution)/shard_map/all_to_all | solution.py:467
  17.1 8.1 %collective-permute-start.1 = (bf16[4,64,256]{2,1,0:T(8,128)(2,1)S(1)}, bf16[4,64,256]{2,1,0:T(8,128)(2,1)S(1)}, u32[]{:S(2)}, u32[]{:S(2)}) collective-permute-start(bf16[4,64,256]{2,1,0:T(8,128)(2,1)S(1)} %get-tuple-element.38), channel_id=1, source_target_pairs={{4,0},{5,1},{6,2},{7,3},{8,4},{9,5},{10,6},{11,7},{12,8},{13,9},{1... | collective-permute-start | bytes 393224 | tf_op jit(solution)/shard_map/ppermute | solution.py:436
  18.4 9.2 %collective-permute-start = (bf16[4,64,256]{2,1,0:T(8,128)(2,1)S(1)}, bf16[4,64,256]{2,1,0:T(8,128)(2,1)S(1)}, u32[]{:S(2)}, u32[]{:S(2)}) collective-permute-start(bf16[4,64,256]{2,1,0:T(8,128)(2,1)S(1)} %get-tuple-element.39), channel_id=1, source_target_pairs={{0,4},{1,5},{2,6},{3,7},{4,8},{5,9},{6,10},{7,11},{8,12},{9,13},{1... | collective-permute-start | bytes 393224 | tf_op jit(solution)/shard_map/ppermute | solution.py:436
  28.2 8.3 %collective-permute-start.2 = (bf16[288,256]{1,0:T(8,128)(2,1)S(1)}, bf16[288,256]{1,0:T(8,128)(2,1)S(1)}, u32[]{:S(2)}, u32[]{:S(2)}) collective-permute-start(bf16[288,256]{1,0:T(8,128)(2,1)S(1)} %get-tuple-element.21), channel_id=1, source_target_pairs={{0,4},{1,5},{2,6},{3,7},{4,8},{5,9},{6,10},{7,11},{8,12},{9,13},{1... | collective-permute-start | bytes 442376 | tf_op jit(solution)/shard_map/ppermute | solution.py:436
  32.6 7.4 %collective-permute-start.3 = (bf16[288,256]{1,0:T(8,128)(2,1)S(1)}, bf16[288,256]{1,0:T(8,128)(2,1)S(1)}, u32[]{:S(2)}, u32[]{:S(2)}) collective-permute-start(bf16[288,256]{1,0:T(8,128)(2,1)S(1)} %get-tuple-element.22), channel_id=1, source_target_pairs={{4,0},{5,1},{6,2},{7,3},{8,4},{9,5},{10,6},{11,7},{12,8},{13,9},{1... | collective-permute-start | bytes 442376 | tf_op jit(solution)/shard_map/ppermute | solution.py:436
  40.1 3.5 %collective-permute-start.4 = (bf16[144,512]{1,0:T(8,128)(2,1)S(1)}, bf16[144,512]{1,0:T(8,128)(2,1)S(1)}, u32[]{:S(2)}, u32[]{:S(2)}) collective-permute-start(bf16[144,512]{1,0:T(8,128)(2,1)S(1)} %get-tuple-element.28), channel_id=1, source_target_pairs={{0,3},{1,0},{2,1},{3,2},{4,7},{5,4},{6,5},{7,6},{8,11},{9,8},{10,9... | collective-permute-start | bytes 442376 | tf_op jit(solution)/shard_map/ppermute | solution.py:436
  40.2 6.1 %collective-permute-start.5 = (bf16[144,512]{1,0:T(8,128)(2,1)S(1)}, bf16[144,512]{1,0:T(8,128)(2,1)S(1)}, u32[]{:S(2)}, u32[]{:S(2)}) collective-permute-start(bf16[144,512]{1,0:T(8,128)(2,1)S(1)} %get-tuple-element.29), channel_id=1, source_target_pairs={{0,1},{1,2},{2,3},{3,0},{4,5},{5,6},{6,7},{7,4},{8,9},{9,10},{10,1... | collective-permute-start | bytes 442376 | tf_op jit(solution)/shard_map/ppermute | solution.py:436
  46.3 50.4 %copy-start.1 = (f32[512,256]{1,0:T(8,128)S(1)}, f32[512,256]{1,0:T(8,128)}, u32[]{:S(2)}) copy-start(f32[512,256]{1,0:T(8,128)} %dep.1) | copy-start | bytes 1572868

commit v5 on v4

--- a/solution.py
+++ b/solution.py
@@ -15,7 +15,7 @@
 BF = jnp.bfloat16
 F32 = jnp.float32
 INTERPRET = False
-G = (9, 13, 10, 12, 16)
+G = (18, 26, 25, 24, 24, 24)
 
 
 def mxu(a, b, dims=((1,), (0,)), precision=None):
@@ -87,23 +87,23 @@
 
 def weights_kernel(taps, projection, jac, weight, w_m, w_n, p_t, p_j, g3):
     _, hidden, channels = taps.shape
-    padded = p_j.shape[0]
+    trim, padded = p_j.shape[0], p_t.shape[1]
 
     def shifted(rows, columns, by):
         return (lax.broadcasted_iota(jnp.int32, (rows, columns), 0) + by
                 == lax.broadcasted_iota(jnp.int32, (rows, columns), 1)).astype(BF)
 
-    wider = shifted(channels, padded, 0)
+    wider, fuller = shifted(channels, padded, 0), shifted(channels, trim, 0)
     for b in range(3):
         total_m, total_n = 0.0, 0.0
         for a in range(3):
             tap = taps[3 * a + b]
             total_m = total_m + mxu(tap, shifted(channels, 3 * padded, a * padded))
-            turned_tap = mxu(wider, tap, ((0,), (1,))).astype(BF)
+            turned_tap = mxu(fuller, tap, ((0,), (1,))).astype(BF)
             total_n = total_n + mxu(turned_tap, shifted(hidden, 3 * hidden, (2 - a) * hidden))
         w_m[b * hidden : (b + 1) * hidden] = total_m.astype(BF)
-        w_n[b * padded : (b + 1) * padded] = total_n.astype(BF)
-    p_j[...] = mxu(wider, projection[...], ((0,), (0,))).astype(BF)
+        w_n[b * trim : (b + 1) * trim] = total_n.astype(BF)
+    p_j[...] = mxu(fuller, projection[...], ((0,), (0,))).astype(BF)
     p_t[...] = mxu(projection[...], wider, ((0,), (0,))).astype(BF)
     tall = jnp.concatenate([jac[...], jnp.zeros((padded - channels, jac.shape[1]), F32)], axis=0)
     gram = mxu(tall * weight[...], tall, ((1,), (1,)), lax.Precision.HIGHEST)
@@ -112,7 +112,7 @@
     total = 0.0
     for k, value in enumerate((hi, lo, hi)):
         total = total + mxu(value, shifted(padded, 3 * padded, k * padded))
-    g3[...] = total.astype(BF)
+    g3[...] = total[:trim].astype(BF)
 
 
 def turned(got, channels, padded):
@@ -143,6 +143,8 @@
 def rows_of(message, padded):
     tall, breadth = message.shape
     rows = message[...].astype(F32).reshape(HALO, tall // HALO, breadth)
+    if padded == tall // HALO:
+        return rows
     return jnp.concatenate([rows, jnp.zeros((HALO, padded - tall // HALO, breadth), F32)], axis=1)
 
 
@@ -161,7 +163,8 @@
 
 
 def grid_kernel(channels, got, out):
-    height, padded, breadth = out.shape
+    height, trim, breadth = out.shape
+    padded = -(-trim // 16) * 16
     slots = got.shape[0]
     turn, lat_row, _, _, lon = turned(got, channels, padded)
     values = turn.astype(BF)
@@ -171,7 +174,7 @@
     def body(block, _):
         lhs = jnp.concatenate(
             [values * (lat_row == block * step + k).astype(F32).astype(BF) for k in range(step)], axis=0)
-        out[pl.ds(block * step, step)] = mxu(lhs, col_hot).reshape(step, padded, breadth)
+        out[pl.ds(block * step, step)] = mxu(lhs, col_hot).reshape(step, padded, breadth)[:, :trim]
         return 0
 
     lax.fori_loop(0, height // step, body, 0)
@@ -224,7 +227,8 @@
 def main_kernel(channels, hidden, cap, flags, got, inner, north, south, from_east, from_west, slope_inner,
                 slope_north, slope_south, w_n, w_m, p_t, p_j, g3, first_out, second_out, reply,
                 field, slope, ga, xb, vec, hi, found):
-    height, padded, breadth = inner.shape
+    height, trim, breadth = inner.shape
+    padded = xb.shape[1]
     wide = breadth + LANES
     ext = height + 2 * HALO
     per = LANES // SIDE
@@ -240,45 +244,49 @@
     def part(x, k):
         return x[:, k * wide : (k + 1) * wide]
 
+    def fill(x):
+        return jnp.concatenate([x, jnp.zeros((padded - trim, x.shape[1]), F32)], axis=0).astype(BF)
+
     def pull(i, ys):
-        u = mxu(p_t[...], join([y.astype(BF) for y in ys]))
+        u = mxu(p_t[...], join([fill(y) for y in ys]))
         for k in range(len(ys)):
             ga[i + k] = (slope[i + k].astype(F32) * part(u, k)).astype(BF)
 
     lane = lax.broadcasted_iota(jnp.int32, (padded + hidden, LANES), 1)
     from_the_west = lane % SIDE < HALO
 
-    def begin(i, mains, slopes, count):
-        at = pl.ds(pl.multiple_of(i // per * LANES, LANES), LANES)
-        both = jnp.where(from_the_west, from_west[:, at].astype(F32), from_east[:, at].astype(F32))
+    def begin(i, mains, slopes):
         ys = []
-        for k in range(count):
-            shift = 2 * LANES - ((i % per) + k) * SIDE - HALO
+        for k in range(len(mains)):
+            if k % HALO == 0:
+                at = pl.ds(pl.multiple_of((i + k) // per * LANES, LANES), LANES)
+                both = jnp.where(from_the_west, from_west[:, at].astype(F32), from_east[:, at].astype(F32))
+            shift = 2 * LANES - (i + k) % per * SIDE - HALO
             edge = pltpu.roll(both, shift % LANES, 1)
-            y = join([mains[k].astype(F32), edge[:padded]])
+            y = join([mains[k].astype(F32), edge[:trim]])
             field[i + k] = y
             slope[i + k] = join([slopes[k], edge[padded:].astype(BF)])
             ys.append(y)
         pull(i, ys)
 
-    above, below = rows_of(north, padded), rows_of(south, padded)
-    begin(0, [above[k] for k in range(HALO)], [slope_north[k] for k in range(HALO)], HALO)
-    begin(HALO + height, [below[k] for k in range(HALO)], [slope_south[k] for k in range(HALO)], HALO)
+    above, below = rows_of(north, trim), rows_of(south, trim)
+    begin(0, [above[k] for k in range(HALO)], [slope_north[k] for k in range(HALO)])
+    begin(HALO + height, [below[k] for k in range(HALO)], [slope_south[k] for k in range(HALO)])
 
     def middle(n, _):
-        i = n * HALO
-        begin(i + HALO, [inner[i + k] for k in range(HALO)], [slope_inner[i + k] for k in range(HALO)], HALO)
+        i = n * G[5]
+        begin(i + HALO, [inner[i + k] for k in range(G[5])], [slope_inner[i + k] for k in range(G[5])])
         return 0
 
-    lax.fori_loop(0, height // HALO, middle, 0)
+    lax.fori_loop(0, height // G[5], middle, 0)
 
     def spread(i, ys):
         o = mxu(w_n[...], join([ga[pl.ds(i + k - 1, 3)].reshape(3 * hidden, wide) for k in range(len(ys))]))
         out = []
         for k, y in enumerate(ys):
             p = part(o, k)
-            out.append(y + p[padded : 2 * padded] + pltpu.roll(p[:padded], wide - 1, 1)
-                       + pltpu.roll(p[2 * padded :], 1, 1))
+            out.append(y + p[trim : 2 * trim] + pltpu.roll(p[:trim], wide - 1, 1)
+                       + pltpu.roll(p[2 * trim :], 1, 1))
         return out
 
     def tangent(i, vs):
@@ -293,8 +301,9 @@
         return [v + part(back, k) for k, v in enumerate(vs)]
 
     def gram_of(s):
-        s_hi = s.astype(BF)
-        s_lo = (s - s_hi.astype(F32)).astype(BF)
+        s_hi = s.astype(BF).astype(F32)
+        s_lo = fill(s - s_hi)
+        s_hi = fill(s_hi)
         return mxu(g3[...], jnp.concatenate([s_hi, s_hi, s_lo], axis=0))
 
     def loop(first, last, size, body):
@@ -309,7 +318,7 @@
     def n_first(i):
         for k, v in enumerate(spread(i, [field[i + k] for k in range(G[0])])):
             vec[i + k] = v
-            xb[i + k] = (v * is_in(i + k)).astype(BF)
+            xb[i + k] = fill(v * is_in(i + k))
 
     loop(1, ext - 1, G[0], n_first)
 
@@ -319,7 +328,7 @@
         ys = []
         for k, s in enumerate(ss):
             y = field[i + k][channels : channels + 1] * part(gs, k)
-            hi[i + k, :padded] = s[:, :breadth].astype(BF)
+            hi[i + k, :padded] = fill(s[:, :breadth])
             field[i + k] = y
             ys.append(y)
         pull(i, ys)
@@ -334,7 +343,7 @@
     def n_second(i):
         for k, v in enumerate(spread(i, [field[i + k] for k in range(G[2])])):
             vec[i + k] = v
-            xb[i + k] = (v * is_in(i + k)).astype(BF)
+            xb[i + k] = fill(v * is_in(i + k))
 
     loop(3, ext - 3, G[2], n_second)
 
@@ -342,7 +351,7 @@
         vs = [vec[i + k] for k in range(G[3])]
         for k, s in enumerate(tangent(i, vs)):
             second_out[i + k - HALO] = vs[k][:, :breadth]
-            hi[i + k, padded:] = s[:, :breadth].astype(BF)
+            hi[i + k, padded:] = fill(s[:, :breadth])
 
     loop(HALO, ext - HALO, G[3], m_second)
 
@@ -364,12 +373,12 @@
 
         loop(HALO, ext - HALO, G[4], gather)
 
-    row0, row1 = found[:padded], found[padded:]
+    row0, row1 = found[:trim], found[padded : padded + trim]
     weight = turn[channels : channels + 1]
     curved0 = gram_of(row0) * weight
     curved1 = gram_of(row1) * weight
-    real = lax.broadcasted_iota(jnp.int32, (padded, slots), 0) < channels
-    first = jnp.where(real, turn, 0.0)
+    real = lax.broadcasted_iota(jnp.int32, (trim, slots), 0) < channels
+    first = jnp.where(real, turn[:trim], 0.0)
 
     def total(x):
         return jnp.sum(jnp.sum(x, axis=0, keepdims=True), axis=1, keepdims=True)
@@ -380,7 +389,7 @@
     for number, value in enumerate(sums):
         for third, piece in enumerate(split3(value)):
             pieces = jnp.where(lane == channels + 3 + 3 * number + third, piece.astype(F32), pieces)
-    filler = jnp.zeros((LANES - padded, slots), F32)
+    filler = jnp.zeros((LANES - trim, slots), F32)
     turned0 = jnp.concatenate([row0, filler], axis=0).T
     turned1 = jnp.concatenate([row1, filler], axis=0).T
     leads = lax.broadcasted_iota(jnp.int32, (slots, LANES), 0)
@@ -444,7 +453,8 @@
     rows, radiances = departure_in.shape
     cap = max(2, 3 * rows // (2 * tiles))
     slots = tiles * cap
-    padded = -(-channels // 16) * 16
+    padded = -(-(channels + 1) // 16) * 16
+    trim = -(-(channels + 1) // 8) * 8
     wide = breadth + LANES
     ext = height + 2 * HALO
     strip = -(-(ext * SIDE) // LANES) * LANES
@@ -471,8 +481,8 @@
 
     w_m, w_n, p_t, p_j, g3 = call(
         weights_kernel,
-        (shape((3 * hidden, 3 * padded), BF), shape((3 * padded, 3 * hidden), BF), shape((hidden, padded), BF),
-         shape((padded, hidden), BF), shape((padded, 3 * padded), BF)),
+        (shape((3 * hidden, 3 * padded), BF), shape((3 * trim, 3 * hidden), BF), shape((hidden, padded), BF),
+         shape((trim, hidden), BF), shape((trim, 3 * padded), BF)),
         (conv_taps, projection, jacobian, weight),
         staged=True,
     )
@@ -483,7 +493,6 @@
     slope_west, slope_east = call(strip_kernel, (shape((hidden, strip), BF),) * 2,
                                   (slope_inner, slope_north, slope_south))
 
-    trim = -(-(channels + 1) // 8) * 8
     north, south = call(
         functools.partial(edge_kernel, channels, height),
         (shape((HALO * trim, breadth), BF),) * 2,
@@ -502,26 +511,26 @@
     )
     from_east = shift2(to_west, 0, -1)
     from_west = shift2(to_east, 0, 1)
-    inner = call(functools.partial(grid_kernel, channels), shape((height, padded, breadth)), (got,))
+    inner = call(functools.partial(grid_kernel, channels), shape((height, trim, breadth)), (got,))
 
     at = lax.axis_index("lat")
     flags = jnp.stack([at > 0, at < lax.axis_size("lat") - 1]).astype(jnp.int32)
     first, second, reply = call(
         functools.partial(main_kernel, channels, hidden, cap),
-        (shape((height, padded, breadth)),) * 2 + (shape((slots, 2 * LANES), BF),),
+        (shape((height, trim, breadth)),) * 2 + (shape((slots, 2 * LANES), BF),),
         (flags, got, inner, from_north, from_south, from_east, from_west, slope_inner, slope_north,
          slope_south, w_n, w_m, p_t, p_j, g3),
         scratch=[
-            pltpu.VMEM((ext, padded, wide), F32),
+            pltpu.VMEM((ext, trim, wide), F32),
             pltpu.VMEM((ext, hidden, wide), BF),
             pltpu.VMEM((ext, hidden, wide), BF),
             pltpu.VMEM((ext, padded, wide), BF),
-            pltpu.VMEM((ext, padded, wide), F32),
+            pltpu.VMEM((ext, trim, wide), F32),
             pltpu.VMEM((ext, 2 * padded, breadth), BF),
             pltpu.VMEM((2 * padded, slots), F32),
         ],
         smem=1,
-        vmem=64,
+        vmem=76,
     )
     back = swap(reply)
     return call(

time: 101 us -> 95.3 us (0.944)
  Pallas kernels: 44.6 us -> 38.6 us
    pallas_call x9, Pallas kernels: 44.6 us -> 38.6 us  [call(): pl.pallas_call(kernel, out_shape=outs, grid=(1,) if staged else (), in_sp...]
  transfers between devices with their start and end apart: 7 -> 7, of which waited for: 4 -> 4; matrix products, arithmetic and copies ran while one was open for 2% -> 2% of each run, Pallas kernels for 5% -> 6%
where the time goes in v5:
time: 95.3 us; the launch traced here: 94.8 us
  Pallas kernels  38.6 us (41%)
  starting transfers between devices  19.4 us (20%)
  blocking collectives  17.5 us (18%)
  waiting for transfers between devices  10.9 us (11%)
  local copies, waits for them, and re-layouts  6.72 us (7%)
  between operations  1.64 us (2%)
    pallas_call x9, Pallas kernels, call(): pl.pallas_call(kernel, out_shape=outs, grid=(1,) if staged else (), in_sp...  38.6 us
    all_to_all x1, blocking collectives, swap(): lax.all_to_all(x.reshape(tiles, cap, -1), ('lat', 'lon'), split_axis=0, c...  17.5 us
    ppermute x6, starting transfers between devices, shift2(): return lax.ppermute(x, ('lat', 'lon'), pairs)  12.1 us
    ppermute x6, waiting for transfers between devices, shift2(): return lax.ppermute(x, ('lat', 'lon'), pairs)  10.9 us
    all_to_all x1, starting transfers between devices, swap(): lax.all_to_all(x.reshape(tiles, cap, -1), ('lat', 'lon'), split_axis=0, c...  7.3 us
    unnamed x24, local copies, waits for them, and re-layouts  6.7 us
  transfers between devices with their start and end apart: 7, of which 4 were waited for; matrix products, arithmetic and copies ran while one was open for 2% of the time, Pallas kernels for 6%

profile of v5, /device:TPU:0, one launch (start us, length us, event | category | flops | bytes accessed | tf_op | source)
XLA Modules:
  0.0 94.8 jit_solution(9740961761651191252)
XLA Ops:
  0.6 0.0 copy-start.6
  1.3 0.0 copy-start
  1.3 1.0 %copy-done = f32[512,256]{1,0:T(8,128)S(1)} copy-done((f32[512,256]{1,0:T(8,128)S(1)}, f32[512,256]{1,0:T(8,128)}, u32[]{:S(2)}) %copy-start) | copy-done | bytes 524312
  2.3 0.0 copy-start.2
  2.3 0.9 copy-done.2
  3.2 0.0 copy-start.5
  3.2 0.7 copy-done.5
  3.9 0.0 copy-start.7
  3.9 0.7 copy-done.7
  4.6 0.0 copy-start.8
  4.6 0.7 copy-done.8
  5.3 0.0 copy-start.9
  5.3 0.7 copy-done.9
  6.0 0.0 copy-start.10
  6.0 0.0 copy-start.3
  6.0 0.0 copy-start.4
  6.0 1.8 %shard_map.113 = (bf16[768,128]{1,0:T(8,128)(2,1)}, s32[1,512]{1,0:T(1,128)S(1)}) custom-call(s32[1]{0:T(128)S(6)} %copy.16.count, f32[512,256]{1,0:T(8,128)S(1)} %copy-done, s32[1,512]{1,0:T(1,128)S(1)} %bitcast.24, s32[1,512]{1,0:T(1,128)S(1)} %bitcast.25, s32[1,512]{1,0:T(1,128)S(1)} %bitcast.26, f32[1,256]{1,0:T(1,128)S(1)} %bitcast.22, ...), custom_call_target="tpu_custom_call" | custom-call | tf_op jit(solution)/shard_map/pallas_call | solution.py:37
  7.8 7.3 %all-to-all-start = ((bf16[32,24,128]{2,1,0:T(8,128)(2,1)}), bf16[32,24,128]{2,1,0:T(8,128)(2,1)S(1)}, u32[]{:S(2)}, u32[]{:S(2)}) async-start(bf16[32,24,128]{2,1,0:T(8,128)(2,1)} %bitcast.6), calls=%async_computation | async-start | bytes 393216 | tf_op jit(solution)/shard_map/all_to_all | solution.py:477
  15.1 1.9 %copy.15 = bf16[64,48,256]{2,0,1:T(8,128)(2,1)S(1)} copy(bf16[64,48,256]{2,1,0:T(8,128)(2,1)} %param.19) | data formatting | bytes 3145728 | tf_op args[9]
  17.1 1.3 %collective-permute-start.1 = (bf16[4,64,256]{2,1,0:T(8,128)(2,1)S(1)}, bf16[4,64,256]{2,1,0:T(8,128)(2,1)S(1)}, u32[]{:S(2)}, u32[]{:S(2)}) collective-permute-start(bf16[4,64,256]{2,1,0:T(8,128)(2,1)S(1)} %get-tuple-element.38), channel_id=1, source_target_pairs={{4,0},{5,1},{6,2},{7,3},{8,4},{9,5},{10,6},{11,7},{12,8},{13,9},{1... | collective-permute-start | bytes 393224 | tf_op jit(solution)/shard_map/ppermute | solution.py:445
  18.4 4.6 %collective-permute-start = (bf16[4,64,256]{2,1,0:T(8,128)(2,1)S(1)}, bf16[4,64,256]{2,1,0:T(8,128)(2,1)S(1)}, u32[]{:S(2)}, u32[]{:S(2)}) collective-permute-start(bf16[4,64,256]{2,1,0:T(8,128)(2,1)S(1)} %get-tuple-element.39), channel_id=1, source_target_pairs={{0,4},{1,5},{2,6},{3,7},{4,8},{5,9},{6,10},{7,11},{8,12},{9,13},{1... | collective-permute-start | bytes 393224 | tf_op jit(solution)/shard_map/ppermute | solution.py:445
  22.9 2.2 %collective-permute-done.1._slope_south.south.slope_south = bf16[4,64,256]{2,1,0:T(8,128)(2,1)S(1)} collective-permute-done((bf16[4,64,256]{2,1,0:T(8,128)(2,1)S(1)}, bf16[4,64,256]{2,1,0:T(8,128)(2,1)S(1)}, u32[]{:S(2)}, u32[]{:S(2)}) %collective-permute-start.1) | collective-permute-done | bytes 131104 | tf_op jit(solution)/shard_map/ppermute | solution.py:445
  25.1 2.5 %collective-permute-done._slope_north.north.slope_north = bf16[4,64,256]{2,1,0:T(8,128)(2,1)S(1)} collective-permute-done((bf16[4,64,256]{2,1,0:T(8,128)(2,1)S(1)}, bf16[4,64,256]{2,1,0:T(8,128)(2,1)S(1)}, u32[]{:S(2)}, u32[]{:S(2)}) %collective-permute-start) | collective-permute-done | bytes 131104 | tf_op jit(solution)/shard_map/ppermute | solution.py:445
  27.6 0.0 all-to-all-done
  27.6 0.5 shard_map.115
  28.2 4.4 %collective-permute-start.2 = (bf16[288,256]{1,0:T(8,128)(2,1)S(1)}, bf16[288,256]{1,0:T(8,128)(2,1)S(1)}, u32[]{:S(2)}, u32[]{:S(2)}) collective-permute-start(bf16[288,256]{1,0:T(8,128)(2,1)S(1)} %get-tuple-element.21), channel_id=1, source_target_pairs={{0,4},{1,5},{2,6},{3,7},{4,8},{5,9},{6,10},{7,11},{8,12},{9,13},{1... | collective-permute-start | bytes 442376 | tf_op jit(solution)/shard_map/ppermute | solution.py:445
  32.6 1.3 %collective-permute-start.3 = (bf16[288,256]{1,0:T(8,128)(2,1)S(1)}, bf16[288,256]{1,0:T(8,128)(2,1)S(1)}, u32[]{:S(2)}, u32[]{:S(2)}) collective-permute-start(bf16[288,256]{1,0:T(8,128)(2,1)S(1)} %get-tuple-element.22), channel_id=1, source_target_pairs={{4,0},{5,1},{6,2},{7,3},{8,4},{9,5},{10,6},{11,7},{12,8},{13,9},{1... | collective-permute-start | bytes 442376 | tf_op jit(solution)/shard_map/ppermute | solution.py:445
  33.9 0.0 copy-done.10
  33.9 0.1 copy.13.projection
  34.0 0.0 copy-done.6
  34.0 0.0 copy-done.3
  34.0 0.0 copy-done.4
  34.0 0.9 shard_map.118
  34.9 0.6 shard_map.117
  35.5 1.0 %shard_map.116 = (bf16[80,512]{1,0:T(8,128)(2,1)S(1)}, bf16[80,512]{1,0:T(8,128)(2,1)S(1)}) custom-call(bf16[768,128]{1,0:T(8,128)(2,1)S(1)} %bitcast.17), custom_call_target="tpu_custom_call" | custom-call | tf_op jit(solution)/shard_map/pallas_call | solution.py:37
  36.5 0.0 collective-permute-done.2.from_north.north
  36.5 3.4 %collective-permute-done.3.from_south.south = bf16[288,256]{1,0:T(8,128)(2,1)S(1)} collective-permute-done((bf16[288,256]{1,0:T(8,128)(2,1)S(1)}, bf16[288,256]{1,0:T(8,128)(2,1)S(1)}, u32[]{:S(2)}, u32[]{:S(2)}) %collective-permute-start.3) | collective-permute-done | bytes 147488 | tf_op jit(solution)/shard_map/ppermute | solution.py:445
  40.0 0.2 shard_map.119
  40.1 0.1 collective-permute-start.4
  40.2 0.5 collective-permute-start.5
  40.7 0.1 add_convert_fusion.flags
  40.8 2.8 %shard_map.114.inner = f32[48,72,256]{2,1,0:T(8,128)S(1)} custom-call(bf16[768,128]{1,0:T(8,128)(2,1)S(1)} %bitcast.18), custom_call_target="tpu_custom_call" | custom-call | tf_op jit(solution)/shard_map/pallas_call | solution.py:37
  43.6 0.0 collective-permute-done.4.from_east
  43.6 2.7 %collective-permute-done.5.from_west = bf16[144,512]{1,0:T(8,128)(2,1)S(1)} collective-permute-done((bf16[144,512]{1,0:T(8,128)(2,1)S(1)}, bf16[144,512]{1,0:T(8,128)(2,1)S(1)}, u32[]{:S(2)}, u32[]{:S(2)}) %collective-permute-start.5) | collective-permute-done | bytes 147488 | tf_op jit(solution)/shard_map/ppermute | solution.py:445
  46.3 0.0 copy-start.1
  46.3 27.0 %shard_map.120 = (f32[48,72,256]{2,1,0:T(8,128)S(1)}, f32[48,72,256]{2,1,0:T(8,128)S(1)}, bf16[768,256]{1,0:T(8,128)(2,1)S(1)}) custom-call(s32[2]{0:T(128)S(1)} %add_convert_fusion.flags, bf16[768,128]{1,0:T(8,128)(2,1)S(1)} %bitcast.19, f32[48,72,256]{2,1,0:T(8,128)S(1)} %shard_map.114.inner, bf16[288,256]{1,0:T(8,128)(2,1)S(1)} %collective-permute-done.2.from_north.north, ...), custom_call_target="tpu_custom_call" | custom-call | tf_op jit(solution)/shard_map/pallas_call | solution.py:37
  73.4 17.5 %all_to_all.10 = bf16[32,24,256]{2,1,0:T(8,128)(2,1)S(1)} all-to-all(bf16[32,24,256]{2,1,0:T(8,128)(2,1)S(1)} %bitcast.21), channel_id=1, replica_groups=mesh['lat'=8,'lon'=4] {'lat','lon'}, dimensions={0} | all-to-all | bytes 786432 | tf_op jit(solution)/shard_map/all_to_all | solution.py:477
  90.8 0.0 copy-done.1
  90.8 3.8 %shard_map.121 = (f32[69,48,256]{2,1,0:T(8,128)}, f32[512,256]{1,0:T(8,128)}) custom-call(bf16[768,256]{1,0:T(8,128)(2,1)S(1)} %bitcast.20, s32[1,512]{1,0:T(1,128)S(1)} %get-tuple-element.35.slot, f32[512,256]{1,0:T(8,128)S(1)} %copy-done.1, f32[69,256]{1,0:T(8,128)S(1)} %copy-done.3, f32[48,72,256]{2,1,0:T(8,128)S(1)} %get-tuple-element.36.first, ...), custom_call_target="tpu_custom_call" | custom-call | tf_op jit(solution)/shard_map/pallas_call | solution.py:37
  (1 shorter events, 0.0 us)
Async XLA Ops:
  0.6 33.4 %copy-start.6 = (f32[256]{0:T(256)S(1)}, f32[256]{0:T(256)}, u32[]{:S(2)}) copy-start(f32[256]{0:T(256)} %param.15) | copy-start | bytes 3076
  1.3 1.0 %copy-start = (f32[512,256]{1,0:T(8,128)S(1)}, f32[512,256]{1,0:T(8,128)}, u32[]{:S(2)}) copy-start(f32[512,256]{1,0:T(8,128)} %dep.1) | copy-start | bytes 1572868
  2.3 0.9 copy-start.2
  3.2 0.7 copy-start.5
  3.9 0.7 copy-start.7
  4.6 0.7 copy-start.8
  5.3 0.7 copy-start.9
  6.0 27.9 %copy-start.10 = (bf16[69,64]{0,1:T(8,128)(2,1)S(1)}, bf16[69,64]{0,1:T(8,128)(2,1)}, u32[]{:S(2)}) copy-start(bf16[69,64]{0,1:T(8,128)(2,1)} %param.18) | copy-start | bytes 26500
  6.0 28.0 %copy-start.3 = (f32[69,256]{1,0:T(8,128)S(1)}, f32[69,256]{1,0:T(8,128)}, u32[]{:S(2)}) copy-start(f32[69,256]{1,0:T(8,128)} %jac.3) | copy-start | bytes 211972
  6.0 28.0 %copy-start.4 = (bf16[9,64,69]{2,1,0:T(8,128)(2,1)S(1)}, bf16[9,64,69]{2,1,0:T(8,128)(2,1)}, u32[]{:S(2)}) copy-start(bf16[9,64,69]{2,1,0:T(8,128)(2,1)} %taps.1) | copy-start | bytes 238468
  7.8 19.8 %all-to-all-start = ((bf16[32,24,128]{2,1,0:T(8,128)(2,1)}), bf16[32,24,128]{2,1,0:T(8,128)(2,1)S(1)}, u32[]{:S(2)}, u32[]{:S(2)}) async-start(bf16[32,24,128]{2,1,0:T(8,128)(2,1)} %bitcast.6), calls=%async_computation | async-start | bytes 393216 | tf_op jit(solution)/shard_map/all_to_all | solution.py:477
  17.1 8.1 %collective-permute-start.1 = (bf16[4,64,256]{2,1,0:T(8,128)(2,1)S(1)}, bf16[4,64,256]{2,1,0:T(8,128)(2,1)S(1)}, u32[]{:S(2)}, u32[]{:S(2)}) collective-permute-start(bf16[4,64,256]{2,1,0:T(8,128)(2,1)S(1)} %get-tuple-element.38), channel_id=1, source_target_pairs={{4,0},{5,1},{6,2},{7,3},{8,4},{9,5},{10,6},{11,7},{12,8},{13,9},{1... | collective-permute-start | bytes 393224 | tf_op jit(solution)/shard_map/ppermute | solution.py:445
  18.4 9.2 %collective-permute-start = (bf16[4,64,256]{2,1,0:T(8,128)(2,1)S(1)}, bf16[4,64,256]{2,1,0:T(8,128)(2,1)S(1)}, u32[]{:S(2)}, u32[]{:S(2)}) collective-permute-start(bf16[4,64,256]{2,1,0:T(8,128)(2,1)S(1)} %get-tuple-element.39), channel_id=1, source_target_pairs={{0,4},{1,5},{2,6},{3,7},{4,8},{5,9},{6,10},{7,11},{8,12},{9,13},{1... | collective-permute-start | bytes 393224 | tf_op jit(solution)/shard_map/ppermute | solution.py:445
  28.2 8.4 %collective-permute-start.2 = (bf16[288,256]{1,0:T(8,128)(2,1)S(1)}, bf16[288,256]{1,0:T(8,128)(2,1)S(1)}, u32[]{:S(2)}, u32[]{:S(2)}) collective-permute-start(bf16[288,256]{1,0:T(8,128)(2,1)S(1)} %get-tuple-element.21), channel_id=1, source_target_pairs={{0,4},{1,5},{2,6},{3,7},{4,8},{5,9},{6,10},{7,11},{8,12},{9,13},{1... | collective-permute-start | bytes 442376 | tf_op jit(solution)/shard_map/ppermute | solution.py:445
  32.6 7.4 %collective-permute-start.3 = (bf16[288,256]{1,0:T(8,128)(2,1)S(1)}, bf16[288,256]{1,0:T(8,128)(2,1)S(1)}, u32[]{:S(2)}, u32[]{:S(2)}) collective-permute-start(bf16[288,256]{1,0:T(8,128)(2,1)S(1)} %get-tuple-element.22), channel_id=1, source_target_pairs={{4,0},{5,1},{6,2},{7,3},{8,4},{9,5},{10,6},{11,7},{12,8},{13,9},{1... | collective-permute-start | bytes 442376 | tf_op jit(solution)/shard_map/ppermute | solution.py:445
  40.1 3.4 %collective-permute-start.4 = (bf16[144,512]{1,0:T(8,128)(2,1)S(1)}, bf16[144,512]{1,0:T(8,128)(2,1)S(1)}, u32[]{:S(2)}, u32[]{:S(2)}) collective-permute-start(bf16[144,512]{1,0:T(8,128)(2,1)S(1)} %get-tuple-element.28), channel_id=1, source_target_pairs={{0,3},{1,0},{2,1},{3,2},{4,7},{5,4},{6,5},{7,6},{8,11},{9,8},{10,9... | collective-permute-start | bytes 442376 | tf_op jit(solution)/shard_map/ppermute | solution.py:445
  40.2 6.1 %collective-permute-start.5 = (bf16[144,512]{1,0:T(8,128)(2,1)S(1)}, bf16[144,512]{1,0:T(8,128)(2,1)S(1)}, u32[]{:S(2)}, u32[]{:S(2)}) collective-permute-start(bf16[144,512]{1,0:T(8,128)(2,1)S(1)} %get-tuple-element.29), channel_id=1, source_target_pairs={{0,1},{1,2},{2,3},{3,0},{4,5},{5,6},{6,7},{7,4},{8,9},{9,10},{10,1... | collective-permute-start | bytes 442376 | tf_op jit(solution)/shard_map/ppermute | solution.py:445
  46.3 44.5 %copy-start.1 = (f32[512,256]{1,0:T(8,128)S(1)}, f32[512,256]{1,0:T(8,128)}, u32[]{:S(2)}) copy-start(f32[512,256]{1,0:T(8,128)} %dep.1) | copy-start | bytes 1572868

commit v6 on v5

--- a/solution.py
+++ b/solution.py
@@ -27,7 +27,7 @@
         if i < smem:
             return pl.BlockSpec(memory_space=pltpu.SMEM)
         if i >= len(args) - unread:
-            return pl.BlockSpec(memory_space=pltpu.HBM if scratch else pl.ANY)
+            return pl.BlockSpec(memory_space=pl.ANY)
         if staged:
             return pl.BlockSpec(x.shape, lambda _: (0,) * x.ndim)
         return pl.BlockSpec(memory_space=pltpu.VMEM)
@@ -53,30 +53,25 @@
     return hi, mid, (rest - mid.astype(F32)).astype(BF)
 
 
-def pack_kernel(tiles, cap, lon_size, channels, count, *refs):
-    sources, (send, slot_out), held, sems = refs[:6], refs[6:8], refs[8:14], refs[14]
-    copies = [pltpu.make_async_copy(src, dst, sems.at[k]) for k, (src, dst) in enumerate(zip(sources, held))]
-    for copy in copies:
-        copy.start()
-    for copy in copies:
-        copy.wait()
-    dep, owner_row, cell_row, qc_row, weight, jac = held
+def pack_kernel(tiles, cap, lon_size, channels, count, dep, meta, tables, send, slot_out):
+    owner_row, cell_row, qc_row = meta[0:1], meta[1:2], meta[2:3]
+    jac, weight = tables[:channels], tables[channels : channels + 1]
     rows = dep.shape[0]
     slots = send.shape[0]
-    hit = (lax.broadcasted_iota(jnp.int32, (tiles, rows), 0) == owner_row[...]).astype(BF)
+    hit = (lax.broadcasted_iota(jnp.int32, (tiles, rows), 0) == owner_row).astype(BF)
     before = (lax.broadcasted_iota(jnp.int32, (rows, rows), 0)
               < lax.broadcasted_iota(jnp.int32, (rows, rows), 1)).astype(BF)
     earlier = mxu(hit, before)
     rank = jnp.sum(earlier * hit.astype(F32), axis=0, keepdims=True)
-    slot = owner_row[...] * cap + rank.astype(jnp.int32)
+    slot = owner_row * cap + rank.astype(jnp.int32)
     slot_out[...] = slot
     place = (lax.broadcasted_iota(jnp.int32, (slots, rows), 0) == slot).astype(BF)
 
     used = (lax.broadcasted_iota(jnp.int32, (1, rows), 1) < count[0]).astype(F32)
-    row_weight = used * qc_row[...].astype(F32)
-    terms = mxu(jac[...], dep[...] * weight[...], ((1,), (1,)), lax.Precision.HIGHEST) * row_weight
-    lat = cell_row[...] // lon_size
-    lon = cell_row[...] - lat * lon_size
+    row_weight = used * qc_row.astype(F32)
+    terms = mxu(jac, dep[...] * weight, ((1,), (1,)), lax.Precision.HIGHEST) * row_weight
+    lat = cell_row // lon_size
+    lon = cell_row - lat * lon_size
     wide = lax.broadcasted_iota(jnp.int32, (LANES, rows), 0)
     terms = jnp.concatenate([terms, jnp.zeros((LANES - channels, rows), F32)], axis=0)
     terms = jnp.where(wide == channels, row_weight, terms)
@@ -107,12 +102,14 @@
     p_t[...] = mxu(projection[...], wider, ((0,), (0,))).astype(BF)
     tall = jnp.concatenate([jac[...], jnp.zeros((padded - channels, jac.shape[1]), F32)], axis=0)
     gram = mxu(tall * weight[...], tall, ((1,), (1,)), lax.Precision.HIGHEST)
-    hi = gram.astype(BF)
-    lo = (gram - hi.astype(F32)).astype(BF)
+    pulled = mxu(p_t[...].astype(F32), gram, precision=lax.Precision.HIGHEST)
+    both = jnp.concatenate([gram[:trim], pulled], axis=0)
+    hi = both.astype(BF)
+    lo = (both - hi.astype(F32)).astype(BF)
     total = 0.0
     for k, value in enumerate((hi, lo, hi)):
         total = total + mxu(value, shifted(padded, 3 * padded, k * padded))
-    g3[...] = total[:trim].astype(BF)
+    g3[...] = total.astype(BF)
 
 
 def turned(got, channels, padded):
@@ -300,11 +297,11 @@
         back = mxu(p_j[...], join(acts))
         return [v + part(back, k) for k, v in enumerate(vs)]
 
-    def gram_of(s):
+    def gram_of(s, matrix):
         s_hi = s.astype(BF).astype(F32)
         s_lo = fill(s - s_hi)
         s_hi = fill(s_hi)
-        return mxu(g3[...], jnp.concatenate([s_hi, s_hi, s_lo], axis=0))
+        return mxu(matrix, jnp.concatenate([s_hi, s_hi, s_lo], axis=0))
 
     def loop(first, last, size, body):
         assert (last - first) % size == 0
@@ -324,14 +321,13 @@
 
     def m_first(i):
         ss = tangent(i, [vec[i + k] for k in range(G[1])])
-        gs = gram_of(join(ss))
-        ys = []
+        gs = gram_of(join(ss), g3[...])
         for k, s in enumerate(ss):
-            y = field[i + k][channels : channels + 1] * part(gs, k)
+            cell_weight = field[i + k][channels : channels + 1]
+            both = part(gs, k)
             hi[i + k, :padded] = fill(s[:, :breadth])
-            field[i + k] = y
-            ys.append(y)
-        pull(i, ys)
+            field[i + k] = cell_weight * both[:trim]
+            ga[i + k] = (slope[i + k].astype(F32) * (cell_weight * both[trim:])).astype(BF)
 
     loop(2, ext - 2, G[1], m_first)
 
@@ -375,8 +371,8 @@
 
     row0, row1 = found[:trim], found[padded : padded + trim]
     weight = turn[channels : channels + 1]
-    curved0 = gram_of(row0) * weight
-    curved1 = gram_of(row1) * weight
+    curved0 = gram_of(row0, g3[:trim]) * weight
+    curved1 = gram_of(row1, g3[:trim]) * weight
     real = lax.broadcasted_iota(jnp.int32, (trim, slots), 0) < channels
     first = jnp.where(real, turn[:trim], 0.0)
 
@@ -463,14 +459,12 @@
         return jax.ShapeDtypeStruct(dims, kind)
 
     weight = channel_weight[None, :]
-    inputs = (departure_in, obs_owner.reshape(1, rows), obs_cell[None, :], qc_mask[None, :], weight, jacobian)
     send, slot = call(
         functools.partial(pack_kernel, tiles, cap, breadth, channels),
         (shape((slots, LANES), BF), shape((1, rows), jnp.int32)),
-        (obs_count,) + inputs,
-        scratch=[pltpu.VMEM(x.shape, x.dtype) for x in inputs] + [pltpu.SemaphoreType.DMA((len(inputs),))],
+        (obs_count, departure_in, jnp.stack([obs_owner[:, 0], obs_cell, qc_mask]),
+         jnp.concatenate([jacobian, weight], axis=0)),
         smem=1,
-        unread=len(inputs),
     )
 
     def swap(x):
@@ -482,7 +476,7 @@
     w_m, w_n, p_t, p_j, g3 = call(
         weights_kernel,
         (shape((3 * hidden, 3 * padded), BF), shape((3 * trim, 3 * hidden), BF), shape((hidden, padded), BF),
-         shape((trim, hidden), BF), shape((trim, 3 * padded), BF)),
+         shape((trim, hidden), BF), shape((trim + hidden, 3 * padded), BF)),
         (conv_taps, projection, jacobian, weight),
         staged=True,
     )

time: 95.3 us -> 92.9 us (0.975)
  local copies, waits for them, and re-layouts: 6.72 us -> 3.12 us
  other arithmetic: 0.07 us -> 1.71 us
    unnamed x24 -> x14, local copies, waits for them, and re-layouts: 6.7 us -> 3.1 us
where the time goes in v6:
time: 92.9 us; the launch traced here: 92.4 us
  Pallas kernels  38.4 us (41%)
  starting transfers between devices  19.4 us (21%)
  blocking collectives  17.5 us (19%)
  waiting for transfers between devices  10.7 us (12%)
  local copies, waits for them, and re-layouts  3.12 us (3%)
  other arithmetic  1.71 us (2%)
  between operations  1.68 us (2%)
    pallas_call x9, Pallas kernels, call(): pl.pallas_call(kernel, out_shape=outs, grid=(1,) if staged else (), in_sp...  38.4 us
    all_to_all x1, blocking collectives, swap(): lax.all_to_all(x.reshape(tiles, cap, -1), ('lat', 'lon'), split_axis=0, c...  17.5 us
    ppermute x6, starting transfers between devices, shift2(): return lax.ppermute(x, ('lat', 'lon'), pairs)  12.1 us
    ppermute x6, waiting for transfers between devices, shift2(): return lax.ppermute(x, ('lat', 'lon'), pairs)  10.7 us
    all_to_all x1, starting transfers between devices, swap(): lax.all_to_all(x.reshape(tiles, cap, -1), ('lat', 'lon'), split_axis=0, c...  7.3 us
    unnamed x14, local copies, waits for them, and re-layouts  3.1 us
  transfers between devices with their start and end apart: 7, of which 4 were waited for; matrix products, arithmetic and copies ran while one was open for 2% of the time, Pallas kernels for 6%

profile of v6, /device:TPU:0, one launch (start us, length us, event | category | flops | bytes accessed | tf_op | source)
XLA Modules:
  0.0 92.4 jit_solution(5692944277073337812)
XLA Ops:
  0.6 0.0 copy-start.2
  0.6 0.0 copy-start.4
  0.7 0.0 copy-start.5
  1.4 0.9 pad_maximum_fusion.tables
  2.3 0.7 pad_add_fusion.meta
  3.0 0.0 copy-start
  3.0 1.0 %copy-done = f32[512,256]{1,0:T(8,128)S(1)} copy-done((f32[512,256]{1,0:T(8,128)S(1)}, f32[512,256]{1,0:T(8,128)}, u32[]{:S(2)}) %copy-start) | copy-done | bytes 524312
  4.0 0.0 copy-start.3
  4.0 1.6 %shard_map.113 = (bf16[768,128]{1,0:T(8,128)(2,1)}, s32[1,512]{1,0:T(1,128)S(1)}) custom-call(s32[1]{0:T(128)S(6)} %copy.16.count, f32[512,256]{1,0:T(8,128)S(1)} %copy-done, s32[3,512]{1,0:T(4,128)S(1)} %pad_add_fusion.meta, f32[70,256]{1,0:T(8,128)S(1)} %pad_maximum_fusion.tables), custom_call_target="tpu_custom_call" | custom-call | tf_op jit(solution)/shard_map/pallas_call | solution.py:37
  5.7 7.3 %all-to-all-start = ((bf16[32,24,128]{2,1,0:T(8,128)(2,1)}), bf16[32,24,128]{2,1,0:T(8,128)(2,1)S(1)}, u32[]{:S(2)}, u32[]{:S(2)}) async-start(bf16[32,24,128]{2,1,0:T(8,128)(2,1)} %bitcast.6), calls=%async_computation | async-start | bytes 393216 | tf_op jit(solution)/shard_map/all_to_all | solution.py:471
  13.0 1.9 %copy.15 = bf16[64,48,256]{2,0,1:T(8,128)(2,1)S(1)} copy(bf16[64,48,256]{2,1,0:T(8,128)(2,1)} %param.19) | data formatting | bytes 3145728 | tf_op args[9]
  15.0 1.3 %collective-permute-start.1 = (bf16[4,64,256]{2,1,0:T(8,128)(2,1)S(1)}, bf16[4,64,256]{2,1,0:T(8,128)(2,1)S(1)}, u32[]{:S(2)}, u32[]{:S(2)}) collective-permute-start(bf16[4,64,256]{2,1,0:T(8,128)(2,1)S(1)} %get-tuple-element.38), channel_id=1, source_target_pairs={{4,0},{5,1},{6,2},{7,3},{8,4},{9,5},{10,6},{11,7},{12,8},{13,9},{1... | collective-permute-start | bytes 393224 | tf_op jit(solution)/shard_map/ppermute | solution.py:441
  16.3 4.6 %collective-permute-start = (bf16[4,64,256]{2,1,0:T(8,128)(2,1)S(1)}, bf16[4,64,256]{2,1,0:T(8,128)(2,1)S(1)}, u32[]{:S(2)}, u32[]{:S(2)}) collective-permute-start(bf16[4,64,256]{2,1,0:T(8,128)(2,1)S(1)} %get-tuple-element.39), channel_id=1, source_target_pairs={{0,4},{1,5},{2,6},{3,7},{4,8},{5,9},{6,10},{7,11},{8,12},{9,13},{1... | collective-permute-start | bytes 393224 | tf_op jit(solution)/shard_map/ppermute | solution.py:441
  20.8 2.2 %collective-permute-done.1._slope_south.south.slope_south = bf16[4,64,256]{2,1,0:T(8,128)(2,1)S(1)} collective-permute-done((bf16[4,64,256]{2,1,0:T(8,128)(2,1)S(1)}, bf16[4,64,256]{2,1,0:T(8,128)(2,1)S(1)}, u32[]{:S(2)}, u32[]{:S(2)}) %collective-permute-start.1) | collective-permute-done | bytes 131104 | tf_op jit(solution)/shard_map/ppermute | solution.py:441
  23.0 2.5 %collective-permute-done._slope_north.north.slope_north = bf16[4,64,256]{2,1,0:T(8,128)(2,1)S(1)} collective-permute-done((bf16[4,64,256]{2,1,0:T(8,128)(2,1)S(1)}, bf16[4,64,256]{2,1,0:T(8,128)(2,1)S(1)}, u32[]{:S(2)}, u32[]{:S(2)}) %collective-permute-start) | collective-permute-done | bytes 131104 | tf_op jit(solution)/shard_map/ppermute | solution.py:441
  25.5 0.0 all-to-all-done
  25.5 0.5 shard_map.115
  26.0 4.4 %collective-permute-start.2 = (bf16[288,256]{1,0:T(8,128)(2,1)S(1)}, bf16[288,256]{1,0:T(8,128)(2,1)S(1)}, u32[]{:S(2)}, u32[]{:S(2)}) collective-permute-start(bf16[288,256]{1,0:T(8,128)(2,1)S(1)} %get-tuple-element.21), channel_id=1, source_target_pairs={{0,4},{1,5},{2,6},{3,7},{4,8},{5,9},{6,10},{7,11},{8,12},{9,13},{1... | collective-permute-start | bytes 442376 | tf_op jit(solution)/shard_map/ppermute | solution.py:441
  30.4 1.3 %collective-permute-start.3 = (bf16[288,256]{1,0:T(8,128)(2,1)S(1)}, bf16[288,256]{1,0:T(8,128)(2,1)S(1)}, u32[]{:S(2)}, u32[]{:S(2)}) collective-permute-start(bf16[288,256]{1,0:T(8,128)(2,1)S(1)} %get-tuple-element.22), channel_id=1, source_target_pairs={{4,0},{5,1},{6,2},{7,3},{8,4},{9,5},{10,6},{11,7},{12,8},{13,9},{1... | collective-permute-start | bytes 442376 | tf_op jit(solution)/shard_map/ppermute | solution.py:441
  31.7 0.0 copy-done.5
  31.8 0.1 copy.13.projection
  31.9 0.0 copy-done.2
  31.9 0.0 copy-done.4
  31.9 0.0 copy-done.3
  31.9 1.1 %shard_map.118 = (bf16[192,240]{1,0:T(8,128)(2,1)S(1)}, bf16[216,192]{1,0:T(8,128)(2,1)S(1)}, bf16[64,80]{1,0:T(8,128)(2,1)S(1)}, bf16[72,64]{1,0:T(8,128)(2,1)S(1)}, bf16[136,240]{1,0:T(8,128)(2,1)S(1)}) custom-call(bf16[9,64,69]{2,1,0:T(8,128)(2,1)S(1)} %copy-done.3, bf16[69,64]{1,0:T(8,128)(2,1)S(1)} %copy.13.projection, f32[69,256]{1,0:T(8,128)S(1)} %copy-done.2, ...), custom_call_target="tpu_custom_call" | custom-call | tf_op jit(solution)/shard_map/pallas_call | solution.py:37
  33.0 0.6 shard_map.117
  33.6 1.0 %shard_map.116 = (bf16[80,512]{1,0:T(8,128)(2,1)S(1)}, bf16[80,512]{1,0:T(8,128)(2,1)S(1)}) custom-call(bf16[768,128]{1,0:T(8,128)(2,1)S(1)} %bitcast.17), custom_call_target="tpu_custom_call" | custom-call | tf_op jit(solution)/shard_map/pallas_call | solution.py:37
  34.6 0.0 collective-permute-done.2.from_north.north
  34.6 3.2 %collective-permute-done.3.from_south.south = bf16[288,256]{1,0:T(8,128)(2,1)S(1)} collective-permute-done((bf16[288,256]{1,0:T(8,128)(2,1)S(1)}, bf16[288,256]{1,0:T(8,128)(2,1)S(1)}, u32[]{:S(2)}, u32[]{:S(2)}) %collective-permute-start.3) | collective-permute-done | bytes 147488 | tf_op jit(solution)/shard_map/ppermute | solution.py:441
  37.8 0.2 shard_map.119
  38.0 0.1 collective-permute-start.4
  38.1 0.5 collective-permute-start.5
  38.6 0.1 add_convert_fusion.flags
  38.6 2.8 %shard_map.114.inner = f32[48,72,256]{2,1,0:T(8,128)S(1)} custom-call(bf16[768,128]{1,0:T(8,128)(2,1)S(1)} %bitcast.18), custom_call_target="tpu_custom_call" | custom-call | tf_op jit(solution)/shard_map/pallas_call | solution.py:37
  41.4 0.0 collective-permute-done.4.from_east
  41.5 2.7 %collective-permute-done.5.from_west = bf16[144,512]{1,0:T(8,128)(2,1)S(1)} collective-permute-done((bf16[144,512]{1,0:T(8,128)(2,1)S(1)}, bf16[144,512]{1,0:T(8,128)(2,1)S(1)}, u32[]{:S(2)}, u32[]{:S(2)}) %collective-permute-start.5) | collective-permute-done | bytes 147488 | tf_op jit(solution)/shard_map/ppermute | solution.py:441
  44.2 0.0 copy-start.1
  44.2 26.8 %shard_map.120 = (f32[48,72,256]{2,1,0:T(8,128)S(1)}, f32[48,72,256]{2,1,0:T(8,128)S(1)}, bf16[768,256]{1,0:T(8,128)(2,1)S(1)}) custom-call(s32[2]{0:T(128)S(1)} %add_convert_fusion.flags, bf16[768,128]{1,0:T(8,128)(2,1)S(1)} %bitcast.19, f32[48,72,256]{2,1,0:T(8,128)S(1)} %shard_map.114.inner, bf16[288,256]{1,0:T(8,128)(2,1)S(1)} %collective-permute-done.2.from_north.north, ...), custom_call_target="tpu_custom_call" | custom-call | tf_op jit(solution)/shard_map/pallas_call | solution.py:37
  71.0 17.5 %all_to_all.10 = bf16[32,24,256]{2,1,0:T(8,128)(2,1)S(1)} all-to-all(bf16[32,24,256]{2,1,0:T(8,128)(2,1)S(1)} %bitcast.21), channel_id=1, replica_groups=mesh['lat'=8,'lon'=4] {'lat','lon'}, dimensions={0} | all-to-all | bytes 786432 | tf_op jit(solution)/shard_map/all_to_all | solution.py:471
  88.5 0.0 copy-done.1
  88.5 3.8 %shard_map.121 = (f32[69,48,256]{2,1,0:T(8,128)}, f32[512,256]{1,0:T(8,128)}) custom-call(bf16[768,256]{1,0:T(8,128)(2,1)S(1)} %bitcast.20, s32[1,512]{1,0:T(1,128)S(1)} %get-tuple-element.35.slot, f32[512,256]{1,0:T(8,128)S(1)} %copy-done.1, f32[69,256]{1,0:T(8,128)S(1)} %copy-done.2, f32[48,72,256]{2,1,0:T(8,128)S(1)} %get-tuple-element.36.first, ...), custom_call_target="tpu_custom_call" | custom-call | tf_op jit(solution)/shard_map/pallas_call | solution.py:37
  (1 shorter events, 0.0 us)
Async XLA Ops:
  0.6 31.2 %copy-start.2 = (f32[69,256]{1,0:T(8,128)S(1)}, f32[69,256]{1,0:T(8,128)}, u32[]{:S(2)}) copy-start(f32[69,256]{1,0:T(8,128)} %jac.3) | copy-start | bytes 211972
  0.6 31.2 %copy-start.4 = (f32[256]{0:T(256)S(1)}, f32[256]{0:T(256)}, u32[]{:S(2)}) copy-start(f32[256]{0:T(256)} %param.15) | copy-start | bytes 3076
  0.7 31.1 %copy-start.5 = (bf16[69,64]{0,1:T(8,128)(2,1)S(1)}, bf16[69,64]{0,1:T(8,128)(2,1)}, u32[]{:S(2)}) copy-start(bf16[69,64]{0,1:T(8,128)(2,1)} %param.18) | copy-start | bytes 26500
  3.0 1.0 %copy-start = (f32[512,256]{1,0:T(8,128)S(1)}, f32[512,256]{1,0:T(8,128)}, u32[]{:S(2)}) copy-start(f32[512,256]{1,0:T(8,128)} %dep.3) | copy-start | bytes 1572868
  4.0 27.8 %copy-start.3 = (bf16[9,64,69]{2,1,0:T(8,128)(2,1)S(1)}, bf16[9,64,69]{2,1,0:T(8,128)(2,1)}, u32[]{:S(2)}) copy-start(bf16[9,64,69]{2,1,0:T(8,128)(2,1)} %taps.1) | copy-start | bytes 238468
  5.7 19.8 %all-to-all-start = ((bf16[32,24,128]{2,1,0:T(8,128)(2,1)}), bf16[32,24,128]{2,1,0:T(8,128)(2,1)S(1)}, u32[]{:S(2)}, u32[]{:S(2)}) async-start(bf16[32,24,128]{2,1,0:T(8,128)(2,1)} %bitcast.6), calls=%async_computation | async-start | bytes 393216 | tf_op jit(solution)/shard_map/all_to_all | solution.py:471
  15.0 8.1 %collective-permute-start.1 = (bf16[4,64,256]{2,1,0:T(8,128)(2,1)S(1)}, bf16[4,64,256]{2,1,0:T(8,128)(2,1)S(1)}, u32[]{:S(2)}, u32[]{:S(2)}) collective-permute-start(bf16[4,64,256]{2,1,0:T(8,128)(2,1)S(1)} %get-tuple-element.38), channel_id=1, source_target_pairs={{4,0},{5,1},{6,2},{7,3},{8,4},{9,5},{10,6},{11,7},{12,8},{13,9},{1... | collective-permute-start | bytes 393224 | tf_op jit(solution)/shard_map/ppermute | solution.py:441
  16.3 9.2 %collective-permute-start = (bf16[4,64,256]{2,1,0:T(8,128)(2,1)S(1)}, bf16[4,64,256]{2,1,0:T(8,128)(2,1)S(1)}, u32[]{:S(2)}, u32[]{:S(2)}) collective-permute-start(bf16[4,64,256]{2,1,0:T(8,128)(2,1)S(1)} %get-tuple-element.39), channel_id=1, source_target_pairs={{0,4},{1,5},{2,6},{3,7},{4,8},{5,9},{6,10},{7,11},{8,12},{9,13},{1... | collective-permute-start | bytes 393224 | tf_op jit(solution)/shard_map/ppermute | solution.py:441
  26.0 8.5 %collective-permute-start.2 = (bf16[288,256]{1,0:T(8,128)(2,1)S(1)}, bf16[288,256]{1,0:T(8,128)(2,1)S(1)}, u32[]{:S(2)}, u32[]{:S(2)}) collective-permute-start(bf16[288,256]{1,0:T(8,128)(2,1)S(1)} %get-tuple-element.21), channel_id=1, source_target_pairs={{0,4},{1,5},{2,6},{3,7},{4,8},{5,9},{6,10},{7,11},{8,12},{9,13},{1... | collective-permute-start | bytes 442376 | tf_op jit(solution)/shard_map/ppermute | solution.py:441
  30.4 7.4 %collective-permute-start.3 = (bf16[288,256]{1,0:T(8,128)(2,1)S(1)}, bf16[288,256]{1,0:T(8,128)(2,1)S(1)}, u32[]{:S(2)}, u32[]{:S(2)}) collective-permute-start(bf16[288,256]{1,0:T(8,128)(2,1)S(1)} %get-tuple-element.22), channel_id=1, source_target_pairs={{4,0},{5,1},{6,2},{7,3},{8,4},{9,5},{10,6},{11,7},{12,8},{13,9},{1... | collective-permute-start | bytes 442376 | tf_op jit(solution)/shard_map/ppermute | solution.py:441
  38.0 3.4 %collective-permute-start.4 = (bf16[144,512]{1,0:T(8,128)(2,1)S(1)}, bf16[144,512]{1,0:T(8,128)(2,1)S(1)}, u32[]{:S(2)}, u32[]{:S(2)}) collective-permute-start(bf16[144,512]{1,0:T(8,128)(2,1)S(1)} %get-tuple-element.28), channel_id=1, source_target_pairs={{0,3},{1,0},{2,1},{3,2},{4,7},{5,4},{6,5},{7,6},{8,11},{9,8},{10,9... | collective-permute-start | bytes 442376 | tf_op jit(solution)/shard_map/ppermute | solution.py:441
  38.1 6.1 %collective-permute-start.5 = (bf16[144,512]{1,0:T(8,128)(2,1)S(1)}, bf16[144,512]{1,0:T(8,128)(2,1)S(1)}, u32[]{:S(2)}, u32[]{:S(2)}) collective-permute-start(bf16[144,512]{1,0:T(8,128)(2,1)S(1)} %get-tuple-element.29), channel_id=1, source_target_pairs={{0,1},{1,2},{2,3},{3,0},{4,5},{5,6},{6,7},{7,4},{8,9},{9,10},{10,1... | collective-permute-start | bytes 442376 | tf_op jit(solution)/shard_map/ppermute | solution.py:441
  44.2 44.3 %copy-start.1 = (f32[512,256]{1,0:T(8,128)S(1)}, f32[512,256]{1,0:T(8,128)}, u32[]{:S(2)}) copy-start(f32[512,256]{1,0:T(8,128)} %dep.3) | copy-start | bytes 1572868

commit v7 on v6

--- a/solution.py
+++ b/solution.py
@@ -238,8 +238,8 @@
     def join(parts):
         return jnp.concatenate(parts, axis=1)
 
-    def part(x, k):
-        return x[:, k * wide : (k + 1) * wide]
+    def part(x, k, lanes=wide):
+        return x[:, k * lanes : (k + 1) * lanes]
 
     def fill(x):
         return jnp.concatenate([x, jnp.zeros((padded - trim, x.shape[1]), F32)], axis=0).astype(BF)
@@ -287,15 +287,16 @@
         return out
 
     def tangent(i, vs):
+        lanes = vs[0].shape[1]
         o = mxu(w_m[...], join([xb[pl.ds(i + k - 1, 3)].reshape(3 * padded, wide) for k in range(len(vs))]))
         acts = []
         for k in range(len(vs)):
             p = part(o, k)
             h = (p[hidden : 2 * hidden] + pltpu.roll(p[:hidden], 1, 1)
                  + pltpu.roll(p[2 * hidden :], wide - 1, 1))
-            acts.append((slope[i + k].astype(F32) * h).astype(BF))
+            acts.append((slope[i + k].astype(F32) * h).astype(BF)[:, :lanes])
         back = mxu(p_j[...], join(acts))
-        return [v + part(back, k) for k, v in enumerate(vs)]
+        return [v + part(back, k, lanes) for k, v in enumerate(vs)]
 
     def gram_of(s, matrix):
         s_hi = s.astype(BF).astype(F32)
@@ -314,13 +315,14 @@
 
     def n_first(i):
         for k, v in enumerate(spread(i, [field[i + k] for k in range(G[0])])):
-            vec[i + k] = v
+            first_out[i + k] = v[:, :breadth]
+            vec[i + k] = v[:, breadth:]
             xb[i + k] = fill(v * is_in(i + k))
 
     loop(1, ext - 1, G[0], n_first)
 
     def m_first(i):
-        ss = tangent(i, [vec[i + k] for k in range(G[1])])
+        ss = tangent(i, [join([first_out[i + k], vec[i + k]]) for k in range(G[1])])
         gs = gram_of(join(ss), g3[...])
         for k, s in enumerate(ss):
             cell_weight = field[i + k][channels : channels + 1]
@@ -331,23 +333,16 @@
 
     loop(2, ext - 2, G[1], m_first)
 
-    def keep_first(i):
-        first_out[i] = vec[i + HALO][:, :breadth]
-
-    loop(0, height, 1, keep_first)
-
     def n_second(i):
         for k, v in enumerate(spread(i, [field[i + k] for k in range(G[2])])):
-            vec[i + k] = v
+            second_out[i + k] = v[:, :breadth]
             xb[i + k] = fill(v * is_in(i + k))
 
     loop(3, ext - 3, G[2], n_second)
 
     def m_second(i):
-        vs = [vec[i + k] for k in range(G[3])]
-        for k, s in enumerate(tangent(i, vs)):
-            second_out[i + k - HALO] = vs[k][:, :breadth]
-            hi[i + k, padded:] = fill(s[:, :breadth])
+        for k, s in enumerate(tangent(i, [second_out[i + k] for k in range(G[3])])):
+            hi[i + k, padded:] = fill(s)
 
     loop(HALO, ext - HALO, G[3], m_second)
 
@@ -423,7 +418,7 @@
         return pltpu.make_async_copy(mixed.at[i], increment.at[:, i], sems.at[i])
 
     for i in range(height):
-        mixed[i] = a * first[i, :channels] + b * second[i, :channels]
+        mixed[i] = a * first[i + HALO, :channels] + b * second[i + HALO, :channels]
         copy(i).start()
     slots_of = lax.broadcasted_iota(jnp.int32, (slots, rows), 0)
     place = (slots_of == slot[...]).astype(BF)
@@ -482,8 +477,9 @@
     )
 
     slope_inner = jnp.transpose(slope, (1, 0, 2))
-    slope_north = shift2(slope_inner[-HALO:], 1, 0)
-    slope_south = shift2(slope_inner[:HALO], -1, 0)
+    low, high = lax.optimization_barrier((slope[:, -HALO:], slope[:, :HALO]))
+    slope_north = shift2(jnp.transpose(low, (1, 0, 2)), 1, 0)
+    slope_south = shift2(jnp.transpose(high, (1, 0, 2)), -1, 0)
     slope_west, slope_east = call(strip_kernel, (shape((hidden, strip), BF),) * 2,
                                   (slope_inner, slope_north, slope_south))
 
@@ -511,7 +507,7 @@
     flags = jnp.stack([at > 0, at < lax.axis_size("lat") - 1]).astype(jnp.int32)
     first, second, reply = call(
         functools.partial(main_kernel, channels, hidden, cap),
-        (shape((height, trim, breadth)),) * 2 + (shape((slots, 2 * LANES), BF),),
+        (shape((ext, trim, breadth)),) * 2 + (shape((slots, 2 * LANES), BF),),
         (flags, got, inner, from_north, from_south, from_east, from_west, slope_inner, slope_north,
          slope_south, w_n, w_m, p_t, p_j, g3),
         scratch=[
@@ -519,7 +515,7 @@
             pltpu.VMEM((ext, hidden, wide), BF),
             pltpu.VMEM((ext, hidden, wide), BF),
             pltpu.VMEM((ext, padded, wide), BF),
-            pltpu.VMEM((ext, trim, wide), F32),
+            pltpu.VMEM((ext, trim, LANES), F32),
             pltpu.VMEM((ext, 2 * padded, breadth), BF),
             pltpu.VMEM((2 * padded, slots), F32),
         ],

time: 92.9 us -> 91.4 us (0.984)
  waiting for transfers between devices: 10.7 us -> 9.13 us
  local copies, waits for them, and re-layouts: 3.12 us -> 4.27 us
    ppermute x6, waiting for transfers between devices: 10.7 us -> 9.13 us  [shift2(): return lax.ppermute(x, ('lat', 'lon'), pairs)]
    slice x1, local copies, waits for them, and re-layouts: 0.02 us -> 1.14 us  [on_device(): low, high = lax.optimization_barrier((slope[:, -HALO:], slope[:, :HALO]))]
  transfers between devices with their start and end apart: 7 -> 7, of which waited for: 4 -> 4; matrix products, arithmetic and copies ran while one was open for 2% -> 4% of each run, Pallas kernels for 6% -> 6%
where the time goes in v7:
time: 91.4 us; the launch traced here: 91 us
  Pallas kernels  37.5 us (41%)
  starting transfers between devices  19.4 us (21%)
  blocking collectives  17.2 us (19%)
  waiting for transfers between devices  9.13 us (10%)
  local copies, waits for them, and re-layouts  4.27 us (5%)
  other arithmetic  1.71 us (2%)
  between operations  1.69 us (2%)
    pallas_call x9, Pallas kernels, call(): pl.pallas_call(kernel, out_shape=outs, grid=(1,) if staged else (), in_sp...  37.5 us
    all_to_all x1, blocking collectives, swap(): lax.all_to_all(x.reshape(tiles, cap, -1), ('lat', 'lon'), split_axis=0, c...  17.2 us
    ppermute x6, starting transfers between devices, shift2(): return lax.ppermute(x, ('lat', 'lon'), pairs)  12.1 us
    ppermute x6, waiting for transfers between devices, shift2(): return lax.ppermute(x, ('lat', 'lon'), pairs)  9.13 us
    all_to_all x1, starting transfers between devices, swap(): lax.all_to_all(x.reshape(tiles, cap, -1), ('lat', 'lon'), split_axis=0, c...  7.3 us
    unnamed x14, local copies, waits for them, and re-layouts  3.1 us
  transfers between devices with their start and end apart: 7, of which 4 were waited for; matrix products, arithmetic and copies ran while one was open for 4% of the time, Pallas kernels for 6%

profile of v7, /device:TPU:0, one launch (start us, length us, event | category | flops | bytes accessed | tf_op | source)
XLA Modules:
  0.0 91.0 jit_solution(3003475685625628316)
XLA Ops:
  0.6 0.0 copy-start.2
  0.6 0.0 copy-start.4
  0.7 0.0 copy-start.5
  1.4 0.9 pad_maximum_fusion.tables
  2.3 0.7 pad_add_fusion.meta
  3.0 0.0 copy-start
  3.0 1.0 %copy-done = f32[512,256]{1,0:T(8,128)S(1)} copy-done((f32[512,256]{1,0:T(8,128)S(1)}, f32[512,256]{1,0:T(8,128)}, u32[]{:S(2)}) %copy-start) | copy-done | bytes 524312
  4.0 0.0 copy-start.3
  4.0 1.6 %shard_map.113 = (bf16[768,128]{1,0:T(8,128)(2,1)}, s32[1,512]{1,0:T(1,128)S(1)}) custom-call(s32[1]{0:T(128)S(6)} %copy.20.count, f32[512,256]{1,0:T(8,128)S(1)} %copy-done, s32[3,512]{1,0:T(4,128)S(1)} %pad_add_fusion.meta, f32[70,256]{1,0:T(8,128)S(1)} %pad_maximum_fusion.tables), custom_call_target="tpu_custom_call" | custom-call | tf_op jit(solution)/shard_map/pallas_call | solution.py:37
  5.7 7.3 %all-to-all-start = ((bf16[32,24,128]{2,1,0:T(8,128)(2,1)}), bf16[32,24,128]{2,1,0:T(8,128)(2,1)S(1)}, u32[]{:S(2)}, u32[]{:S(2)}) async-start(bf16[32,24,128]{2,1,0:T(8,128)(2,1)} %bitcast.6), calls=%async_computation | async-start | bytes 393216 | tf_op jit(solution)/shard_map/all_to_all | solution.py:466
  13.0 1.1 %fusion = (bf16[64,4,256]{2,1,0:T(4,128)(2,1)S(1)}, bf16[64,4,256]{2,1,0:T(4,128)(2,1)S(1)}) fusion(bf16[64,48,256]{2,1,0:T(8,128)(2,1)} %param.19), kind=kLoop, calls=%fused_computation.4 | loop fusion | bytes 524288 | tf_op jit(solution)/shard_map/slice | solution.py:480
  14.2 1.3 %collective-permute-start.1 = (bf16[4,64,256]{2,1,0:T(8,128)(2,1)S(1)}, bf16[4,64,256]{2,1,0:T(8,128)(2,1)S(1)}, u32[]{:S(2)}, u32[]{:S(2)}) collective-permute-start(bf16[4,64,256]{2,1,0:T(8,128)(2,1)S(1)} %bitcast.26), channel_id=1, source_target_pairs={{4,0},{5,1},{6,2},{7,3},{8,4},{9,5},{10,6},{11,7},{12,8},{13,9},{1... | collective-permute-start | bytes 393224 | tf_op jit(solution)/shard_map/ppermute | solution.py:436
  15.5 4.6 %collective-permute-start = (bf16[4,64,256]{2,1,0:T(8,128)(2,1)S(1)}, bf16[4,64,256]{2,1,0:T(8,128)(2,1)S(1)}, u32[]{:S(2)}, u32[]{:S(2)}) collective-permute-start(bf16[4,64,256]{2,1,0:T(8,128)(2,1)S(1)} %bitcast.25), channel_id=1, source_target_pairs={{0,4},{1,5},{2,6},{3,7},{4,8},{5,9},{6,10},{7,11},{8,12},{9,13},{1... | collective-permute-start | bytes 393224 | tf_op jit(solution)/shard_map/ppermute | solution.py:436
  20.0 2.4 %collective-permute-done.1._slope_south.south.slope_south = bf16[4,64,256]{2,1,0:T(8,128)(2,1)S(1)} collective-permute-done((bf16[4,64,256]{2,1,0:T(8,128)(2,1)S(1)}, bf16[4,64,256]{2,1,0:T(8,128)(2,1)S(1)}, u32[]{:S(2)}, u32[]{:S(2)}) %collective-permute-start.1) | collective-permute-done | bytes 131104 | tf_op jit(solution)/shard_map/ppermute | solution.py:436
  22.5 2.6 %collective-permute-done._slope_north.north.slope_north = bf16[4,64,256]{2,1,0:T(8,128)(2,1)S(1)} collective-permute-done((bf16[4,64,256]{2,1,0:T(8,128)(2,1)S(1)}, bf16[4,64,256]{2,1,0:T(8,128)(2,1)S(1)}, u32[]{:S(2)}, u32[]{:S(2)}) %collective-permute-start) | collective-permute-done | bytes 131104 | tf_op jit(solution)/shard_map/ppermute | solution.py:436
  25.0 0.0 all-to-all-done
  25.0 0.5 shard_map.115
  25.6 4.4 %collective-permute-start.2 = (bf16[288,256]{1,0:T(8,128)(2,1)S(1)}, bf16[288,256]{1,0:T(8,128)(2,1)S(1)}, u32[]{:S(2)}, u32[]{:S(2)}) collective-permute-start(bf16[288,256]{1,0:T(8,128)(2,1)S(1)} %get-tuple-element.25), channel_id=1, source_target_pairs={{0,4},{1,5},{2,6},{3,7},{4,8},{5,9},{6,10},{7,11},{8,12},{9,13},{1... | collective-permute-start | bytes 442376 | tf_op jit(solution)/shard_map/ppermute | solution.py:436
  30.0 1.3 %collective-permute-start.3 = (bf16[288,256]{1,0:T(8,128)(2,1)S(1)}, bf16[288,256]{1,0:T(8,128)(2,1)S(1)}, u32[]{:S(2)}, u32[]{:S(2)}) collective-permute-start(bf16[288,256]{1,0:T(8,128)(2,1)S(1)} %get-tuple-element.26), channel_id=1, source_target_pairs={{4,0},{5,1},{6,2},{7,3},{8,4},{9,5},{10,6},{11,7},{12,8},{13,9},{1... | collective-permute-start | bytes 442376 | tf_op jit(solution)/shard_map/ppermute | solution.py:436
  31.3 1.9 %copy.19 = bf16[64,48,256]{2,0,1:T(8,128)(2,1)S(1)} copy(bf16[64,48,256]{2,1,0:T(8,128)(2,1)} %param.19) | data formatting | bytes 3145728 | tf_op args[9]
  33.2 0.0 copy-done.5
  33.2 0.1 copy.15.projection
  33.3 0.0 copy-done.2
  33.3 0.0 copy-done.4
  33.4 0.0 copy-done.3
  33.4 1.1 %shard_map.118 = (bf16[192,240]{1,0:T(8,128)(2,1)S(1)}, bf16[216,192]{1,0:T(8,128)(2,1)S(1)}, bf16[64,80]{1,0:T(8,128)(2,1)S(1)}, bf16[72,64]{1,0:T(8,128)(2,1)S(1)}, bf16[136,240]{1,0:T(8,128)(2,1)S(1)}) custom-call(bf16[9,64,69]{2,1,0:T(8,128)(2,1)S(1)} %copy-done.3, bf16[69,64]{1,0:T(8,128)(2,1)S(1)} %copy.15.projection, f32[69,256]{1,0:T(8,128)S(1)} %copy-done.2, ...), custom_call_target="tpu_custom_call" | custom-call | tf_op jit(solution)/shard_map/pallas_call | solution.py:37
  34.5 0.6 shard_map.117
  35.0 1.0 %shard_map.116 = (bf16[80,512]{1,0:T(8,128)(2,1)S(1)}, bf16[80,512]{1,0:T(8,128)(2,1)S(1)}) custom-call(bf16[768,128]{1,0:T(8,128)(2,1)S(1)} %bitcast.18), custom_call_target="tpu_custom_call" | custom-call | tf_op jit(solution)/shard_map/pallas_call | solution.py:37
  36.0 0.0 collective-permute-done.2.from_north.north
  36.0 1.3 %collective-permute-done.3.from_south.south = bf16[288,256]{1,0:T(8,128)(2,1)S(1)} collective-permute-done((bf16[288,256]{1,0:T(8,128)(2,1)S(1)}, bf16[288,256]{1,0:T(8,128)(2,1)S(1)}, u32[]{:S(2)}, u32[]{:S(2)}) %collective-permute-start.3) | collective-permute-done | bytes 147488 | tf_op jit(solution)/shard_map/ppermute | solution.py:436
  37.4 0.2 shard_map.119
  37.5 0.1 collective-permute-start.4
  37.6 0.5 collective-permute-start.5
  38.1 0.1 add_convert_fusion.flags
  38.2 2.8 %shard_map.114.inner = f32[48,72,256]{2,1,0:T(8,128)S(1)} custom-call(bf16[768,128]{1,0:T(8,128)(2,1)S(1)} %bitcast.19), custom_call_target="tpu_custom_call" | custom-call | tf_op jit(solution)/shard_map/pallas_call | solution.py:37
  41.0 0.0 collective-permute-done.4.from_east
  41.0 2.8 %collective-permute-done.5.from_west = bf16[144,512]{1,0:T(8,128)(2,1)S(1)} collective-permute-done((bf16[144,512]{1,0:T(8,128)(2,1)S(1)}, bf16[144,512]{1,0:T(8,128)(2,1)S(1)}, u32[]{:S(2)}, u32[]{:S(2)}) %collective-permute-start.5) | collective-permute-done | bytes 147488 | tf_op jit(solution)/shard_map/ppermute | solution.py:436
  43.8 0.0 copy-start.1
  43.8 26.0 %shard_map.120 = (f32[56,72,256]{2,1,0:T(8,128)S(1)}, f32[56,72,256]{2,1,0:T(8,128)S(1)}, bf16[768,256]{1,0:T(8,128)(2,1)S(1)}) custom-call(s32[2]{0:T(128)S(1)} %add_convert_fusion.flags, bf16[768,128]{1,0:T(8,128)(2,1)S(1)} %bitcast.20, f32[48,72,256]{2,1,0:T(8,128)S(1)} %shard_map.114.inner, bf16[288,256]{1,0:T(8,128)(2,1)S(1)} %collective-permute-done.2.from_north.north, ...), custom_call_target="tpu_custom_call" | custom-call | tf_op jit(solution)/shard_map/pallas_call | solution.py:37
  69.8 17.2 %all_to_all.10 = bf16[32,24,256]{2,1,0:T(8,128)(2,1)S(1)} all-to-all(bf16[32,24,256]{2,1,0:T(8,128)(2,1)S(1)} %bitcast.22), channel_id=1, replica_groups=mesh['lat'=8,'lon'=4] {'lat','lon'}, dimensions={0} | all-to-all | bytes 786432 | tf_op jit(solution)/shard_map/all_to_all | solution.py:466
  87.0 0.0 copy-done.1
  87.0 3.8 %shard_map.121 = (f32[69,48,256]{2,1,0:T(8,128)}, f32[512,256]{1,0:T(8,128)}) custom-call(bf16[768,256]{1,0:T(8,128)(2,1)S(1)} %bitcast.21, s32[1,512]{1,0:T(1,128)S(1)} %get-tuple-element.39.slot, f32[512,256]{1,0:T(8,128)S(1)} %copy-done.1, f32[69,256]{1,0:T(8,128)S(1)} %copy-done.2, f32[56,72,256]{2,1,0:T(8,128)S(1)} %get-tuple-element.40.first, ...), custom_call_target="tpu_custom_call" | custom-call | tf_op jit(solution)/shard_map/pallas_call | solution.py:37
  (2 shorter events, 0.0 us)
Async XLA Ops:
  0.6 32.7 %copy-start.2 = (f32[69,256]{1,0:T(8,128)S(1)}, f32[69,256]{1,0:T(8,128)}, u32[]{:S(2)}) copy-start(f32[69,256]{1,0:T(8,128)} %jac.3) | copy-start | bytes 211972
  0.6 32.7 %copy-start.4 = (f32[256]{0:T(256)S(1)}, f32[256]{0:T(256)}, u32[]{:S(2)}) copy-start(f32[256]{0:T(256)} %param.15) | copy-start | bytes 3076
  0.7 32.6 %copy-start.5 = (bf16[69,64]{0,1:T(8,128)(2,1)S(1)}, bf16[69,64]{0,1:T(8,128)(2,1)}, u32[]{:S(2)}) copy-start(bf16[69,64]{0,1:T(8,128)(2,1)} %param.18) | copy-start | bytes 26500
  3.0 1.0 %copy-start = (f32[512,256]{1,0:T(8,128)S(1)}, f32[512,256]{1,0:T(8,128)}, u32[]{:S(2)}) copy-start(f32[512,256]{1,0:T(8,128)} %dep.3) | copy-start | bytes 1572868
  4.0 29.3 %copy-start.3 = (bf16[9,64,69]{2,1,0:T(8,128)(2,1)S(1)}, bf16[9,64,69]{2,1,0:T(8,128)(2,1)}, u32[]{:S(2)}) copy-start(bf16[9,64,69]{2,1,0:T(8,128)(2,1)} %taps.1) | copy-start | bytes 238468
  5.7 19.4 %all-to-all-start = ((bf16[32,24,128]{2,1,0:T(8,128)(2,1)}), bf16[32,24,128]{2,1,0:T(8,128)(2,1)S(1)}, u32[]{:S(2)}, u32[]{:S(2)}) async-start(bf16[32,24,128]{2,1,0:T(8,128)(2,1)} %bitcast.6), calls=%async_computation | async-start | bytes 393216 | tf_op jit(solution)/shard_map/all_to_all | solution.py:466
  14.2 8.3 %collective-permute-start.1 = (bf16[4,64,256]{2,1,0:T(8,128)(2,1)S(1)}, bf16[4,64,256]{2,1,0:T(8,128)(2,1)S(1)}, u32[]{:S(2)}, u32[]{:S(2)}) collective-permute-start(bf16[4,64,256]{2,1,0:T(8,128)(2,1)S(1)} %bitcast.26), channel_id=1, source_target_pairs={{4,0},{5,1},{6,2},{7,3},{8,4},{9,5},{10,6},{11,7},{12,8},{13,9},{1... | collective-permute-start | bytes 393224 | tf_op jit(solution)/shard_map/ppermute | solution.py:436
  15.5 9.6 %collective-permute-start = (bf16[4,64,256]{2,1,0:T(8,128)(2,1)S(1)}, bf16[4,64,256]{2,1,0:T(8,128)(2,1)S(1)}, u32[]{:S(2)}, u32[]{:S(2)}) collective-permute-start(bf16[4,64,256]{2,1,0:T(8,128)(2,1)S(1)} %bitcast.25), channel_id=1, source_target_pairs={{0,4},{1,5},{2,6},{3,7},{4,8},{5,9},{6,10},{7,11},{8,12},{9,13},{1... | collective-permute-start | bytes 393224 | tf_op jit(solution)/shard_map/ppermute | solution.py:436
  25.6 10.5 %collective-permute-start.2 = (bf16[288,256]{1,0:T(8,128)(2,1)S(1)}, bf16[288,256]{1,0:T(8,128)(2,1)S(1)}, u32[]{:S(2)}, u32[]{:S(2)}) collective-permute-start(bf16[288,256]{1,0:T(8,128)(2,1)S(1)} %get-tuple-element.25), channel_id=1, source_target_pairs={{0,4},{1,5},{2,6},{3,7},{4,8},{5,9},{6,10},{7,11},{8,12},{9,13},{1... | collective-permute-start | bytes 442376 | tf_op jit(solution)/shard_map/ppermute | solution.py:436
  30.0 7.4 %collective-permute-start.3 = (bf16[288,256]{1,0:T(8,128)(2,1)S(1)}, bf16[288,256]{1,0:T(8,128)(2,1)S(1)}, u32[]{:S(2)}, u32[]{:S(2)}) collective-permute-start(bf16[288,256]{1,0:T(8,128)(2,1)S(1)} %get-tuple-element.26), channel_id=1, source_target_pairs={{4,0},{5,1},{6,2},{7,3},{8,4},{9,5},{10,6},{11,7},{12,8},{13,9},{1... | collective-permute-start | bytes 442376 | tf_op jit(solution)/shard_map/ppermute | solution.py:436
  37.5 3.4 %collective-permute-start.4 = (bf16[144,512]{1,0:T(8,128)(2,1)S(1)}, bf16[144,512]{1,0:T(8,128)(2,1)S(1)}, u32[]{:S(2)}, u32[]{:S(2)}) collective-permute-start(bf16[144,512]{1,0:T(8,128)(2,1)S(1)} %get-tuple-element.32), channel_id=1, source_target_pairs={{0,3},{1,0},{2,1},{3,2},{4,7},{5,4},{6,5},{7,6},{8,11},{9,8},{10,9... | collective-permute-start | bytes 442376 | tf_op jit(solution)/shard_map/ppermute | solution.py:436
  37.6 6.2 %collective-permute-start.5 = (bf16[144,512]{1,0:T(8,128)(2,1)S(1)}, bf16[144,512]{1,0:T(8,128)(2,1)S(1)}, u32[]{:S(2)}, u32[]{:S(2)}) collective-permute-start(bf16[144,512]{1,0:T(8,128)(2,1)S(1)} %get-tuple-element.33), channel_id=1, source_target_pairs={{0,1},{1,2},{2,3},{3,0},{4,5},{5,6},{6,7},{7,4},{8,9},{9,10},{10,1... | collective-permute-start | bytes 442376 | tf_op jit(solution)/shard_map/ppermute | solution.py:436
  43.8 43.2 %copy-start.1 = (f32[512,256]{1,0:T(8,128)S(1)}, f32[512,256]{1,0:T(8,128)}, u32[]{:S(2)}) copy-start(f32[512,256]{1,0:T(8,128)} %dep.3) | copy-start | bytes 1572868

commit v8 on v7

--- a/solution.py
+++ b/solution.py
@@ -11,6 +11,7 @@
 ITERS = 2
 HALO = 4
 LANES = 128
+GROUP = 8
 SIDE = 2 * HALO
 BF = jnp.bfloat16
 F32 = jnp.float32
@@ -379,22 +380,32 @@
     pieces = jnp.zeros((1, LANES), F32)
     for number, value in enumerate(sums):
         for third, piece in enumerate(split3(value)):
-            pieces = jnp.where(lane == channels + 3 + 3 * number + third, piece.astype(F32), pieces)
-    filler = jnp.zeros((LANES - trim, slots), F32)
-    turned0 = jnp.concatenate([row0, filler], axis=0).T
-    turned1 = jnp.concatenate([row1, filler], axis=0).T
-    leads = lax.broadcasted_iota(jnp.int32, (slots, LANES), 0)
-    is_lead = leads % cap == 0
-    lanes = lax.broadcasted_iota(jnp.int32, (slots, LANES), 1)
-    reply[:, :LANES] = jnp.where(lanes < channels, turned0, jnp.where(is_lead, pieces, 0.0)).astype(BF)
-    reply[:, LANES:] = turned1.astype(BF)
-
-
-def scalars(reply, channels):
-    sums = jnp.sum(reply[:, :LANES].astype(F32), axis=0, keepdims=True)
+            pieces = jnp.where(lane == 3 * number + third, piece.astype(F32), pieces)
+    size = reply.shape[0] * cap // slots
+    slot = lax.broadcasted_iota(jnp.int32, (1, slots), 1)
+    near, far, turn_of = reply_rows(slot, cap, size)
+    start = jnp.concatenate([row0, row1[: LANES - trim]], axis=0).astype(BF)
+    end = jnp.concatenate([row1[LANES - trim :]] * GROUP, axis=0)
+    tail = LANES // GROUP
+    end = jnp.where(lax.broadcasted_iota(jnp.int32, (LANES, slots), 0) // tail == turn_of, end, 0.0).astype(BF)
+    at = lax.broadcasted_iota(jnp.int32, (reply.shape[0], slots), 0)
+    packed = mxu((at == near).astype(BF), start, ((1,), (1,))) + mxu((at == far).astype(BF), end, ((1,), (1,)))
+    row = lax.broadcasted_iota(jnp.int32, reply.shape, 0)
+    reply[...] = jnp.where(row % size == size - 1, pieces, packed).astype(BF)
+
+
+def reply_rows(slot, cap, size):
+    block = slot // cap
+    inside = slot - block * cap
+    return block * size + inside, block * size + cap + inside // GROUP, inside % GROUP
+
+
+def scalars(reply, size):
+    row = lax.broadcasted_iota(jnp.int32, reply.shape, 0)
+    sums = jnp.sum(jnp.where(row % size == size - 1, reply[...].astype(F32), 0.0), axis=0, keepdims=True)
 
     def value(number):
-        at = channels + 3 + 3 * number
+        at = 3 * number
         return sums[:, at : at + 1] + sums[:, at + 1 : at + 2] + sums[:, at + 2 : at + 3]
 
     a00, a01, a11, d11 = (value(n) for n in range(4))
@@ -408,11 +419,10 @@
     return step0 + step1 * c0, step1 * c1
 
 
-def final_kernel(channels, back, slot, dep, jac, first, second, increment, departures, mixed, sems):
-    slots = back.shape[0]
+def final_kernel(channels, cap, size, back, slot, dep, jac, first, second, increment, departures, mixed, sems):
     rows = dep.shape[0]
     height = mixed.shape[0]
-    a, b = scalars(back, channels)
+    a, b = scalars(back, size)
 
     def copy(i):
         return pltpu.make_async_copy(mixed.at[i], increment.at[:, i], sems.at[i])
@@ -420,11 +430,16 @@
     for i in range(height):
         mixed[i] = a * first[i + HALO, :channels] + b * second[i + HALO, :channels]
         copy(i).start()
-    slots_of = lax.broadcasted_iota(jnp.int32, (slots, rows), 0)
-    place = (slots_of == slot[...]).astype(BF)
-    own = mxu(place, back[...], ((0,), (0,)))
-    state = a * own[:, :channels] + b * own[:, LANES : LANES + channels]
-    departures[...] = dep[...] - mxu(state, jac[...], precision=lax.Precision.HIGHEST)
+    near, far, turn_of = reply_rows(slot[...], cap, size)
+    at = lax.broadcasted_iota(jnp.int32, (back.shape[0], rows), 0)
+    start = mxu(back[...], (at == near).astype(BF), ((0,), (0,)))
+    end = mxu(back[...], (at == far).astype(BF), ((0,), (0,)))
+    tail = LANES // GROUP
+    end = jnp.where(lax.broadcasted_iota(jnp.int32, (LANES, rows), 0) // tail == turn_of, end, 0.0)
+    end = functools.reduce(jnp.add, [end[k * tail : (k + 1) * tail] for k in range(GROUP)])
+    trim = first.shape[1]
+    state = a * start[:trim] + b * jnp.concatenate([start[trim:], end], axis=0)
+    departures[...] = dep[...] - mxu(state[:channels], jac[...], ((0,), (0,)), lax.Precision.HIGHEST)
     for i in range(height):
         copy(i).wait()
 
@@ -446,6 +461,8 @@
     slots = tiles * cap
     padded = -(-(channels + 1) // 16) * 16
     trim = -(-(channels + 1) // 8) * 8
+    assert 2 * trim == LANES + LANES // GROUP
+    size = -(-(cap + -(-cap // GROUP) + 1) // 8) * 8
     wide = breadth + LANES
     ext = height + 2 * HALO
     strip = -(-(ext * SIDE) // LANES) * LANES
@@ -463,8 +480,8 @@
     )
 
     def swap(x):
-        return lax.all_to_all(x.reshape(tiles, cap, -1), ("lat", "lon"), split_axis=0, concat_axis=0,
-                              tiled=True).reshape(slots, -1)
+        return lax.all_to_all(x.reshape(tiles, -1, LANES), ("lat", "lon"), split_axis=0, concat_axis=0,
+                              tiled=True).reshape(x.shape)
 
     got = swap(send)
 
@@ -507,7 +524,7 @@
     flags = jnp.stack([at > 0, at < lax.axis_size("lat") - 1]).astype(jnp.int32)
     first, second, reply = call(
         functools.partial(main_kernel, channels, hidden, cap),
-        (shape((ext, trim, breadth)),) * 2 + (shape((slots, 2 * LANES), BF),),
+        (shape((ext, trim, breadth)),) * 2 + (shape((tiles * size, LANES), BF),),
         (flags, got, inner, from_north, from_south, from_east, from_west, slope_inner, slope_north,
          slope_south, w_n, w_m, p_t, p_j, g3),
         scratch=[
@@ -524,7 +541,7 @@
     )
     back = swap(reply)
     return call(
-        functools.partial(final_kernel, channels),
+        functools.partial(final_kernel, channels, cap, size),
         (shape((channels, height, breadth)), shape((rows, radiances))),
         (back, slot, departure_in, jacobian, first, second),
         scratch=[pltpu.VMEM((height, channels, breadth), F32), pltpu.SemaphoreType.DMA((height,))],

time: 91.4 us -> 89.1 us (0.975)
  blocking collectives: 17.2 us -> 14.7 us
    all_to_all x1, blocking collectives: 17.2 us -> 14.7 us  [swap(): lax.all_to_all(x.reshape(tiles, -1, LANES), ('lat', 'lon'), split_axis=0,...]
where the time goes in v8:
time: 89.1 us; the launch traced here: 88.6 us
  Pallas kernels  37.8 us (42%)
  starting transfers between devices  19.4 us (22%)
  blocking collectives  14.7 us (16%)
  waiting for transfers between devices  9.13 us (10%)
  local copies, waits for them, and re-layouts  4.27 us (5%)
  other arithmetic  1.71 us (2%)
  between operations  1.68 us (2%)
    pallas_call x9, Pallas kernels, call(): pl.pallas_call(kernel, out_shape=outs, grid=(1,) if staged else (), in_sp...  37.8 us
    all_to_all x1, blocking collectives, swap(): lax.all_to_all(x.reshape(tiles, -1, LANES), ('lat', 'lon'), split_axis=0,...  14.7 us
    ppermute x6, starting transfers between devices, shift2(): return lax.ppermute(x, ('lat', 'lon'), pairs)  12.1 us
    ppermute x6, waiting for transfers between devices, shift2(): return lax.ppermute(x, ('lat', 'lon'), pairs)  9.13 us
    all_to_all x1, starting transfers between devices, swap(): lax.all_to_all(x.reshape(tiles, -1, LANES), ('lat', 'lon'), split_axis=0,...  7.3 us
    unnamed x14, local copies, waits for them, and re-layouts  3.1 us
  transfers between devices with their start and end apart: 7, of which 4 were waited for; matrix products, arithmetic and copies ran while one was open for 4% of the time, Pallas kernels for 6%

profile of v8, /device:TPU:0, one launch (start us, length us, event | category | flops | bytes accessed | tf_op | source)
XLA Modules:
  0.0 88.6 jit_solution(12248687494022504514)
XLA Ops:
  0.6 0.0 copy-start.2
  0.6 0.0 copy-start.4
  0.7 0.0 copy-start.5
  1.4 0.9 %pad_maximum_fusion.tables = f32[70,256]{1,0:T(8,128)S(1)} fusion(f32[1,256]{1,0:T(1,128)} %bitcast.23, f32[69,256]{1,0:T(8,128)} %jac.3), kind=kLoop, calls=%fused_computation | loop fusion | flops 17920 | bytes 143360 | tf_op jit(solution)/shard_map/concatenate | solution.py:478
  2.3 0.7 pad_add_fusion.meta
  3.0 0.0 copy-start
  3.0 1.0 %copy-done = f32[512,256]{1,0:T(8,128)S(1)} copy-done((f32[512,256]{1,0:T(8,128)S(1)}, f32[512,256]{1,0:T(8,128)}, u32[]{:S(2)}) %copy-start) | copy-done | bytes 524312
  4.0 0.0 copy-start.3
  4.0 1.6 %shard_map.113 = (bf16[768,128]{1,0:T(8,128)(2,1)}, s32[1,512]{1,0:T(1,128)S(1)}) custom-call(s32[1]{0:T(128)S(6)} %copy.20.count, f32[512,256]{1,0:T(8,128)S(1)} %copy-done, s32[3,512]{1,0:T(4,128)S(1)} %pad_add_fusion.meta, f32[70,256]{1,0:T(8,128)S(1)} %pad_maximum_fusion.tables), custom_call_target="tpu_custom_call" | custom-call | tf_op jit(solution)/shard_map/pallas_call | solution.py:38
  5.7 7.3 %all-to-all-start = ((bf16[32,24,128]{2,1,0:T(8,128)(2,1)}), bf16[32,24,128]{2,1,0:T(8,128)(2,1)S(1)}, u32[]{:S(2)}, u32[]{:S(2)}) async-start(bf16[32,24,128]{2,1,0:T(8,128)(2,1)} %bitcast.6), calls=%async_computation | async-start | bytes 393216 | tf_op jit(solution)/shard_map/all_to_all | solution.py:483
  13.0 1.1 %fusion = (bf16[64,4,256]{2,1,0:T(4,128)(2,1)S(1)}, bf16[64,4,256]{2,1,0:T(4,128)(2,1)S(1)}) fusion(bf16[64,48,256]{2,1,0:T(8,128)(2,1)} %param.19), kind=kLoop, calls=%fused_computation.4 | loop fusion | bytes 524288 | tf_op jit(solution)/shard_map/slice | solution.py:497
  14.2 1.3 %collective-permute-start.1 = (bf16[4,64,256]{2,1,0:T(8,128)(2,1)S(1)}, bf16[4,64,256]{2,1,0:T(8,128)(2,1)S(1)}, u32[]{:S(2)}, u32[]{:S(2)}) collective-permute-start(bf16[4,64,256]{2,1,0:T(8,128)(2,1)S(1)} %bitcast.26), channel_id=1, source_target_pairs={{4,0},{5,1},{6,2},{7,3},{8,4},{9,5},{10,6},{11,7},{12,8},{13,9},{1... | collective-permute-start | bytes 393224 | tf_op jit(solution)/shard_map/ppermute | solution.py:451
  15.5 4.6 %collective-permute-start = (bf16[4,64,256]{2,1,0:T(8,128)(2,1)S(1)}, bf16[4,64,256]{2,1,0:T(8,128)(2,1)S(1)}, u32[]{:S(2)}, u32[]{:S(2)}) collective-permute-start(bf16[4,64,256]{2,1,0:T(8,128)(2,1)S(1)} %bitcast.25), channel_id=1, source_target_pairs={{0,4},{1,5},{2,6},{3,7},{4,8},{5,9},{6,10},{7,11},{8,12},{9,13},{1... | collective-permute-start | bytes 393224 | tf_op jit(solution)/shard_map/ppermute | solution.py:451
  20.0 2.4 %collective-permute-done.1._slope_south.south.slope_south = bf16[4,64,256]{2,1,0:T(8,128)(2,1)S(1)} collective-permute-done((bf16[4,64,256]{2,1,0:T(8,128)(2,1)S(1)}, bf16[4,64,256]{2,1,0:T(8,128)(2,1)S(1)}, u32[]{:S(2)}, u32[]{:S(2)}) %collective-permute-start.1) | collective-permute-done | bytes 131104 | tf_op jit(solution)/shard_map/ppermute | solution.py:451
  22.5 2.6 %collective-permute-done._slope_north.north.slope_north = bf16[4,64,256]{2,1,0:T(8,128)(2,1)S(1)} collective-permute-done((bf16[4,64,256]{2,1,0:T(8,128)(2,1)S(1)}, bf16[4,64,256]{2,1,0:T(8,128)(2,1)S(1)}, u32[]{:S(2)}, u32[]{:S(2)}) %collective-permute-start) | collective-permute-done | bytes 131104 | tf_op jit(solution)/shard_map/ppermute | solution.py:451
  25.0 0.0 all-to-all-done
  25.0 0.5 shard_map.115
  25.6 4.4 %collective-permute-start.2 = (bf16[288,256]{1,0:T(8,128)(2,1)S(1)}, bf16[288,256]{1,0:T(8,128)(2,1)S(1)}, u32[]{:S(2)}, u32[]{:S(2)}) collective-permute-start(bf16[288,256]{1,0:T(8,128)(2,1)S(1)} %get-tuple-element.25), channel_id=1, source_target_pairs={{0,4},{1,5},{2,6},{3,7},{4,8},{5,9},{6,10},{7,11},{8,12},{9,13},{1... | collective-permute-start | bytes 442376 | tf_op jit(solution)/shard_map/ppermute | solution.py:451
  30.0 1.3 %collective-permute-start.3 = (bf16[288,256]{1,0:T(8,128)(2,1)S(1)}, bf16[288,256]{1,0:T(8,128)(2,1)S(1)}, u32[]{:S(2)}, u32[]{:S(2)}) collective-permute-start(bf16[288,256]{1,0:T(8,128)(2,1)S(1)} %get-tuple-element.26), channel_id=1, source_target_pairs={{4,0},{5,1},{6,2},{7,3},{8,4},{9,5},{10,6},{11,7},{12,8},{13,9},{1... | collective-permute-start | bytes 442376 | tf_op jit(solution)/shard_map/ppermute | solution.py:451
  31.3 1.9 %copy.19 = bf16[64,48,256]{2,0,1:T(8,128)(2,1)S(1)} copy(bf16[64,48,256]{2,1,0:T(8,128)(2,1)} %param.19) | data formatting | bytes 3145728 | tf_op args[9]
  33.2 0.0 copy-done.5
  33.2 0.1 copy.15.projection
  33.3 0.0 copy-done.2
  33.3 0.0 copy-done.4
  33.4 0.0 copy-done.3
  33.4 1.1 %shard_map.118 = (bf16[192,240]{1,0:T(8,128)(2,1)S(1)}, bf16[216,192]{1,0:T(8,128)(2,1)S(1)}, bf16[64,80]{1,0:T(8,128)(2,1)S(1)}, bf16[72,64]{1,0:T(8,128)(2,1)S(1)}, bf16[136,240]{1,0:T(8,128)(2,1)S(1)}) custom-call(bf16[9,64,69]{2,1,0:T(8,128)(2,1)S(1)} %copy-done.3, bf16[69,64]{1,0:T(8,128)(2,1)S(1)} %copy.15.projection, f32[69,256]{1,0:T(8,128)S(1)} %copy-done.2, ...), custom_call_target="tpu_custom_call" | custom-call | tf_op jit(solution)/shard_map/pallas_call | solution.py:38
  34.5 0.6 shard_map.117
  35.0 1.0 %shard_map.116 = (bf16[80,512]{1,0:T(8,128)(2,1)S(1)}, bf16[80,512]{1,0:T(8,128)(2,1)S(1)}) custom-call(bf16[768,128]{1,0:T(8,128)(2,1)S(1)} %bitcast.18), custom_call_target="tpu_custom_call" | custom-call | tf_op jit(solution)/shard_map/pallas_call | solution.py:38
  36.0 0.0 collective-permute-done.2.from_north.north
  36.0 1.3 %collective-permute-done.3.from_south.south = bf16[288,256]{1,0:T(8,128)(2,1)S(1)} collective-permute-done((bf16[288,256]{1,0:T(8,128)(2,1)S(1)}, bf16[288,256]{1,0:T(8,128)(2,1)S(1)}, u32[]{:S(2)}, u32[]{:S(2)}) %collective-permute-start.3) | collective-permute-done | bytes 147488 | tf_op jit(solution)/shard_map/ppermute | solution.py:451
  37.4 0.2 shard_map.119
  37.5 0.1 collective-permute-start.4
  37.6 0.5 collective-permute-start.5
  38.1 0.1 add_convert_fusion.flags
  38.2 2.8 %shard_map.114.inner = f32[48,72,256]{2,1,0:T(8,128)S(1)} custom-call(bf16[768,128]{1,0:T(8,128)(2,1)S(1)} %bitcast.19), custom_call_target="tpu_custom_call" | custom-call | tf_op jit(solution)/shard_map/pallas_call | solution.py:38
  41.0 0.0 collective-permute-done.4.from_east
  41.0 2.8 %collective-permute-done.5.from_west = bf16[144,512]{1,0:T(8,128)(2,1)S(1)} collective-permute-done((bf16[144,512]{1,0:T(8,128)(2,1)S(1)}, bf16[144,512]{1,0:T(8,128)(2,1)S(1)}, u32[]{:S(2)}, u32[]{:S(2)}) %collective-permute-start.5) | collective-permute-done | bytes 147488 | tf_op jit(solution)/shard_map/ppermute | solution.py:451
  43.8 0.0 copy-start.1
  43.8 26.5 %shard_map.120 = (f32[56,72,256]{2,1,0:T(8,128)S(1)}, f32[56,72,256]{2,1,0:T(8,128)S(1)}, bf16[1024,128]{1,0:T(8,128)(2,1)S(1)}) custom-call(s32[2]{0:T(128)S(1)} %add_convert_fusion.flags, bf16[768,128]{1,0:T(8,128)(2,1)S(1)} %bitcast.20, f32[48,72,256]{2,1,0:T(8,128)S(1)} %shard_map.114.inner, ...), custom_call_target="tpu_custom_call" | custom-call | tf_op jit(solution)/shard_map/pallas_call | solution.py:38
  70.3 14.7 %all_to_all.10 = bf16[32,32,128]{2,1,0:T(8,128)(2,1)S(1)} all-to-all(bf16[32,32,128]{2,1,0:T(8,128)(2,1)S(1)} %bitcast.22), channel_id=1, replica_groups=mesh['lat'=8,'lon'=4] {'lat','lon'}, dimensions={0} | all-to-all | bytes 524288 | tf_op jit(solution)/shard_map/all_to_all | solution.py:483
  85.0 0.0 copy-done.1
  85.0 3.5 %shard_map.121 = (f32[69,48,256]{2,1,0:T(8,128)}, f32[512,256]{1,0:T(8,128)}) custom-call(bf16[1024,128]{1,0:T(8,128)(2,1)S(1)} %bitcast.21, s32[1,512]{1,0:T(1,128)S(1)} %get-tuple-element.39.slot, f32[512,256]{1,0:T(8,128)S(1)} %copy-done.1, f32[69,256]{1,0:T(8,128)S(1)} %copy-done.2, f32[56,72,256]{2,1,0:T(8,128)S(1)} %get-tuple-element.40.first, ...), custom_call_target="tpu_custom_call" | custom-call | tf_op jit(solution)/shard_map/pallas_call | solution.py:38
  (2 shorter events, 0.0 us)
Async XLA Ops:
  0.6 32.7 %copy-start.2 = (f32[69,256]{1,0:T(8,128)S(1)}, f32[69,256]{1,0:T(8,128)}, u32[]{:S(2)}) copy-start(f32[69,256]{1,0:T(8,128)} %jac.3) | copy-start | bytes 211972
  0.6 32.7 %copy-start.4 = (f32[256]{0:T(256)S(1)}, f32[256]{0:T(256)}, u32[]{:S(2)}) copy-start(f32[256]{0:T(256)} %param.15) | copy-start | bytes 3076
  0.7 32.6 %copy-start.5 = (bf16[69,64]{0,1:T(8,128)(2,1)S(1)}, bf16[69,64]{0,1:T(8,128)(2,1)}, u32[]{:S(2)}) copy-start(bf16[69,64]{0,1:T(8,128)(2,1)} %param.18) | copy-start | bytes 26500
  3.0 1.0 %copy-start = (f32[512,256]{1,0:T(8,128)S(1)}, f32[512,256]{1,0:T(8,128)}, u32[]{:S(2)}) copy-start(f32[512,256]{1,0:T(8,128)} %dep.3) | copy-start | bytes 1572868
  4.0 29.3 %copy-start.3 = (bf16[9,64,69]{2,1,0:T(8,128)(2,1)S(1)}, bf16[9,64,69]{2,1,0:T(8,128)(2,1)}, u32[]{:S(2)}) copy-start(bf16[9,64,69]{2,1,0:T(8,128)(2,1)} %taps.1) | copy-start | bytes 238468
  5.7 19.4 %all-to-all-start = ((bf16[32,24,128]{2,1,0:T(8,128)(2,1)}), bf16[32,24,128]{2,1,0:T(8,128)(2,1)S(1)}, u32[]{:S(2)}, u32[]{:S(2)}) async-start(bf16[32,24,128]{2,1,0:T(8,128)(2,1)} %bitcast.6), calls=%async_computation | async-start | bytes 393216 | tf_op jit(solution)/shard_map/all_to_all | solution.py:483
  14.2 8.3 %collective-permute-start.1 = (bf16[4,64,256]{2,1,0:T(8,128)(2,1)S(1)}, bf16[4,64,256]{2,1,0:T(8,128)(2,1)S(1)}, u32[]{:S(2)}, u32[]{:S(2)}) collective-permute-start(bf16[4,64,256]{2,1,0:T(8,128)(2,1)S(1)} %bitcast.26), channel_id=1, source_target_pairs={{4,0},{5,1},{6,2},{7,3},{8,4},{9,5},{10,6},{11,7},{12,8},{13,9},{1... | collective-permute-start | bytes 393224 | tf_op jit(solution)/shard_map/ppermute | solution.py:451
  15.5 9.6 %collective-permute-start = (bf16[4,64,256]{2,1,0:T(8,128)(2,1)S(1)}, bf16[4,64,256]{2,1,0:T(8,128)(2,1)S(1)}, u32[]{:S(2)}, u32[]{:S(2)}) collective-permute-start(bf16[4,64,256]{2,1,0:T(8,128)(2,1)S(1)} %bitcast.25), channel_id=1, source_target_pairs={{0,4},{1,5},{2,6},{3,7},{4,8},{5,9},{6,10},{7,11},{8,12},{9,13},{1... | collective-permute-start | bytes 393224 | tf_op jit(solution)/shard_map/ppermute | solution.py:451
  25.6 10.5 %collective-permute-start.2 = (bf16[288,256]{1,0:T(8,128)(2,1)S(1)}, bf16[288,256]{1,0:T(8,128)(2,1)S(1)}, u32[]{:S(2)}, u32[]{:S(2)}) collective-permute-start(bf16[288,256]{1,0:T(8,128)(2,1)S(1)} %get-tuple-element.25), channel_id=1, source_target_pairs={{0,4},{1,5},{2,6},{3,7},{4,8},{5,9},{6,10},{7,11},{8,12},{9,13},{1... | collective-permute-start | bytes 442376 | tf_op jit(solution)/shard_map/ppermute | solution.py:451
  30.0 7.4 %collective-permute-start.3 = (bf16[288,256]{1,0:T(8,128)(2,1)S(1)}, bf16[288,256]{1,0:T(8,128)(2,1)S(1)}, u32[]{:S(2)}, u32[]{:S(2)}) collective-permute-start(bf16[288,256]{1,0:T(8,128)(2,1)S(1)} %get-tuple-element.26), channel_id=1, source_target_pairs={{4,0},{5,1},{6,2},{7,3},{8,4},{9,5},{10,6},{11,7},{12,8},{13,9},{1... | collective-permute-start | bytes 442376 | tf_op jit(solution)/shard_map/ppermute | solution.py:451
  37.5 3.4 %collective-permute-start.4 = (bf16[144,512]{1,0:T(8,128)(2,1)S(1)}, bf16[144,512]{1,0:T(8,128)(2,1)S(1)}, u32[]{:S(2)}, u32[]{:S(2)}) collective-permute-start(bf16[144,512]{1,0:T(8,128)(2,1)S(1)} %get-tuple-element.32), channel_id=1, source_target_pairs={{0,3},{1,0},{2,1},{3,2},{4,7},{5,4},{6,5},{7,6},{8,11},{9,8},{10,9... | collective-permute-start | bytes 442376 | tf_op jit(solution)/shard_map/ppermute | solution.py:451
  37.6 6.2 %collective-permute-start.5 = (bf16[144,512]{1,0:T(8,128)(2,1)S(1)}, bf16[144,512]{1,0:T(8,128)(2,1)S(1)}, u32[]{:S(2)}, u32[]{:S(2)}) collective-permute-start(bf16[144,512]{1,0:T(8,128)(2,1)S(1)} %get-tuple-element.33), channel_id=1, source_target_pairs={{0,1},{1,2},{2,3},{3,0},{4,5},{5,6},{6,7},{7,4},{8,9},{9,10},{10,1... | collective-permute-start | bytes 442376 | tf_op jit(solution)/shard_map/ppermute | solution.py:451
  43.8 41.2 %copy-start.1 = (f32[512,256]{1,0:T(8,128)S(1)}, f32[512,256]{1,0:T(8,128)}, u32[]{:S(2)}) copy-start(f32[512,256]{1,0:T(8,128)} %dep.3) | copy-start | bytes 1572868

commit v9 on v8

--- a/solution.py
+++ b/solution.py
@@ -54,10 +54,10 @@
     return hi, mid, (rest - mid.astype(F32)).astype(BF)
 
 
-def pack_kernel(tiles, cap, lon_size, channels, count, dep, meta, tables, send, slot_out):
+def pack_kernel(tiles, cap, lon_size, channels, count, meta, table, send, slot_out):
     owner_row, cell_row, qc_row = meta[0:1], meta[1:2], meta[2:3]
-    jac, weight = tables[:channels], tables[channels : channels + 1]
-    rows = dep.shape[0]
+    rows = meta.shape[1]
+    dep, jac, weight = table[:rows], table[rows : rows + channels], table[rows + channels :]
     slots = send.shape[0]
     hit = (lax.broadcasted_iota(jnp.int32, (tiles, rows), 0) == owner_row).astype(BF)
     before = (lax.broadcasted_iota(jnp.int32, (rows, rows), 0)
@@ -70,7 +70,7 @@
 
     used = (lax.broadcasted_iota(jnp.int32, (1, rows), 1) < count[0]).astype(F32)
     row_weight = used * qc_row.astype(F32)
-    terms = mxu(jac, dep[...] * weight, ((1,), (1,)), lax.Precision.HIGHEST) * row_weight
+    terms = mxu(jac, dep * weight, ((1,), (1,)), lax.Precision.HIGHEST) * row_weight
     lat = cell_row // lon_size
     lon = cell_row - lat * lon_size
     wide = lax.broadcasted_iota(jnp.int32, (LANES, rows), 0)
@@ -124,7 +124,7 @@
     return jnp.where(keep, turn[:padded], 0.0), lat_row, lon_row, lat_col, lon_col
 
 
-def edge_kernel(channels, height, got, _slope_north, _slope_south, north, south):
+def edge_kernel(channels, height, got, north, south):
     tall, breadth = north.shape
     trim = tall // HALO
     slots = got.shape[0]
@@ -474,8 +474,8 @@
     send, slot = call(
         functools.partial(pack_kernel, tiles, cap, breadth, channels),
         (shape((slots, LANES), BF), shape((1, rows), jnp.int32)),
-        (obs_count, departure_in, jnp.stack([obs_owner[:, 0], obs_cell, qc_mask]),
-         jnp.concatenate([jacobian, weight], axis=0)),
+        (obs_count, jnp.stack([obs_owner[:, 0], obs_cell, qc_mask]),
+         jnp.concatenate([departure_in, jacobian, weight], axis=0)),
         smem=1,
     )
 
@@ -503,10 +503,10 @@
     north, south = call(
         functools.partial(edge_kernel, channels, height),
         (shape((HALO * trim, breadth), BF),) * 2,
-        (got, slope_north, slope_south),
-        unread=2,
+        (got,),
     )
     from_south = shift2(north, -1, 0)
+    south, slope_north, slope_south = lax.optimization_barrier((south, slope_north, slope_south))
     from_north = shift2(south, 1, 0)
     west, east = call(
         functools.partial(side_kernel, channels, height, breadth), (shape((padded, strip), BF),) * 2, (got,))

time: 89.1 us -> 87.7 us (0.984)
  local copies, waits for them, and re-layouts: 4.27 us -> 3.24 us
    ppermute x6, waiting for transfers between devices: 9.13 us -> 6.64 us  [shift2(): return lax.ppermute(x, ('lat', 'lon'), pairs)]
    all_to_all x1, waiting for transfers between devices: 0.01 us -> 1.93 us  [swap(): lax.all_to_all(x.reshape(tiles, -1, LANES), ('lat', 'lon'), split_axis=0,...]
    unnamed x14 -> x12, local copies, waits for them, and re-layouts: 3.1 us -> 2.06 us
  transfers between devices with their start and end apart: 7 -> 7, of which waited for: 4 -> 4; matrix products, arithmetic and copies ran while one was open for 4% -> 4% of each run, Pallas kernels for 6% -> 7%
where the time goes in v9:
time: 87.7 us; the launch traced here: 87.3 us
  Pallas kernels  37.8 us (43%)
  starting transfers between devices  19.4 us (22%)
  blocking collectives  14.7 us (17%)
  waiting for transfers between devices  8.58 us (10%)
  local copies, waits for them, and re-layouts  3.24 us (4%)
  other arithmetic  1.94 us (2%)
  between operations  1.69 us (2%)
    pallas_call x9, Pallas kernels, call(): pl.pallas_call(kernel, out_shape=outs, grid=(1,) if staged else (), in_sp...  37.8 us
    all_to_all x1, blocking collectives, swap(): lax.all_to_all(x.reshape(tiles, -1, LANES), ('lat', 'lon'), split_axis=0,...  14.7 us
    ppermute x6, starting transfers between devices, shift2(): return lax.ppermute(x, ('lat', 'lon'), pairs)  12.1 us
    all_to_all x1, starting transfers between devices, swap(): lax.all_to_all(x.reshape(tiles, -1, LANES), ('lat', 'lon'), split_axis=0,...  7.3 us
    ppermute x6, waiting for transfers between devices, shift2(): return lax.ppermute(x, ('lat', 'lon'), pairs)  6.64 us
    unnamed x12, local copies, waits for them, and re-layouts  2.06 us
    all_to_all x1, waiting for transfers between devices, swap(): lax.all_to_all(x.reshape(tiles, -1, LANES), ('lat', 'lon'), split_axis=0,...  1.93 us
  transfers between devices with their start and end apart: 7, of which 4 were waited for; matrix products, arithmetic and copies ran while one was open for 4% of the time, Pallas kernels for 7%

profile of v9, /device:TPU:0, one launch (start us, length us, event | category | flops | bytes accessed | tf_op | source)
XLA Modules:
  0.0 87.3 jit_solution(12443703490892428872)
XLA Ops:
  0.6 0.0 copy-start.1
  0.6 0.0 copy-start.3
  0.7 0.0 copy-start.4
  0.7 0.0 copy-start.2
  1.4 0.7 pad_add_fusion.meta
  2.1 1.1 %pad_maximum_fusion.table = f32[582,256]{1,0:T(8,128)S(1)} fusion(f32[1,256]{1,0:T(1,128)} %bitcast.23, f32[69,256]{1,0:T(8,128)} %jac.3, f32[512,256]{1,0:T(8,128)} %dep.1), kind=kLoop, calls=%fused_computation | loop fusion | flops 297984 | bytes 1191936 | tf_op jit(solution)/shard_map/concatenate | solution.py:478
  3.2 1.6 %shard_map.113 = (bf16[768,128]{1,0:T(8,128)(2,1)}, s32[1,512]{1,0:T(1,128)S(1)}) custom-call(s32[1]{0:T(128)S(6)} %copy.20.count, s32[3,512]{1,0:T(4,128)S(1)} %pad_add_fusion.meta, f32[582,256]{1,0:T(8,128)S(1)} %pad_maximum_fusion.table), custom_call_target="tpu_custom_call" | custom-call | tf_op jit(solution)/shard_map/pallas_call | solution.py:38
  4.9 7.3 %all-to-all-start = ((bf16[32,24,128]{2,1,0:T(8,128)(2,1)}), bf16[32,24,128]{2,1,0:T(8,128)(2,1)S(1)}, u32[]{:S(2)}, u32[]{:S(2)}) async-start(bf16[32,24,128]{2,1,0:T(8,128)(2,1)} %bitcast.6), calls=%async_computation | async-start | bytes 393216 | tf_op jit(solution)/shard_map/all_to_all | solution.py:483
  12.2 1.1 %fusion = (bf16[64,4,256]{2,1,0:T(4,128)(2,1)S(1)}, bf16[64,4,256]{2,1,0:T(4,128)(2,1)S(1)}) fusion(bf16[64,48,256]{2,1,0:T(8,128)(2,1)} %param.19), kind=kLoop, calls=%fused_computation.4 | loop fusion | bytes 524288 | tf_op jit(solution)/shard_map/slice | solution.py:497
  13.4 1.3 %collective-permute-start.1 = (bf16[4,64,256]{2,1,0:T(8,128)(2,1)S(1)}, bf16[4,64,256]{2,1,0:T(8,128)(2,1)S(1)}, u32[]{:S(2)}, u32[]{:S(2)}) collective-permute-start(bf16[4,64,256]{2,1,0:T(8,128)(2,1)S(1)} %bitcast.26), channel_id=1, source_target_pairs={{4,0},{5,1},{6,2},{7,3},{8,4},{9,5},{10,6},{11,7},{12,8},{13,9},{1... | collective-permute-start | bytes 393224 | tf_op jit(solution)/shard_map/ppermute | solution.py:451
  14.7 4.6 %collective-permute-start = (bf16[4,64,256]{2,1,0:T(8,128)(2,1)S(1)}, bf16[4,64,256]{2,1,0:T(8,128)(2,1)S(1)}, u32[]{:S(2)}, u32[]{:S(2)}) collective-permute-start(bf16[4,64,256]{2,1,0:T(8,128)(2,1)S(1)} %bitcast.25), channel_id=1, source_target_pairs={{0,4},{1,5},{2,6},{3,7},{4,8},{5,9},{6,10},{7,11},{8,12},{9,13},{1... | collective-permute-start | bytes 393224 | tf_op jit(solution)/shard_map/ppermute | solution.py:451
  19.2 1.9 %all-to-all-done = bf16[32,24,128]{2,1,0:T(8,128)(2,1)S(1)} async-done(((bf16[32,24,128]{2,1,0:T(8,128)(2,1)}), bf16[32,24,128]{2,1,0:T(8,128)(2,1)S(1)}, u32[]{:S(2)}, u32[]{:S(2)}) %all-to-all-start) | async-done | bytes 196640 | tf_op jit(solution)/shard_map/all_to_all | solution.py:483
  21.2 0.5 shard_map.115
  21.7 0.0 collective-permute-done.1.south.slope_south
  21.7 2.5 %collective-permute-done.north.slope_north = bf16[4,64,256]{2,1,0:T(8,128)(2,1)S(1)} collective-permute-done((bf16[4,64,256]{2,1,0:T(8,128)(2,1)S(1)}, bf16[4,64,256]{2,1,0:T(8,128)(2,1)S(1)}, u32[]{:S(2)}, u32[]{:S(2)}) %collective-permute-start) | collective-permute-done | bytes 131104 | tf_op jit(solution)/shard_map/ppermute | solution.py:451
  24.2 4.4 %collective-permute-start.2 = (bf16[288,256]{1,0:T(8,128)(2,1)S(1)}, bf16[288,256]{1,0:T(8,128)(2,1)S(1)}, u32[]{:S(2)}, u32[]{:S(2)}) collective-permute-start(bf16[288,256]{1,0:T(8,128)(2,1)S(1)} %get-tuple-element.29), channel_id=1, source_target_pairs={{0,4},{1,5},{2,6},{3,7},{4,8},{5,9},{6,10},{7,11},{8,12},{9,13},{1... | collective-permute-start | bytes 442376 | tf_op jit(solution)/shard_map/ppermute | solution.py:451
  28.6 1.3 %collective-permute-start.3 = (bf16[288,256]{1,0:T(8,128)(2,1)S(1)}, bf16[288,256]{1,0:T(8,128)(2,1)S(1)}, u32[]{:S(2)}, u32[]{:S(2)}) collective-permute-start(bf16[288,256]{1,0:T(8,128)(2,1)S(1)} %get-tuple-element.30), channel_id=1, source_target_pairs={{4,0},{5,1},{6,2},{7,3},{8,4},{9,5},{10,6},{11,7},{12,8},{13,9},{1... | collective-permute-start | bytes 442376 | tf_op jit(solution)/shard_map/ppermute | solution.py:451
  29.9 1.9 %copy.19 = bf16[64,48,256]{2,0,1:T(8,128)(2,1)S(1)} copy(bf16[64,48,256]{2,1,0:T(8,128)(2,1)} %param.19) | data formatting | bytes 3145728 | tf_op args[9]
  31.9 0.0 copy-done.4
  31.9 0.1 copy.15.projection
  32.0 0.0 copy-done.1
  32.0 0.0 copy-done.3
  32.0 0.0 copy-done.2
  32.0 1.1 %shard_map.118 = (bf16[192,240]{1,0:T(8,128)(2,1)S(1)}, bf16[216,192]{1,0:T(8,128)(2,1)S(1)}, bf16[64,80]{1,0:T(8,128)(2,1)S(1)}, bf16[72,64]{1,0:T(8,128)(2,1)S(1)}, bf16[136,240]{1,0:T(8,128)(2,1)S(1)}) custom-call(bf16[9,64,69]{2,1,0:T(8,128)(2,1)S(1)} %copy-done.2, bf16[69,64]{1,0:T(8,128)(2,1)S(1)} %copy.15.projection, f32[69,256]{1,0:T(8,128)S(1)} %copy-done.1, ...), custom_call_target="tpu_custom_call" | custom-call | tf_op jit(solution)/shard_map/pallas_call | solution.py:38
  33.1 0.6 shard_map.117
  33.7 1.0 %shard_map.116 = (bf16[80,512]{1,0:T(8,128)(2,1)S(1)}, bf16[80,512]{1,0:T(8,128)(2,1)S(1)}) custom-call(bf16[768,128]{1,0:T(8,128)(2,1)S(1)} %bitcast.18), custom_call_target="tpu_custom_call" | custom-call | tf_op jit(solution)/shard_map/pallas_call | solution.py:38
  34.7 0.0 collective-permute-done.2.from_north.north
  34.7 1.3 %collective-permute-done.3.from_south.south = bf16[288,256]{1,0:T(8,128)(2,1)S(1)} collective-permute-done((bf16[288,256]{1,0:T(8,128)(2,1)S(1)}, bf16[288,256]{1,0:T(8,128)(2,1)S(1)}, u32[]{:S(2)}, u32[]{:S(2)}) %collective-permute-start.3) | collective-permute-done | bytes 147488 | tf_op jit(solution)/shard_map/ppermute | solution.py:451
  36.0 0.2 shard_map.119
  36.2 0.1 collective-permute-start.4
  36.2 0.5 collective-permute-start.5
  36.7 0.1 add_convert_fusion.flags
  36.8 2.8 %shard_map.114.inner = f32[48,72,256]{2,1,0:T(8,128)S(1)} custom-call(bf16[768,128]{1,0:T(8,128)(2,1)S(1)} %bitcast.19), custom_call_target="tpu_custom_call" | custom-call | tf_op jit(solution)/shard_map/pallas_call | solution.py:38
  39.6 0.0 collective-permute-done.4.from_east
  39.6 2.8 %collective-permute-done.5.from_west = bf16[144,512]{1,0:T(8,128)(2,1)S(1)} collective-permute-done((bf16[144,512]{1,0:T(8,128)(2,1)S(1)}, bf16[144,512]{1,0:T(8,128)(2,1)S(1)}, u32[]{:S(2)}, u32[]{:S(2)}) %collective-permute-start.5) | collective-permute-done | bytes 147488 | tf_op jit(solution)/shard_map/ppermute | solution.py:451
  42.4 0.0 copy-start
  42.4 26.5 %shard_map.120 = (f32[56,72,256]{2,1,0:T(8,128)S(1)}, f32[56,72,256]{2,1,0:T(8,128)S(1)}, bf16[1024,128]{1,0:T(8,128)(2,1)S(1)}) custom-call(s32[2]{0:T(128)S(1)} %add_convert_fusion.flags, bf16[768,128]{1,0:T(8,128)(2,1)S(1)} %bitcast.20, f32[48,72,256]{2,1,0:T(8,128)S(1)} %shard_map.114.inner, ...), custom_call_target="tpu_custom_call" | custom-call | tf_op jit(solution)/shard_map/pallas_call | solution.py:38
  69.0 14.7 %all_to_all.10 = bf16[32,32,128]{2,1,0:T(8,128)(2,1)S(1)} all-to-all(bf16[32,32,128]{2,1,0:T(8,128)(2,1)S(1)} %bitcast.22), channel_id=1, replica_groups=mesh['lat'=8,'lon'=4] {'lat','lon'}, dimensions={0} | all-to-all | bytes 524288 | tf_op jit(solution)/shard_map/all_to_all | solution.py:483
  83.6 0.0 copy-done
  83.6 3.5 %shard_map.121 = (f32[69,48,256]{2,1,0:T(8,128)}, f32[512,256]{1,0:T(8,128)}) custom-call(bf16[1024,128]{1,0:T(8,128)(2,1)S(1)} %bitcast.21, s32[1,512]{1,0:T(1,128)S(1)} %get-tuple-element.45.slot, f32[512,256]{1,0:T(8,128)S(1)} %copy-done, f32[69,256]{1,0:T(8,128)S(1)} %copy-done.1, f32[56,72,256]{2,1,0:T(8,128)S(1)} %get-tuple-element.46.first, ...), custom_call_target="tpu_custom_call" | custom-call | tf_op jit(solution)/shard_map/pallas_call | solution.py:38
  (2 shorter events, 0.0 us)
Async XLA Ops:
  0.6 31.4 %copy-start.1 = (f32[69,256]{1,0:T(8,128)S(1)}, f32[69,256]{1,0:T(8,128)}, u32[]{:S(2)}) copy-start(f32[69,256]{1,0:T(8,128)} %jac.3) | copy-start | bytes 211972
  0.6 31.3 %copy-start.3 = (f32[256]{0:T(256)S(1)}, f32[256]{0:T(256)}, u32[]{:S(2)}) copy-start(f32[256]{0:T(256)} %param.15) | copy-start | bytes 3076
  0.7 31.2 %copy-start.4 = (bf16[69,64]{0,1:T(8,128)(2,1)S(1)}, bf16[69,64]{0,1:T(8,128)(2,1)}, u32[]{:S(2)}) copy-start(bf16[69,64]{0,1:T(8,128)(2,1)} %param.18) | copy-start | bytes 26500
  0.7 31.3 %copy-start.2 = (bf16[9,64,69]{2,1,0:T(8,128)(2,1)S(1)}, bf16[9,64,69]{2,1,0:T(8,128)(2,1)}, u32[]{:S(2)}) copy-start(bf16[9,64,69]{2,1,0:T(8,128)(2,1)} %taps.1) | copy-start | bytes 238468
  4.9 16.3 %all-to-all-start = ((bf16[32,24,128]{2,1,0:T(8,128)(2,1)}), bf16[32,24,128]{2,1,0:T(8,128)(2,1)S(1)}, u32[]{:S(2)}, u32[]{:S(2)}) async-start(bf16[32,24,128]{2,1,0:T(8,128)(2,1)} %bitcast.6), calls=%async_computation | async-start | bytes 393216 | tf_op jit(solution)/shard_map/all_to_all | solution.py:483
  13.4 8.3 %collective-permute-start.1 = (bf16[4,64,256]{2,1,0:T(8,128)(2,1)S(1)}, bf16[4,64,256]{2,1,0:T(8,128)(2,1)S(1)}, u32[]{:S(2)}, u32[]{:S(2)}) collective-permute-start(bf16[4,64,256]{2,1,0:T(8,128)(2,1)S(1)} %bitcast.26), channel_id=1, source_target_pairs={{4,0},{5,1},{6,2},{7,3},{8,4},{9,5},{10,6},{11,7},{12,8},{13,9},{1... | collective-permute-start | bytes 393224 | tf_op jit(solution)/shard_map/ppermute | solution.py:451
  14.7 9.6 %collective-permute-start = (bf16[4,64,256]{2,1,0:T(8,128)(2,1)S(1)}, bf16[4,64,256]{2,1,0:T(8,128)(2,1)S(1)}, u32[]{:S(2)}, u32[]{:S(2)}) collective-permute-start(bf16[4,64,256]{2,1,0:T(8,128)(2,1)S(1)} %bitcast.25), channel_id=1, source_target_pairs={{0,4},{1,5},{2,6},{3,7},{4,8},{5,9},{6,10},{7,11},{8,12},{9,13},{1... | collective-permute-start | bytes 393224 | tf_op jit(solution)/shard_map/ppermute | solution.py:451
  24.2 10.5 %collective-permute-start.2 = (bf16[288,256]{1,0:T(8,128)(2,1)S(1)}, bf16[288,256]{1,0:T(8,128)(2,1)S(1)}, u32[]{:S(2)}, u32[]{:S(2)}) collective-permute-start(bf16[288,256]{1,0:T(8,128)(2,1)S(1)} %get-tuple-element.29), channel_id=1, source_target_pairs={{0,4},{1,5},{2,6},{3,7},{4,8},{5,9},{6,10},{7,11},{8,12},{9,13},{1... | collective-permute-start | bytes 442376 | tf_op jit(solution)/shard_map/ppermute | solution.py:451
  28.6 7.4 %collective-permute-start.3 = (bf16[288,256]{1,0:T(8,128)(2,1)S(1)}, bf16[288,256]{1,0:T(8,128)(2,1)S(1)}, u32[]{:S(2)}, u32[]{:S(2)}) collective-permute-start(bf16[288,256]{1,0:T(8,128)(2,1)S(1)} %get-tuple-element.30), channel_id=1, source_target_pairs={{4,0},{5,1},{6,2},{7,3},{8,4},{9,5},{10,6},{11,7},{12,8},{13,9},{1... | collective-permute-start | bytes 442376 | tf_op jit(solution)/shard_map/ppermute | solution.py:451
  36.2 3.4 %collective-permute-start.4 = (bf16[144,512]{1,0:T(8,128)(2,1)S(1)}, bf16[144,512]{1,0:T(8,128)(2,1)S(1)}, u32[]{:S(2)}, u32[]{:S(2)}) collective-permute-start(bf16[144,512]{1,0:T(8,128)(2,1)S(1)} %get-tuple-element.36), channel_id=1, source_target_pairs={{0,3},{1,0},{2,1},{3,2},{4,7},{5,4},{6,5},{7,6},{8,11},{9,8},{10,9... | collective-permute-start | bytes 442376 | tf_op jit(solution)/shard_map/ppermute | solution.py:451
  36.2 6.2 %collective-permute-start.5 = (bf16[144,512]{1,0:T(8,128)(2,1)S(1)}, bf16[144,512]{1,0:T(8,128)(2,1)S(1)}, u32[]{:S(2)}, u32[]{:S(2)}) collective-permute-start(bf16[144,512]{1,0:T(8,128)(2,1)S(1)} %get-tuple-element.37), channel_id=1, source_target_pairs={{0,1},{1,2},{2,3},{3,0},{4,5},{5,6},{6,7},{7,4},{8,9},{9,10},{10,1... | collective-permute-start | bytes 442376 | tf_op jit(solution)/shard_map/ppermute | solution.py:451
  42.4 41.2 %copy-start = (f32[512,256]{1,0:T(8,128)S(1)}, f32[512,256]{1,0:T(8,128)}, u32[]{:S(2)}) copy-start(f32[512,256]{1,0:T(8,128)} %dep.1) | copy-start | bytes 1572868

commit v10 on v9

--- a/solution.py
+++ b/solution.py
@@ -16,7 +16,7 @@
 BF = jnp.bfloat16
 F32 = jnp.float32
 INTERPRET = False
-G = (18, 26, 25, 24, 24, 24)
+G = (27, 26, 25, 24, 48, 48)
 
 
 def mxu(a, b, dims=((1,), (0,)), precision=None):

time: 87.7 us -> 87.4 us (level)
  no operation moved by 1% of the time
where the time goes in v10:
time: 87.4 us; the launch traced here: 87 us
  Pallas kernels  37.5 us (43%)
  starting transfers between devices  19.4 us (22%)
  blocking collectives  14.7 us (17%)
  waiting for transfers between devices  8.58 us (10%)
  local copies, waits for them, and re-layouts  3.24 us (4%)
  other arithmetic  1.94 us (2%)
  between operations  1.7 us (2%)
    pallas_call x9, Pallas kernels, call(): pl.pallas_call(kernel, out_shape=outs, grid=(1,) if staged else (), in_sp...  37.5 us
    all_to_all x1, blocking collectives, swap(): lax.all_to_all(x.reshape(tiles, -1, LANES), ('lat', 'lon'), split_axis=0,...  14.7 us
    ppermute x6, starting transfers between devices, shift2(): return lax.ppermute(x, ('lat', 'lon'), pairs)  12.1 us
    all_to_all x1, starting transfers between devices, swap(): lax.all_to_all(x.reshape(tiles, -1, LANES), ('lat', 'lon'), split_axis=0,...  7.3 us
    ppermute x6, waiting for transfers between devices, shift2(): return lax.ppermute(x, ('lat', 'lon'), pairs)  6.64 us
    unnamed x12, local copies, waits for them, and re-layouts  2.06 us
    all_to_all x1, waiting for transfers between devices, swap(): lax.all_to_all(x.reshape(tiles, -1, LANES), ('lat', 'lon'), split_axis=0,...  1.93 us
  transfers between devices with their start and end apart: 7, of which 4 were waited for; matrix products, arithmetic and copies ran while one was open for 4% of the time, Pallas kernels for 7%

profile of v10, /device:TPU:0, one launch (start us, length us, event | category | flops | bytes accessed | tf_op | source)
XLA Modules:
  0.0 87.0 jit_solution(12692726396746036964)
XLA Ops:
  0.6 0.0 copy-start.1
  0.6 0.0 copy-start.3
  0.7 0.0 copy-start.4
  0.7 0.0 copy-start.2
  1.4 0.7 pad_add_fusion.meta
  2.1 1.1 %pad_maximum_fusion.table = f32[582,256]{1,0:T(8,128)S(1)} fusion(f32[1,256]{1,0:T(1,128)} %bitcast.23, f32[69,256]{1,0:T(8,128)} %jac.3, f32[512,256]{1,0:T(8,128)} %dep.1), kind=kLoop, calls=%fused_computation | loop fusion | flops 297984 | bytes 1191936 | tf_op jit(solution)/shard_map/concatenate | solution.py:478
  3.2 1.6 %shard_map.113 = (bf16[768,128]{1,0:T(8,128)(2,1)}, s32[1,512]{1,0:T(1,128)S(1)}) custom-call(s32[1]{0:T(128)S(6)} %copy.20.count, s32[3,512]{1,0:T(4,128)S(1)} %pad_add_fusion.meta, f32[582,256]{1,0:T(8,128)S(1)} %pad_maximum_fusion.table), custom_call_target="tpu_custom_call" | custom-call | tf_op jit(solution)/shard_map/pallas_call | solution.py:38
  4.9 7.3 %all-to-all-start = ((bf16[32,24,128]{2,1,0:T(8,128)(2,1)}), bf16[32,24,128]{2,1,0:T(8,128)(2,1)S(1)}, u32[]{:S(2)}, u32[]{:S(2)}) async-start(bf16[32,24,128]{2,1,0:T(8,128)(2,1)} %bitcast.6), calls=%async_computation | async-start | bytes 393216 | tf_op jit(solution)/shard_map/all_to_all | solution.py:483
  12.2 1.1 %fusion = (bf16[64,4,256]{2,1,0:T(4,128)(2,1)S(1)}, bf16[64,4,256]{2,1,0:T(4,128)(2,1)S(1)}) fusion(bf16[64,48,256]{2,1,0:T(8,128)(2,1)} %param.19), kind=kLoop, calls=%fused_computation.4 | loop fusion | bytes 524288 | tf_op jit(solution)/shard_map/slice | solution.py:497
  13.4 1.3 %collective-permute-start.1 = (bf16[4,64,256]{2,1,0:T(8,128)(2,1)S(1)}, bf16[4,64,256]{2,1,0:T(8,128)(2,1)S(1)}, u32[]{:S(2)}, u32[]{:S(2)}) collective-permute-start(bf16[4,64,256]{2,1,0:T(8,128)(2,1)S(1)} %bitcast.26), channel_id=1, source_target_pairs={{4,0},{5,1},{6,2},{7,3},{8,4},{9,5},{10,6},{11,7},{12,8},{13,9},{1... | collective-permute-start | bytes 393224 | tf_op jit(solution)/shard_map/ppermute | solution.py:451
  14.7 4.6 %collective-permute-start = (bf16[4,64,256]{2,1,0:T(8,128)(2,1)S(1)}, bf16[4,64,256]{2,1,0:T(8,128)(2,1)S(1)}, u32[]{:S(2)}, u32[]{:S(2)}) collective-permute-start(bf16[4,64,256]{2,1,0:T(8,128)(2,1)S(1)} %bitcast.25), channel_id=1, source_target_pairs={{0,4},{1,5},{2,6},{3,7},{4,8},{5,9},{6,10},{7,11},{8,12},{9,13},{1... | collective-permute-start | bytes 393224 | tf_op jit(solution)/shard_map/ppermute | solution.py:451
  19.2 1.9 %all-to-all-done = bf16[32,24,128]{2,1,0:T(8,128)(2,1)S(1)} async-done(((bf16[32,24,128]{2,1,0:T(8,128)(2,1)}), bf16[32,24,128]{2,1,0:T(8,128)(2,1)S(1)}, u32[]{:S(2)}, u32[]{:S(2)}) %all-to-all-start) | async-done | bytes 196640 | tf_op jit(solution)/shard_map/all_to_all | solution.py:483
  21.2 0.5 shard_map.115
  21.7 0.0 collective-permute-done.1.south.slope_south
  21.7 2.5 %collective-permute-done.north.slope_north = bf16[4,64,256]{2,1,0:T(8,128)(2,1)S(1)} collective-permute-done((bf16[4,64,256]{2,1,0:T(8,128)(2,1)S(1)}, bf16[4,64,256]{2,1,0:T(8,128)(2,1)S(1)}, u32[]{:S(2)}, u32[]{:S(2)}) %collective-permute-start) | collective-permute-done | bytes 131104 | tf_op jit(solution)/shard_map/ppermute | solution.py:451
  24.2 4.4 %collective-permute-start.2 = (bf16[288,256]{1,0:T(8,128)(2,1)S(1)}, bf16[288,256]{1,0:T(8,128)(2,1)S(1)}, u32[]{:S(2)}, u32[]{:S(2)}) collective-permute-start(bf16[288,256]{1,0:T(8,128)(2,1)S(1)} %get-tuple-element.29), channel_id=1, source_target_pairs={{0,4},{1,5},{2,6},{3,7},{4,8},{5,9},{6,10},{7,11},{8,12},{9,13},{1... | collective-permute-start | bytes 442376 | tf_op jit(solution)/shard_map/ppermute | solution.py:451
  28.6 1.3 %collective-permute-start.3 = (bf16[288,256]{1,0:T(8,128)(2,1)S(1)}, bf16[288,256]{1,0:T(8,128)(2,1)S(1)}, u32[]{:S(2)}, u32[]{:S(2)}) collective-permute-start(bf16[288,256]{1,0:T(8,128)(2,1)S(1)} %get-tuple-element.30), channel_id=1, source_target_pairs={{4,0},{5,1},{6,2},{7,3},{8,4},{9,5},{10,6},{11,7},{12,8},{13,9},{1... | collective-permute-start | bytes 442376 | tf_op jit(solution)/shard_map/ppermute | solution.py:451
  29.9 1.9 %copy.19 = bf16[64,48,256]{2,0,1:T(8,128)(2,1)S(1)} copy(bf16[64,48,256]{2,1,0:T(8,128)(2,1)} %param.19) | data formatting | bytes 3145728 | tf_op args[9]
  31.9 0.0 copy-done.4
  31.9 0.1 copy.15.projection
  32.0 0.0 copy-done.1
  32.0 0.0 copy-done.3
  32.0 0.0 copy-done.2
  32.0 1.1 %shard_map.118 = (bf16[192,240]{1,0:T(8,128)(2,1)S(1)}, bf16[216,192]{1,0:T(8,128)(2,1)S(1)}, bf16[64,80]{1,0:T(8,128)(2,1)S(1)}, bf16[72,64]{1,0:T(8,128)(2,1)S(1)}, bf16[136,240]{1,0:T(8,128)(2,1)S(1)}) custom-call(bf16[9,64,69]{2,1,0:T(8,128)(2,1)S(1)} %copy-done.2, bf16[69,64]{1,0:T(8,128)(2,1)S(1)} %copy.15.projection, f32[69,256]{1,0:T(8,128)S(1)} %copy-done.1, ...), custom_call_target="tpu_custom_call" | custom-call | tf_op jit(solution)/shard_map/pallas_call | solution.py:38
  33.1 0.6 shard_map.117
  33.7 1.0 %shard_map.116 = (bf16[80,512]{1,0:T(8,128)(2,1)S(1)}, bf16[80,512]{1,0:T(8,128)(2,1)S(1)}) custom-call(bf16[768,128]{1,0:T(8,128)(2,1)S(1)} %bitcast.18), custom_call_target="tpu_custom_call" | custom-call | tf_op jit(solution)/shard_map/pallas_call | solution.py:38
  34.7 0.0 collective-permute-done.2.from_north.north
  34.7 1.3 %collective-permute-done.3.from_south.south = bf16[288,256]{1,0:T(8,128)(2,1)S(1)} collective-permute-done((bf16[288,256]{1,0:T(8,128)(2,1)S(1)}, bf16[288,256]{1,0:T(8,128)(2,1)S(1)}, u32[]{:S(2)}, u32[]{:S(2)}) %collective-permute-start.3) | collective-permute-done | bytes 147488 | tf_op jit(solution)/shard_map/ppermute | solution.py:451
  36.0 0.2 shard_map.119
  36.2 0.1 collective-permute-start.4
  36.2 0.5 collective-permute-start.5
  36.7 0.1 add_convert_fusion.flags
  36.8 2.8 %shard_map.114.inner = f32[48,72,256]{2,1,0:T(8,128)S(1)} custom-call(bf16[768,128]{1,0:T(8,128)(2,1)S(1)} %bitcast.19), custom_call_target="tpu_custom_call" | custom-call | tf_op jit(solution)/shard_map/pallas_call | solution.py:38
  39.6 0.0 collective-permute-done.4.from_east
  39.6 2.8 %collective-permute-done.5.from_west = bf16[144,512]{1,0:T(8,128)(2,1)S(1)} collective-permute-done((bf16[144,512]{1,0:T(8,128)(2,1)S(1)}, bf16[144,512]{1,0:T(8,128)(2,1)S(1)}, u32[]{:S(2)}, u32[]{:S(2)}) %collective-permute-start.5) | collective-permute-done | bytes 147488 | tf_op jit(solution)/shard_map/ppermute | solution.py:451
  42.4 0.0 copy-start
  42.4 26.2 %shard_map.120 = (f32[56,72,256]{2,1,0:T(8,128)S(1)}, f32[56,72,256]{2,1,0:T(8,128)S(1)}, bf16[1024,128]{1,0:T(8,128)(2,1)S(1)}) custom-call(s32[2]{0:T(128)S(1)} %add_convert_fusion.flags, bf16[768,128]{1,0:T(8,128)(2,1)S(1)} %bitcast.20, f32[48,72,256]{2,1,0:T(8,128)S(1)} %shard_map.114.inner, ...), custom_call_target="tpu_custom_call" | custom-call | tf_op jit(solution)/shard_map/pallas_call | solution.py:38
  68.6 14.7 %all_to_all.10 = bf16[32,32,128]{2,1,0:T(8,128)(2,1)S(1)} all-to-all(bf16[32,32,128]{2,1,0:T(8,128)(2,1)S(1)} %bitcast.22), channel_id=1, replica_groups=mesh['lat'=8,'lon'=4] {'lat','lon'}, dimensions={0} | all-to-all | bytes 524288 | tf_op jit(solution)/shard_map/all_to_all | solution.py:483
  83.3 0.0 copy-done
  83.3 3.5 %shard_map.121 = (f32[69,48,256]{2,1,0:T(8,128)}, f32[512,256]{1,0:T(8,128)}) custom-call(bf16[1024,128]{1,0:T(8,128)(2,1)S(1)} %bitcast.21, s32[1,512]{1,0:T(1,128)S(1)} %get-tuple-element.45.slot, f32[512,256]{1,0:T(8,128)S(1)} %copy-done, f32[69,256]{1,0:T(8,128)S(1)} %copy-done.1, f32[56,72,256]{2,1,0:T(8,128)S(1)} %get-tuple-element.46.first, ...), custom_call_target="tpu_custom_call" | custom-call | tf_op jit(solution)/shard_map/pallas_call | solution.py:38
  (2 shorter events, 0.0 us)
Async XLA Ops:
  0.6 31.4 %copy-start.1 = (f32[69,256]{1,0:T(8,128)S(1)}, f32[69,256]{1,0:T(8,128)}, u32[]{:S(2)}) copy-start(f32[69,256]{1,0:T(8,128)} %jac.3) | copy-start | bytes 211972
  0.6 31.3 %copy-start.3 = (f32[256]{0:T(256)S(1)}, f32[256]{0:T(256)}, u32[]{:S(2)}) copy-start(f32[256]{0:T(256)} %param.15) | copy-start | bytes 3076
  0.7 31.2 %copy-start.4 = (bf16[69,64]{0,1:T(8,128)(2,1)S(1)}, bf16[69,64]{0,1:T(8,128)(2,1)}, u32[]{:S(2)}) copy-start(bf16[69,64]{0,1:T(8,128)(2,1)} %param.18) | copy-start | bytes 26500
  0.7 31.3 %copy-start.2 = (bf16[9,64,69]{2,1,0:T(8,128)(2,1)S(1)}, bf16[9,64,69]{2,1,0:T(8,128)(2,1)}, u32[]{:S(2)}) copy-start(bf16[9,64,69]{2,1,0:T(8,128)(2,1)} %taps.1) | copy-start | bytes 238468
  4.9 16.3 %all-to-all-start = ((bf16[32,24,128]{2,1,0:T(8,128)(2,1)}), bf16[32,24,128]{2,1,0:T(8,128)(2,1)S(1)}, u32[]{:S(2)}, u32[]{:S(2)}) async-start(bf16[32,24,128]{2,1,0:T(8,128)(2,1)} %bitcast.6), calls=%async_computation | async-start | bytes 393216 | tf_op jit(solution)/shard_map/all_to_all | solution.py:483
  13.4 8.3 %collective-permute-start.1 = (bf16[4,64,256]{2,1,0:T(8,128)(2,1)S(1)}, bf16[4,64,256]{2,1,0:T(8,128)(2,1)S(1)}, u32[]{:S(2)}, u32[]{:S(2)}) collective-permute-start(bf16[4,64,256]{2,1,0:T(8,128)(2,1)S(1)} %bitcast.26), channel_id=1, source_target_pairs={{4,0},{5,1},{6,2},{7,3},{8,4},{9,5},{10,6},{11,7},{12,8},{13,9},{1... | collective-permute-start | bytes 393224 | tf_op jit(solution)/shard_map/ppermute | solution.py:451
  14.7 9.6 %collective-permute-start = (bf16[4,64,256]{2,1,0:T(8,128)(2,1)S(1)}, bf16[4,64,256]{2,1,0:T(8,128)(2,1)S(1)}, u32[]{:S(2)}, u32[]{:S(2)}) collective-permute-start(bf16[4,64,256]{2,1,0:T(8,128)(2,1)S(1)} %bitcast.25), channel_id=1, source_target_pairs={{0,4},{1,5},{2,6},{3,7},{4,8},{5,9},{6,10},{7,11},{8,12},{9,13},{1... | collective-permute-start | bytes 393224 | tf_op jit(solution)/shard_map/ppermute | solution.py:451
  24.2 10.5 %collective-permute-start.2 = (bf16[288,256]{1,0:T(8,128)(2,1)S(1)}, bf16[288,256]{1,0:T(8,128)(2,1)S(1)}, u32[]{:S(2)}, u32[]{:S(2)}) collective-permute-start(bf16[288,256]{1,0:T(8,128)(2,1)S(1)} %get-tuple-element.29), channel_id=1, source_target_pairs={{0,4},{1,5},{2,6},{3,7},{4,8},{5,9},{6,10},{7,11},{8,12},{9,13},{1... | collective-permute-start | bytes 442376 | tf_op jit(solution)/shard_map/ppermute | solution.py:451
  28.6 7.4 %collective-permute-start.3 = (bf16[288,256]{1,0:T(8,128)(2,1)S(1)}, bf16[288,256]{1,0:T(8,128)(2,1)S(1)}, u32[]{:S(2)}, u32[]{:S(2)}) collective-permute-start(bf16[288,256]{1,0:T(8,128)(2,1)S(1)} %get-tuple-element.30), channel_id=1, source_target_pairs={{4,0},{5,1},{6,2},{7,3},{8,4},{9,5},{10,6},{11,7},{12,8},{13,9},{1... | collective-permute-start | bytes 442376 | tf_op jit(solution)/shard_map/ppermute | solution.py:451
  36.2 3.4 %collective-permute-start.4 = (bf16[144,512]{1,0:T(8,128)(2,1)S(1)}, bf16[144,512]{1,0:T(8,128)(2,1)S(1)}, u32[]{:S(2)}, u32[]{:S(2)}) collective-permute-start(bf16[144,512]{1,0:T(8,128)(2,1)S(1)} %get-tuple-element.36), channel_id=1, source_target_pairs={{0,3},{1,0},{2,1},{3,2},{4,7},{5,4},{6,5},{7,6},{8,11},{9,8},{10,9... | collective-permute-start | bytes 442376 | tf_op jit(solution)/shard_map/ppermute | solution.py:451
  36.2 6.2 %collective-permute-start.5 = (bf16[144,512]{1,0:T(8,128)(2,1)S(1)}, bf16[144,512]{1,0:T(8,128)(2,1)S(1)}, u32[]{:S(2)}, u32[]{:S(2)}) collective-permute-start(bf16[144,512]{1,0:T(8,128)(2,1)S(1)} %get-tuple-element.37), channel_id=1, source_target_pairs={{0,1},{1,2},{2,3},{3,0},{4,5},{5,6},{6,7},{7,4},{8,9},{9,10},{10,1... | collective-permute-start | bytes 442376 | tf_op jit(solution)/shard_map/ppermute | solution.py:451
  42.4 40.9 %copy-start = (f32[512,256]{1,0:T(8,128)S(1)}, f32[512,256]{1,0:T(8,128)}, u32[]{:S(2)}) copy-start(f32[512,256]{1,0:T(8,128)} %dep.1) | copy-start | bytes 1572868
